TPU v7x, 256 devices: a whole 4x4x8 slice. The times are simulated.
256 devices in a mesh: row: 16 (over z, core), col: 16 (over y, x).
Axes of the slice: x: 4, y: 4, z: 8, core: 2. Of those that a mesh axis runs over, the one named last changes fastest.
Arguments:
- a_matrix: bfloat16 [32768, 24576], P('row', 'col'), may hold values from -6 to 6
- omega: bfloat16 [24576, 512], P('col'), may hold values from -0.0390625 to 0.0390625
- leaf_pivots: int32 [16, 2048], P('row'), may hold values from 0 to 2047, each once within a row
- upper_pivots: int32 [3, 8, 1024], replicated, may hold values from 0 to 1023, each once within a row
- ranks: int32 [4, 16], replicated, may hold values from 256 to 512
Outputs:
- leaf_interp: float32 [16, 1536, 512], P('row', 'col')
- upper_interp: float32 [3, 16, 512, 512], P(None, 'row', 'col')
Inputs may be any that keep to these rules, and one draw needn't show every extreme that they name: Each row of leaf_pivots and of upper_pivots is a permutation. Rows of ranks beyond the level's node count are not read.
All inputs are finite; a program needn't handle non-finite values. Where the computation divides by a largest or mean magnitude, that divisor is 1e-20 or more.
Results may differ from a plain program's by a relative error of at most 0.0003.
Values sent between devices are 32-bit elements; how exact they have to be, the bound alone decides.
No kernel may reach another device: no remote copies, remote signals or barrier semaphores. Data moves between devices by JAX's collectives and lax.ppermute only.
A program may use at most 128 MiB of HBM per device.

v0:
```python
import functools
import math

import jax
import jax.numpy as jnp
from jax import lax
from jax.experimental import pallas as pl
from jax.experimental.pallas import tpu as pltpu
from jax.sharding import Mesh, PartitionSpec as P

K = 512
S = 512
LEAF = 2048
NEWTON = 6
F32 = jnp.float32
BF16 = jnp.bfloat16


def hop(block, axis, first):
    masks = (1, 3) if first else (3, 1)
    route = []
    for core in range(2):
        for place in range(4):
            route.append((core * 4 + place, core * 4 + (place ^ masks[core])))
    return lax.ppermute(block, ("core", axis), route)


def swapped(block, axis, mask):
    count = lax.axis_size(axis)
    return lax.ppermute(block, axis, [(i, i ^ mask) for i in range(count)])


def split3(value):
    high = lax.reduce_precision(value, 8, 7)
    rest = value - high
    middle = lax.reduce_precision(rest, 8, 7)
    return jnp.concatenate([high, middle, rest - middle], 0).astype(BF16)


def pick(value, order, kept):
    rows, length = value.shape
    place = lax.broadcasted_iota(jnp.int32, (length, order.shape[0]), 0)
    chosen = ((place == order[None, :]) & kept[None, :]).astype(BF16)
    parts = jnp.dot(split3(value), chosen, preferred_element_type=F32)
    return parts[:rows] + parts[rows : 2 * rows] + parts[2 * rows :]


def ordered_kernel(place_ref, omega_ref, a_ref, out_a_ref, out_b_ref, lhs_ref, *, sent):
    @pl.when(pl.program_id(0) == 0)
    def _():
        x, y, core = place_ref[0], place_ref[1], place_ref[2]
        near = jnp.where(core == 0, 1, 3)
        far = jnp.where(core == 0, 3, 1)
        row = lax.broadcasted_iota(jnp.int32, (256, 1), 0)
        outer = (row >> 6) & 1
        if sent:
            first = jnp.where(outer == 0, near, 2)
        else:
            first = jnp.where(outer == 0, 0, far)
        inner = (row >> 4) & 3
        second = jnp.where(
            inner == 0, 0, jnp.where(inner == 1, far, jnp.where(inner == 2, near, 2))
        )
        half_a = (x ^ first) * 64 + (y ^ second) * 16
        half_b = (x ^ second) * 64 + (y ^ first) * 16 + 256
        old = jnp.where(row < 128, half_a, half_b) + (row & 15)
        place = lax.broadcasted_iota(jnp.int32, (256, S), 1)
        chosen = jnp.where(place == old, 1.0, 0.0).astype(BF16)
        lhs_ref[...] = lax.dot_general(
            chosen, omega_ref[...], (((1,), (1,)), ((), ())), preferred_element_type=F32
        ).astype(BF16)

    rows = lax.dot_general(
        lhs_ref[...], a_ref[...], (((1,), (1,)), ((), ())), preferred_element_type=F32
    )
    out_a_ref[...] = rows[:128]
    out_b_ref[...] = rows[128:]


def ordered_samples(place, omega, a_matrix, sent):
    depth = a_matrix.shape[1]
    block = 256
    out = jax.ShapeDtypeStruct((128, LEAF), F32)
    return pl.pallas_call(
        functools.partial(ordered_kernel, sent=sent),
        grid_spec=pltpu.PrefetchScalarGridSpec(
            num_scalar_prefetch=1,
            grid=(LEAF // block,),
            in_specs=[
                pl.BlockSpec((depth, S), lambda i, _: (0, 0)),
                pl.BlockSpec((block, depth), lambda i, _: (i, 0)),
            ],
            out_specs=[pl.BlockSpec((128, block), lambda i, _: (0, i))] * 2,
            scratch_shapes=[pltpu.VMEM((256, depth), BF16)],
        ),
        out_shape=[out, out],
        compiler_params=pltpu.CompilerParams(vmem_limit_bytes=32 * 2**20),
        cost_estimate=pl.CostEstimate(
            flops=2 * 256 * depth * (LEAF + S),
            bytes_accessed=2 * depth * (LEAF + S) + 4 * 256 * LEAF,
            transcendentals=0,
        ),
        name="sent_samples" if sent else "kept_samples",
    )(place, omega, a_matrix)


def parts2(value):
    high = value.astype(BF16)
    return high, (value - high.astype(F32)).astype(BF16)


def dot3(left, right, dims):
    left_high, left_low = parts2(left)
    right_high, right_low = right

    def one(u, v):
        return lax.dot_general(u, v, (dims, ((), ())), preferred_element_type=F32)

    return one(left_high, right_high) + (one(left_low, right_high) + one(left_high, right_low))


def solve_kernel(skeleton_ref, redundant_ref, out_ref):
    skeleton = skeleton_ref[...]
    parts = parts2(skeleton)
    over_samples = ((0,), (0,))
    plain = ((1,), (0,))
    rows = lax.broadcasted_iota(jnp.int32, (K, K), 0)
    columns = lax.broadcasted_iota(jnp.int32, (K, K), 1)
    identity = jnp.where(rows == columns, 1.0, 0.0)
    gram = dot3(skeleton, parts, over_samples) * (1.0 / (8.0 * S)) + identity
    cross = dot3(redundant_ref[...], parts, over_samples)
    sums = jnp.sum(jnp.abs(gram), axis=0, keepdims=True)
    bound = jnp.max(sums, axis=1, keepdims=True)
    power = identity - gram / bound
    out = cross / (math.sqrt(S) * bound)
    for step in range(NEWTON):
        parts = parts2(power)
        out = out + dot3(out, parts, plain)
        if step < NEWTON - 1:
            power = dot3(power, parts, plain)
    out_ref[...] = out


def solve(skeleton, redundant):
    rows = redundant.shape[1]
    return pl.pallas_call(
        solve_kernel,
        out_shape=jax.ShapeDtypeStruct((rows, K), F32),
        in_specs=[pl.BlockSpec(memory_space=pltpu.VMEM)] * 2,
        out_specs=pl.BlockSpec(memory_space=pltpu.VMEM),
        compiler_params=pltpu.CompilerParams(vmem_limit_bytes=40 * 2**20),
        cost_estimate=pl.CostEstimate(
            flops=6 * 6 * (K + rows) * K * K, bytes_accessed=4 * (S + rows) * K, transcendentals=0
        ),
        name="solve",
    )(skeleton, redundant)


def local(a_matrix, omega, leaf_pivots, upper_pivots, ranks):
    z, core, y, x = (lax.axis_index(name) for name in ("z", "core", "y", "x"))
    place = jnp.stack([x, y, core]).astype(jnp.int32)
    send_a, send_b = ordered_samples(place, omega, a_matrix, True)
    got_a, got_b = hop(send_a, "x", True), hop(send_b, "y", True)
    keep_a, keep_b = ordered_samples(place, omega, a_matrix, False)
    sum_a, sum_b = keep_a + got_a, keep_b + got_b
    got_a, got_b = hop(sum_a[64:], "x", False), hop(sum_b[64:], "y", False)
    sum_a, sum_b = sum_a[:64] + got_a, sum_b[:64] + got_b
    got_a, got_b = hop(sum_a[32:], "y", True), hop(sum_b[32:], "x", True)
    sum_a, sum_b = sum_a[:32] + got_a, sum_b[:32] + got_b
    got_a, got_b = hop(sum_a[16:], "y", False), hop(sum_b[16:], "x", False)
    samples = jnp.concatenate([sum_a[:16] + got_a, sum_b[:16] + got_b], 0)

    def compress(rows, pivots, rank):
        kept = jnp.arange(pivots.shape[0]) < rank
        kept = kept | (jnp.arange(pivots.shape[0]) >= K)
        moved = pick(rows, pivots, kept)
        return moved[:, :K], moved[:, K:]

    row_index = z * 2 + core
    skeleton, leaf_redundant = compress(samples, leaf_pivots[0], ranks[0, row_index])
    leaf_skeleton = skeleton
    levels = []
    for level, axis, mask in ((1, "core", 1), (2, "z", 1), (3, "z", 2)):
        sibling = swapped(skeleton, axis, mask)
        side = row_index >> (level - 1) & 1
        rows = jnp.concatenate(
            [jnp.where(side == 0, skeleton, sibling), jnp.where(side == 0, sibling, skeleton)], 1
        )
        node = row_index >> level
        skeleton, redundant = compress(rows, upper_pivots[level - 1, node], ranks[level, node])
        levels.append(jnp.concatenate([skeleton, redundant], 1))

    odd = z & 1
    upper = jnp.where(core == 0, levels[0], jnp.where(odd == 0, levels[1], levels[2]))
    spread = jnp.concatenate(
        [
            jnp.broadcast_to(leaf_skeleton[None], (16, 32, K)),
            jnp.broadcast_to(upper[None, :, :K], (16, 32, K)),
            leaf_redundant.reshape(32, 16, 96).transpose(1, 0, 2),
            upper[:, K:].reshape(32, 16, 32).transpose(1, 0, 2),
        ],
        2,
    )
    whole = lax.all_to_all(spread, ("y", "x"), 0, 0, tiled=False).reshape(S, 2 * K + 128)
    leaf_interp = solve(whole[:, :K], whole[:, 2 * K : 2 * K + 96])
    upper_interp = solve(whole[:, K : 2 * K], whole[:, 2 * K + 96 :])

    other = swapped(upper_interp, "core", 1)
    level_1 = jnp.where(core == 0, upper_interp, other)
    chip = jnp.where(core == 0, other, upper_interp)
    beside = swapped(chip, "z", 1)
    level_2 = jnp.where(odd == 0, chip, beside)
    level_3 = jnp.where(odd == 0, beside, chip)
    return (leaf_interp[None], jnp.stack([level_1, level_2, level_3])[:, None])


def solution(mesh):
    grid = Mesh(mesh.devices.reshape(8, 2, 4, 4), ("z", "core", "y", "x"))
    row, col = ("z", "core"), ("y", "x")
    return jax.shard_map(
        local,
        mesh=grid,
        in_specs=(P(row, col), P(col, None), P(row, None), P(), P()),
        out_specs=(P(row, col, None), P(None, row, col, None)),
        check_vma=False,
    )
```

profile of v0, /device:TPU:1, one launch (start us, length us, event | category | flops | bytes accessed | tf_op | source)
XLA Modules:
  0.0 137.4 jit_solution(9042960125765887140)
XLA Ops:
  0.6 0.1 pad_add_fusion.place_ref
  0.7 2.8 %copy-done = bf16[2048,1536]{1,0:T(8,128)(2,1)S(1)} copy-done((bf16[2048,1536]{1,0:T(8,128)(2,1)S(1)}, bf16[2048,1536]{1,0:T(8,128)(2,1)}, u32[]{:S(2)}) %copy-start) | copy-done | bytes 6291480
  3.5 1.4 %copy-done.1 = bf16[1536,512]{1,0:T(8,128)(2,1)S(1)} copy-done((bf16[1536,512]{1,0:T(8,128)(2,1)S(1)}, bf16[1536,512]{1,0:T(8,128)(2,1)}, u32[]{:S(2)}) %copy-start.1) | copy-done | bytes 1572888
  4.9 4.6 %sent_samples.1 = (f32[128,2048]{1,0:T(8,128)S(1)}, f32[128,2048]{1,0:T(8,128)S(1)}) custom-call(s32[3]{0:T(128)S(1)} %pad_add_fusion.place_ref, bf16[1536,512]{1,0:T(8,128)(2,1)S(1)} %copy-done.1, bf16[2048,1536]{1,0:T(8,128)(2,1)S(1)} %copy-done), custom_call_target="tpu_custom_call" | custom-call | flops 2013265920 | bytes 9961472 | tf_op jit(solution)/shard_map/sent_samples/pallas_call | solution.py:84
  9.5 3.4 %collective-permute-start = (f32[128,2048]{1,0:T(8,128)S(1)}, f32[128,2048]{1,0:T(8,128)S(1)}, u32[]{:S(2)}, u32[]{:S(2)}) collective-permute-start(f32[128,2048]{1,0:T(8,128)S(1)} %get-tuple-element.7), channel_id=1, source_target_pairs={{0,1},{1,0},{2,3},{3,2},{16,19},{17,18},{18,17},{19,16},{4,5},{5,4... | collective-permute-start | bytes 3145736 | tf_op jit(solution)/shard_map/ppermute | solution.py:25
  12.9 2.7 %collective-permute-start.4 = (f32[128,2048]{1,0:T(8,128)S(1)}, f32[128,2048]{1,0:T(8,128)}, u32[]{:S(2)}, u32[]{:S(2)}) collective-permute-start(f32[128,2048]{1,0:T(8,128)S(1)} %get-tuple-element.9), channel_id=1, source_target_pairs={{0,4},{4,0},{8,12},{12,8},{16,28},{20,24},{24,20},{28,16},{1,5},{5... | collective-permute-start | bytes 3145736 | tf_op jit(solution)/shard_map/ppermute | solution.py:25
  15.6 4.6 %kept_samples.1 = (f32[128,2048]{1,0:T(8,128)S(1)}, f32[128,2048]{1,0:T(8,128)S(1)}) custom-call(s32[3]{0:T(128)S(1)} %pad_add_fusion.place_ref, bf16[1536,512]{1,0:T(8,128)(2,1)S(1)} %copy-done.1, bf16[2048,1536]{1,0:T(8,128)(2,1)S(1)} %copy-done), custom_call_target="tpu_custom_call" | custom-call | flops 2013265920 | bytes 9961472 | tf_op jit(solution)/shard_map/kept_samples/pallas_call | solution.py:84
  20.2 4.9 %collective-permute-done = f32[128,2048]{1,0:T(8,128)S(1)} collective-permute-done((f32[128,2048]{1,0:T(8,128)S(1)}, f32[128,2048]{1,0:T(8,128)S(1)}, u32[]{:S(2)}, u32[]{:S(2)}) %collective-permute-start) | collective-permute-done | bytes 1048608 | tf_op jit(solution)/shard_map/ppermute | solution.py:25
  25.0 0.1 add.72
  25.2 0.8 slice.144
  26.0 0.6 collective-permute-start.1
  26.6 0.0 copy-done.2
  26.6 0.7 constant_dynamic-slice_fusion.6
  27.3 0.8 constant_dynamic-slice_fusion
  28.1 0.0 collective-permute-done.4
  28.1 1.3 add.76
  29.5 0.0 copy-start.3
  29.5 1.4 %collective-permute-start.5 = (f32[64,2048]{1,0:T(8,128)S(1)}, f32[64,2048]{1,0:T(8,128)S(1)}, u32[]{:S(2)}, u32[]{:S(2)}) collective-permute-start(f32[64,2048]{1,0:T(8,128)S(1)} %slice.150), channel_id=1, source_target_pairs={{0,12},{4,8},{8,4},{12,0},{16,20},{20,16},{24,28},{28,24},{1,13},{... | collective-permute-start | bytes 1572872 | tf_op jit(solution)/shard_map/ppermute | solution.py:25
  30.9 0.6 fusion.46
  31.5 3.2 %collective-permute-done.1 = f32[64,2048]{1,0:T(8,128)} collective-permute-done((f32[64,2048]{1,0:T(8,128)}, f32[64,2048]{1,0:T(8,128)}, u32[]{:S(2)}, u32[]{:S(2)}) %collective-permute-start.1) | collective-permute-done | bytes 524320 | tf_op jit(solution)/shard_map/ppermute | solution.py:25
  34.7 1.1 slice_add_fusion.1
  35.8 3.0 %collective-permute-start.2 = (f32[32,2048]{1,0:T(8,128)S(1)}, f32[32,2048]{1,0:T(8,128)S(1)}, u32[]{:S(2)}, u32[]{:S(2)}) collective-permute-start(f32[32,2048]{1,0:T(8,128)S(1)} %slice.146), channel_id=1, source_target_pairs={{0,4},{4,0},{8,12},{12,8},{16,28},{20,24},{24,20},{28,16},{1,5},{5... | collective-permute-start | bytes 786440 | tf_op jit(solution)/shard_map/ppermute | solution.py:25
  38.8 0.0 collective-permute-done.5
  38.8 0.1 slice_add_fusion
  38.9 2.6 %collective-permute-start.6 = (f32[32,2048]{1,0:T(8,128)S(1)}, f32[32,2048]{1,0:T(8,128)S(1)}, u32[]{:S(2)}, u32[]{:S(2)}) collective-permute-start(f32[32,2048]{1,0:T(8,128)S(1)} %slice.152), channel_id=1, source_target_pairs={{0,1},{1,0},{2,3},{3,2},{16,19},{17,18},{18,17},{19,16},{4,5},{5,4... | collective-permute-start | bytes 786440 | tf_op jit(solution)/shard_map/ppermute | solution.py:25
  41.5 3.6 %collective-permute-done.2 = f32[32,2048]{1,0:T(8,128)S(1)} collective-permute-done((f32[32,2048]{1,0:T(8,128)S(1)}, f32[32,2048]{1,0:T(8,128)S(1)}, u32[]{:S(2)}, u32[]{:S(2)}) %collective-permute-start.2) | collective-permute-done | bytes 262176 | tf_op jit(solution)/shard_map/ppermute | solution.py:25
  45.1 0.5 collective-permute-start.3
  45.6 0.0 collective-permute-done.6
  45.7 0.1 collective-permute-start.7
  45.8 3.6 %collective-permute-done.3 = f32[16,2048]{1,0:T(8,128)S(1)} collective-permute-done((f32[16,2048]{1,0:T(8,128)S(1)}, f32[16,2048]{1,0:T(8,128)S(1)}, u32[]{:S(2)}, u32[]{:S(2)}) %collective-permute-start.3) | collective-permute-done | bytes 131104 | tf_op jit(solution)/shard_map/ppermute | solution.py:25
  49.4 1.6 %collective-permute-done.7 = f32[16,2048]{1,0:T(8,128)S(1)} collective-permute-done((f32[16,2048]{1,0:T(8,128)S(1)}, f32[16,2048]{1,0:T(8,128)S(1)}, u32[]{:S(2)}, u32[]{:S(2)}) %collective-permute-start.7) | collective-permute-done | bytes 131104 | tf_op jit(solution)/shard_map/ppermute | solution.py:25
  51.0 0.1 reduce-precision_convert_fusion.1
  51.1 0.0 copy-done.3
  51.1 4.0 %fusion.1 = f32[96,2048]{1,0:T(8,128)S(1)} fusion(s32[2048]{0:T(1024)S(1)} %bitcast.37, pred[2048]{0:T(1024)(128)(4,1)S(1)} %fusion.46, bf16[32,2048]{1,0:T(8,128)(2,1)S(1)} %get-tuple-element.18, bf16[32,2048]{1,0:T(8,128)(2,1)S(1)} %get-tuple-element.17, bf16[32,2048]{1,0:T(8,128)(2,1)S(1)} %get-tuple-element.16), kind=kOutput, calls=%fused_computation.2 | convolution fusion | flops 814874624 | bytes 1189888 | tf_op jit(solution)/shard_map/dot_general | solution.py:44
  55.1 8.5 %collective-permute-start.8 = (f32[32,512]{1,0:T(8,128)S(1)}, f32[32,512]{1,0:T(8,128)S(1)}, u32[]{:S(2)}, u32[]{:S(2)}) collective-permute-start(f32[32,512]{1,0:T(8,128)S(1)} %slice.158), channel_id=1, source_target_pairs={{0,16},{16,0},{1,17},{17,1},{2,18},{18,2},{3,19},{19,3},{4,20},{20... | collective-permute-start | bytes 196616 | tf_op jit(solution)/shard_map/ppermute | solution.py:30
  63.6 0.6 fusion.49
  64.2 0.3 collective-permute-done.8
  64.5 1.0 fusion.12
  65.6 1.9 %collective-permute-start.9 = (f32[32,512]{1,0:T(8,128)S(1)}, f32[32,512]{1,0:T(8,128)S(1)}, u32[]{:S(2)}, u32[]{:S(2)}) collective-permute-start(f32[32,512]{1,0:T(8,128)S(1)} %slice.162), channel_id=1, source_target_pairs={{0,32},{32,0},{64,96},{96,64},{128,160},{160,128},{192,224},{224,1... | collective-permute-start | bytes 196616 | tf_op jit(solution)/shard_map/ppermute | solution.py:30
  67.5 0.6 fusion.48
  68.2 1.4 %collective-permute-done.9 = f32[32,512]{1,0:T(8,128)S(1)} collective-permute-done((f32[32,512]{1,0:T(8,128)S(1)}, f32[32,512]{1,0:T(8,128)S(1)}, u32[]{:S(2)}, u32[]{:S(2)}) %collective-permute-start.9) | collective-permute-done | bytes 65568 | tf_op jit(solution)/shard_map/ppermute | solution.py:30
  69.7 1.0 fusion.10
  70.8 3.1 %collective-permute-start.10 = (f32[32,512]{1,0:T(8,128)S(1)}, f32[32,512]{1,0:T(8,128)S(1)}, u32[]{:S(2)}, u32[]{:S(2)}) collective-permute-start(f32[32,512]{1,0:T(8,128)S(1)} %slice.166), channel_id=1, source_target_pairs={{0,64},{32,96},{64,0},{96,32},{128,192},{160,224},{192,128},{224,1... | collective-permute-start | bytes 196616 | tf_op jit(solution)/shard_map/ppermute | solution.py:30
  73.8 0.6 fusion.47
  74.5 0.1 reshape.50
  74.6 0.8 copy.13
  75.4 0.1 collective-permute-done.10
  75.5 1.0 fusion.8
  76.6 0.1 fusion.45
  76.7 0.1 reshape.51
  76.8 0.8 copy.12
  77.6 0.1 broadcast_in_dim.9
  77.7 1.1 broadcast_in_dim.8
  78.8 2.4 %concatenate.42 = f32[16,32,1152]{2,1,0:T(8,128)S(1)} concatenate(f32[16,32,512]{2,1,0:T(8,128)} %broadcast_in_dim.8, f32[16,32,512]{2,1,0:T(8,128)S(1)} %broadcast_in_dim.9, f32[16,32,96]{2,1,0:T(8,128)} %bitcast.32, f32[16,32,32]{2,1,0:T(8,128)} %bitcast.33), dimensions={2} | concatenate | bytes 4718592 | tf_op jit(solution)/shard_map/concatenate | solution.py:195
  81.3 32.9 %all_to_all.5 = f32[16,32,1152]{2,1,0:T(8,128)S(1)} all-to-all(f32[16,32,1152]{2,1,0:T(8,128)S(1)} %concatenate.42), channel_id=1, replica_groups=mesh['z'=8,'core'=2,'y'=4,'x'=4] {'y','x'}, dimensions={0} | all-to-all | bytes 4718592 | tf_op jit(solution)/shard_map/all_to_all | solution.py:204
  114.2 0.3 fusion.54
  114.4 0.1 slice.176.redundant_ref
  114.6 7.6 %solve.3 = f32[32,512]{1,0:T(8,128)S(1)} custom-call(f32[512,512]{1,0:T(8,128)S(1)} %get-tuple-element.12.skeleton_ref, f32[512,32]{1,0:T(8,128)S(1)} %slice.176.redundant_ref), custom_call_target="tpu_custom_call" | custom-call | flops 5133828096 | bytes 1114112 | tf_op jit(solution)/shard_map/solve/pallas_call | solution.py:146
  122.2 3.7 %collective-permute-start.11 = (f32[32,512]{1,0:T(8,128)S(1)}, f32[32,512]{1,0:T(8,128)S(1)}, u32[]{:S(2)}, u32[]{:S(2)}) collective-permute-start(f32[32,512]{1,0:T(8,128)S(1)} %solve.3), channel_id=1, source_target_pairs={{0,16},{16,0},{1,17},{17,1},{2,18},{18,2},{3,19},{19,3},{4,20},{20... | collective-permute-start | bytes 196616 | tf_op jit(solution)/shard_map/ppermute | solution.py:30
  125.8 0.9 collective-permute-done.11
  126.7 1.7 %collective-permute-start.12 = (f32[32,512]{1,0:T(8,128)S(1)}, f32[32,512]{1,0:T(8,128)S(1)}, u32[]{:S(2)}, u32[]{:S(2)}) collective-permute-start(f32[32,512]{1,0:T(8,128)S(1)} %get-tuple-element.24), channel_id=1, source_target_pairs={{0,32},{32,0},{64,96},{96,64},{128,160},{160,128},{192,224},{224,1... | collective-permute-start | bytes 196616 | tf_op jit(solution)/shard_map/ppermute | solution.py:30
  128.5 8.2 %solve.2 = f32[96,512]{1,0:T(8,128)} custom-call(f32[512,512]{1,0:T(8,128)S(1)} %get-tuple-element.13.skeleton_ref, f32[512,96]{1,0:T(8,128)S(1)} %slice.174.redundant_ref), custom_call_target="tpu_custom_call" | custom-call | flops 5737807872 | bytes 1245184 | tf_op jit(solution)/shard_map/solve/pallas_call | solution.py:146
  136.6 0.0 collective-permute-done.12
  136.7 0.7 maximum_bitcast_fusion
  (29 shorter events, 0.5 us)
Async XLA Ops:
  0.7 2.8 %copy-start = (bf16[2048,1536]{1,0:T(8,128)(2,1)S(1)}, bf16[2048,1536]{1,0:T(8,128)(2,1)}, u32[]{:S(2)}) copy-start(bf16[2048,1536]{1,0:T(8,128)(2,1)} %a_ref.3) | copy-start | bytes 18874372
  3.5 1.4 %copy-start.1 = (bf16[1536,512]{1,0:T(8,128)(2,1)S(1)}, bf16[1536,512]{1,0:T(8,128)(2,1)}, u32[]{:S(2)}) copy-start(bf16[1536,512]{1,0:T(8,128)(2,1)} %omega_ref.3) | copy-start | bytes 4718596
  9.5 15.6 %collective-permute-start = (f32[128,2048]{1,0:T(8,128)S(1)}, f32[128,2048]{1,0:T(8,128)S(1)}, u32[]{:S(2)}, u32[]{:S(2)}) collective-permute-start(f32[128,2048]{1,0:T(8,128)S(1)} %get-tuple-element.7), channel_id=1, source_target_pairs={{0,1},{1,0},{2,3},{3,2},{16,19},{17,18},{18,17},{19,16},{4,5},{5,4... | collective-permute-start | bytes 3145736 | tf_op jit(solution)/shard_map/ppermute | solution.py:25
  12.9 13.8 %copy-start.2 = (s32[4,16]{1,0:T(4,128)S(1)}, s32[4,16]{1,0:T(4,128)}, u32[]{:S(2)}) copy-start(s32[4,16]{1,0:T(4,128)} %param.9) | copy-start | bytes 772
  12.9 15.2 %collective-permute-start.4 = (f32[128,2048]{1,0:T(8,128)S(1)}, f32[128,2048]{1,0:T(8,128)}, u32[]{:S(2)}, u32[]{:S(2)}) collective-permute-start(f32[128,2048]{1,0:T(8,128)S(1)} %get-tuple-element.9), channel_id=1, source_target_pairs={{0,4},{4,0},{8,12},{12,8},{16,28},{20,24},{24,20},{28,16},{1,5},{5... | collective-permute-start | bytes 3145736 | tf_op jit(solution)/shard_map/ppermute | solution.py:25
  26.0 8.6 %collective-permute-start.1 = (f32[64,2048]{1,0:T(8,128)}, f32[64,2048]{1,0:T(8,128)}, u32[]{:S(2)}, u32[]{:S(2)}) collective-permute-start(f32[64,2048]{1,0:T(8,128)} %slice.144), channel_id=1, source_target_pairs={{0,3},{1,2},{2,1},{3,0},{16,17},{17,16},{18,19},{19,18},{4,7},{5,6... | collective-permute-start | bytes 1572872 | tf_op jit(solution)/shard_map/ppermute | solution.py:25
  29.5 21.6 %copy-start.3 = (s32[1,2048]{1,0:T(1,128)S(1)}, s32[1,2048]{1,0:T(1,128)}, u32[]{:S(2)}) copy-start(s32[1,2048]{1,0:T(1,128)} %param.7) | copy-start | bytes 24580
  29.5 9.3 %collective-permute-start.5 = (f32[64,2048]{1,0:T(8,128)S(1)}, f32[64,2048]{1,0:T(8,128)S(1)}, u32[]{:S(2)}, u32[]{:S(2)}) collective-permute-start(f32[64,2048]{1,0:T(8,128)S(1)} %slice.150), channel_id=1, source_target_pairs={{0,12},{4,8},{8,4},{12,0},{16,20},{20,16},{24,28},{28,24},{1,13},{... | collective-permute-start | bytes 1572872 | tf_op jit(solution)/shard_map/ppermute | solution.py:25
  35.8 9.3 %collective-permute-start.2 = (f32[32,2048]{1,0:T(8,128)S(1)}, f32[32,2048]{1,0:T(8,128)S(1)}, u32[]{:S(2)}, u32[]{:S(2)}) collective-permute-start(f32[32,2048]{1,0:T(8,128)S(1)} %slice.146), channel_id=1, source_target_pairs={{0,4},{4,0},{8,12},{12,8},{16,28},{20,24},{24,20},{28,16},{1,5},{5... | collective-permute-start | bytes 786440 | tf_op jit(solution)/shard_map/ppermute | solution.py:25
  38.9 6.7 %collective-permute-start.6 = (f32[32,2048]{1,0:T(8,128)S(1)}, f32[32,2048]{1,0:T(8,128)S(1)}, u32[]{:S(2)}, u32[]{:S(2)}) collective-permute-start(f32[32,2048]{1,0:T(8,128)S(1)} %slice.152), channel_id=1, source_target_pairs={{0,1},{1,0},{2,3},{3,2},{16,19},{17,18},{18,17},{19,16},{4,5},{5,4... | collective-permute-start | bytes 786440 | tf_op jit(solution)/shard_map/ppermute | solution.py:25
  45.1 4.2 %collective-permute-start.3 = (f32[16,2048]{1,0:T(8,128)S(1)}, f32[16,2048]{1,0:T(8,128)S(1)}, u32[]{:S(2)}, u32[]{:S(2)}) collective-permute-start(f32[16,2048]{1,0:T(8,128)S(1)} %slice.148), channel_id=1, source_target_pairs={{0,12},{4,8},{8,4},{12,0},{16,20},{20,16},{24,28},{28,24},{1,13},{... | collective-permute-start | bytes 393224 | tf_op jit(solution)/shard_map/ppermute | solution.py:25
  45.7 5.3 %collective-permute-start.7 = (f32[16,2048]{1,0:T(8,128)S(1)}, f32[16,2048]{1,0:T(8,128)S(1)}, u32[]{:S(2)}, u32[]{:S(2)}) collective-permute-start(f32[16,2048]{1,0:T(8,128)S(1)} %slice.154), channel_id=1, source_target_pairs={{0,3},{1,2},{2,1},{3,0},{16,17},{17,16},{18,19},{19,18},{4,7},{5,6... | collective-permute-start | bytes 393224 | tf_op jit(solution)/shard_map/ppermute | solution.py:25
  55.1 9.4 %collective-permute-start.8 = (f32[32,512]{1,0:T(8,128)S(1)}, f32[32,512]{1,0:T(8,128)S(1)}, u32[]{:S(2)}, u32[]{:S(2)}) collective-permute-start(f32[32,512]{1,0:T(8,128)S(1)} %slice.158), channel_id=1, source_target_pairs={{0,16},{16,0},{1,17},{17,1},{2,18},{18,2},{3,19},{19,3},{4,20},{20... | collective-permute-start | bytes 196616 | tf_op jit(solution)/shard_map/ppermute | solution.py:30
  65.6 4.0 %collective-permute-start.9 = (f32[32,512]{1,0:T(8,128)S(1)}, f32[32,512]{1,0:T(8,128)S(1)}, u32[]{:S(2)}, u32[]{:S(2)}) collective-permute-start(f32[32,512]{1,0:T(8,128)S(1)} %slice.162), channel_id=1, source_target_pairs={{0,32},{32,0},{64,96},{96,64},{128,160},{160,128},{192,224},{224,1... | collective-permute-start | bytes 196616 | tf_op jit(solution)/shard_map/ppermute | solution.py:30
  70.8 4.7 %collective-permute-start.10 = (f32[32,512]{1,0:T(8,128)S(1)}, f32[32,512]{1,0:T(8,128)S(1)}, u32[]{:S(2)}, u32[]{:S(2)}) collective-permute-start(f32[32,512]{1,0:T(8,128)S(1)} %slice.166), channel_id=1, source_target_pairs={{0,64},{32,96},{64,0},{96,32},{128,192},{160,224},{192,128},{224,1... | collective-permute-start | bytes 196616 | tf_op jit(solution)/shard_map/ppermute | solution.py:30
  122.2 4.6 %collective-permute-start.11 = (f32[32,512]{1,0:T(8,128)S(1)}, f32[32,512]{1,0:T(8,128)S(1)}, u32[]{:S(2)}, u32[]{:S(2)}) collective-permute-start(f32[32,512]{1,0:T(8,128)S(1)} %solve.3), channel_id=1, source_target_pairs={{0,16},{16,0},{1,17},{17,1},{2,18},{18,2},{3,19},{19,3},{4,20},{20... | collective-permute-start | bytes 196616 | tf_op jit(solution)/shard_map/ppermute | solution.py:30
  126.7 9.9 %collective-permute-start.12 = (f32[32,512]{1,0:T(8,128)S(1)}, f32[32,512]{1,0:T(8,128)S(1)}, u32[]{:S(2)}, u32[]{:S(2)}) collective-permute-start(f32[32,512]{1,0:T(8,128)S(1)} %get-tuple-element.24), channel_id=1, source_target_pairs={{0,32},{32,0},{64,96},{96,64},{128,160},{160,128},{192,224},{224,1... | collective-permute-start | bytes 196616 | tf_op jit(solution)/shard_map/ppermute | solution.py:30
where the time goes:
time: 138 us; the launch traced here: 137 us
  starting transfers between devices  33.1 us (24%)
  blocking collectives  32.9 us (24%)
  Pallas kernels  24.9 us (18%)
  waiting for transfers between devices  19.5 us (14%)
  local copies, waits for them, and re-layouts  12.5 us (9%)
  matrix products  7.08 us (5%)
  other arithmetic  6.33 us (5%)
    all_to_all x1, blocking collectives, local(): lax.all_to_all(spread, ('y', 'x'), 0, 0, tiled=False)  32.9 us
    ppermute x5, starting transfers between devices, swapped(): return lax.ppermute(block, axis, [(i, i ^ mask) for i in range(count)])  18.8 us
    ppermute x8, waiting for transfers between devices, hop(): return lax.ppermute(block, ('core', axis), route)  16.9 us
    pallas_call x2, Pallas kernels, solve(): pl.pallas_call(solve_kernel, out_shape=jax.ShapeDtypeStruct((rows, K), F3...  15.8 us
    ppermute x8, starting transfers between devices, hop(): return lax.ppermute(block, ('core', axis), route)  14.3 us
    pallas_call x2, Pallas kernels, ordered_samples(): pl.pallas_call(functools.partial(ordered_kernel, sent=sent), grid_spec=pl...  9.11 us
    dot_general x4, matrix products, pick(): parts = jnp.dot(split3(value), chosen, preferred_element_type=F32)  7.08 us
    unnamed x8, local copies, waits for them, and re-layouts  4.2 us
  transfers between devices with their start and end apart: 13, of which 9 were waited for; matrix products, arithmetic and copies ran while one was open for 6% of the time, Pallas kernels for 9%

commit v1 on v0

v1 whole, which is shorter than its diff:
```python
import functools
import math

import jax
import jax.numpy as jnp
from jax import lax
from jax.experimental import pallas as pl
from jax.experimental.pallas import tpu as pltpu
from jax.sharding import Mesh, PartitionSpec as P

K = 512
S = 512
LEAF = 2048
NEWTON = 6
F32 = jnp.float32
VMEM = pl.BlockSpec(memory_space=pltpu.VMEM)
ANY = pl.BlockSpec(memory_space=pl.ANY)
BF16 = jnp.bfloat16


def hop(block, axis, first):
    masks = (1, 3) if first else (3, 1)
    route = []
    for core in range(2):
        for place in range(4):
            route.append((core * 4 + place, core * 4 + (place ^ masks[core])))
    return lax.ppermute(block, ("core", axis), route)


def swapped(block, axis, mask):
    count = lax.axis_size(axis)
    return lax.ppermute(block, axis, [(i, i ^ mask) for i in range(count)])


def ordered_kernel(place_ref, omega_ref, a_ref, out_a_ref, out_b_ref, lhs_ref, *, sent):
    @pl.when(pl.program_id(0) == 0)
    def _():
        x, y, core = place_ref[0], place_ref[1], place_ref[2]
        near = jnp.where(core == 0, 1, 3)
        far = jnp.where(core == 0, 3, 1)
        row = lax.broadcasted_iota(jnp.int32, (256, 1), 0)
        outer = (row >> 6) & 1
        if sent:
            first = jnp.where(outer == 0, near, 2)
        else:
            first = jnp.where(outer == 0, 0, far)
        inner = (row >> 4) & 3
        second = jnp.where(
            inner == 0, 0, jnp.where(inner == 1, far, jnp.where(inner == 2, near, 2))
        )
        half_a = (x ^ first) * 64 + (y ^ second) * 16
        half_b = (x ^ second) * 64 + (y ^ first) * 16 + 256
        old = jnp.where(row < 128, half_a, half_b) + (row & 15)
        place = lax.broadcasted_iota(jnp.int32, (256, S), 1)
        chosen = jnp.where(place == old, 1.0, 0.0).astype(BF16)
        lhs_ref[...] = lax.dot_general(
            chosen, omega_ref[...], (((1,), (1,)), ((), ())), preferred_element_type=F32
        ).astype(BF16)

    rows = lax.dot_general(
        lhs_ref[...], a_ref[...], (((1,), (1,)), ((), ())), preferred_element_type=F32
    )
    out_a_ref[...] = rows[:128]
    out_b_ref[...] = rows[128:]


def ordered_samples(place, omega, a_matrix, sent):
    depth = a_matrix.shape[1]
    block = 1024
    out = jax.ShapeDtypeStruct((128, LEAF), F32)
    return pl.pallas_call(
        functools.partial(ordered_kernel, sent=sent),
        grid_spec=pltpu.PrefetchScalarGridSpec(
            num_scalar_prefetch=1,
            grid=(LEAF // block,),
            in_specs=[
                pl.BlockSpec((depth, S), lambda i, _: (0, 0)),
                pl.BlockSpec((block, depth), lambda i, _: (i, 0)),
            ],
            out_specs=[pl.BlockSpec((128, block), lambda i, _: (0, i))] * 2,
            scratch_shapes=[pltpu.VMEM((256, depth), BF16)],
        ),
        out_shape=[out, out],
        compiler_params=pltpu.CompilerParams(vmem_limit_bytes=56 * 2**20),
        cost_estimate=pl.CostEstimate(
            flops=2 * 256 * depth * (LEAF + S),
            bytes_accessed=2 * depth * (LEAF + S) + 4 * 256 * LEAF,
            transcendentals=0,
        ),
        name="sent_samples" if sent else "kept_samples",
    )(place, omega, a_matrix)


def parts2(value):
    high = value.astype(BF16)
    return high, (value - high.astype(F32)).astype(BF16)


def product(left, right):
    return jnp.dot(left, right, preferred_element_type=F32)


def solve_kernel(*refs, packed):
    out_ref = refs[-1]
    if packed:
        own_ref, got_ref = refs[:2]
        skeleton = jnp.concatenate([own_ref[:, :K], got_ref[:, :K]], 0)
        pieces = [own_ref[:128], own_ref[128:], got_ref[:128], got_ref[128:]]
        redundant = jnp.concatenate(
            [
                piece[:, K + 32 * slot : K + 32 * slot + 32]
                for piece, slot in zip(pieces, (0, 2, 1, 3))
            ],
            0,
        )
    else:
        own_ref, rest_ref, got_ref = refs[:3]
        skeleton = jnp.concatenate([own_ref[:, :K], got_ref[:, :K]], 0)
        redundant = jnp.concatenate([rest_ref[:, :96], got_ref[:, K : K + 96]], 0)
    count = redundant.shape[1]
    identity = jnp.where(
        lax.broadcasted_iota(jnp.int32, (K, K), 0) == lax.broadcasted_iota(jnp.int32, (K, K), 1),
        1.0,
        0.0,
    )

    def times(square, rows, high, low):
        rows_high, rows_low = parts2(rows)
        left = [rows_high, rows_low] if square is None else [square, rows_high, rows_low]
        first = product(jnp.concatenate(left, 0), high)
        second = product(jnp.concatenate(left[:-1], 0), low)
        start = 0 if square is None else K
        moved = (second[start:] + first[start + count :]) + first[start : start + count]
        if square is None:
            return None, moved
        mixed = second[:K]
        return first[:K] + (mixed + mixed.T), moved

    high, low = parts2(skeleton)
    gram, cross = times(parts2(skeleton.T)[0], redundant.T, high, low)
    gram = gram * (1.0 / (8.0 * S)) + identity
    bound = jnp.max(jnp.sum(jnp.abs(gram), axis=0, keepdims=True), axis=1, keepdims=True)
    power = identity - gram / bound
    out = cross / (math.sqrt(S) * bound)
    for step in range(NEWTON):
        high, low = parts2(power)
        power, moved = times(high if step < NEWTON - 1 else None, out, high, low)
        out = out + moved
    out_ref[...] = out


def solve(whole, rows, packed, after=()):
    return pl.pallas_call(
        functools.partial(solve_kernel, packed=packed),
        out_shape=jax.ShapeDtypeStruct((rows, K), F32),
        in_specs=[VMEM] * len(whole) + [ANY] * len(after),
        out_specs=VMEM,
        compiler_params=pltpu.CompilerParams(vmem_limit_bytes=24 * 2**20),
        cost_estimate=pl.CostEstimate(
            flops=6 * 6 * (K + rows) * K * K, bytes_accessed=4 * (S + rows) * K, transcendentals=0
        ),
        name="solve_upper" if packed else "solve_leaf",
    )(*whole, *after)


def add_kernel(kept_a, got_a, kept_b, got_b, out_a, out_b, *, first):
    rows = out_a.shape[0]
    part = slice(first, first + rows)
    out_a[...] = kept_a[part] + got_a[part]
    out_b[...] = kept_b[part] + got_b[part]


def added(kept, got, first, name):
    rows = kept[0].shape[0] // 2
    out = jax.ShapeDtypeStruct((rows, LEAF), F32)
    return pl.pallas_call(
        functools.partial(add_kernel, first=first),
        in_specs=[VMEM] * 4,
        out_specs=[VMEM] * 2,
        out_shape=[out, out],
        compiler_params=pltpu.CompilerParams(vmem_limit_bytes=16 * 2**20),
        cost_estimate=pl.CostEstimate(
            flops=2 * rows * LEAF, bytes_accessed=24 * rows * LEAF, transcendentals=0
        ),
        name=name,
    )(kept[0], got[0], kept[1], got[1])


def parts3(value):
    high = value.astype(BF16)
    rest = value - high.astype(F32)
    middle = rest.astype(BF16)
    low = (rest - middle.astype(F32)).astype(BF16)
    return jnp.concatenate([high, middle, low], 0)


def picked(parts, order):
    place = lax.broadcasted_iota(jnp.int32, (parts.shape[1], order.shape[1]), 0)
    chosen = jnp.where(place == order, 1.0, 0.0).astype(BF16)
    moved = jnp.dot(parts, chosen, preferred_element_type=F32)
    return (moved[:32] + moved[32:64]) + moved[64:]


def finish_kernel(order_ref, *refs):
    terms, (skeleton_ref, parts_ref) = refs[:-2], refs[-2:]
    half = len(terms) // 2
    totals = []
    for group in (terms[:half], terms[half:]):
        total = group[0][:16]
        for term in group[1:]:
            total = total + term[:16]
        totals.append(total)
    parts = parts3(jnp.concatenate(totals, 0))
    parts_ref[...] = parts
    skeleton_ref[...] = picked(parts, order_ref[...])


def finished(order, terms_a, terms_b):
    terms = [*terms_a, *terms_b]
    return pl.pallas_call(
        finish_kernel,
        in_specs=[VMEM] * (1 + len(terms)),
        out_specs=[VMEM] * 2,
        out_shape=[
            jax.ShapeDtypeStruct((32, K), F32),
            jax.ShapeDtypeStruct((96, LEAF), BF16),
        ],
        compiler_params=pltpu.CompilerParams(vmem_limit_bytes=16 * 2**20),
        cost_estimate=pl.CostEstimate(
            flops=2 * 96 * LEAF * K, bytes_accessed=4 * 16 * len(terms) * LEAF, transcendentals=0
        ),
        name="finish_samples",
    )(order, *terms)


def call(kernel, name, inputs, shapes, after=(), flops=10**6):
    return pl.pallas_call(
        kernel,
        in_specs=[VMEM] * len(inputs) + [ANY] * len(after),
        out_specs=[VMEM] * len(shapes),
        out_shape=[jax.ShapeDtypeStruct(shape, F32) for shape in shapes],
        compiler_params=pltpu.CompilerParams(vmem_limit_bytes=16 * 2**20),
        cost_estimate=pl.CostEstimate(flops=flops, bytes_accessed=10**6, transcendentals=0),
        name=name,
    )(*inputs, *after)


def leaf_kernel(order_ref, parts_ref, skeleton_ref, _, payload_ref, rest_ref):
    parts = parts_ref[...]
    payload_ref[:, :K] = skeleton_ref[...]
    for i in range(4):
        part = slice(i * K, i * K + K)
        moved = picked(parts, order_ref[:, part])
        if i < 2:
            rest_ref[:, part] = moved
        else:
            payload_ref[:, (i - 1) * K : i * K] = moved


def pack(own, rest, got, payload_ref, rest_ref):
    rows, half = own.shape[0], rest.shape[1] // 2
    payload_ref[:rows, :K] = own[:, :K]
    payload_ref[rows:, :K] = got[:, :K]
    payload_ref[:rows, K:] = rest[:, half:]
    payload_ref[rows:, K:] = got[:, K + half :]
    rest_ref[:rows] = rest[:, :half]
    rest_ref[rows:] = got[:, K : K + half]


def pack_kernel(own, rest, got, payload_ref, rest_ref):
    pack(own, rest, got, payload_ref, rest_ref)


def pack_all_kernel(own, rest, got, payload_ref):
    rows = own.shape[0]
    payload_ref[:rows, :K] = own[:, :K]
    payload_ref[:rows, K:] = rest[...]
    payload_ref[rows:] = got[...]


def stack_kernel(own, got, payload_ref):
    rows = own.shape[0]
    payload_ref[:rows] = own[...]
    payload_ref[rows:] = got[...]


def level_1_kernel(order, own, sibling, skeleton_ref, redundant_ref):
    moved = picked(parts3(jnp.concatenate([own[...], sibling[...]], 1)), order[...])
    skeleton_ref[...] = moved[:, :K]
    redundant_ref[...] = moved[:, K:]


def level_2_kernel(
    order, own, sibling, leaf, rest, got, skeleton_ref, redundant_ref, payload_ref, rest_ref
):
    level_1_kernel(order, own, sibling, skeleton_ref, redundant_ref)
    pack(leaf, rest, got, payload_ref, rest_ref)


def level_3_kernel(
    order, own, sibling, leaf, rest, got, which, skeleton_1, redundant_1, redundant_2,
    upper_ref, upper_rest_ref, payload_ref, rest_ref,
):
    moved = picked(parts3(jnp.concatenate([own[...], sibling[...]], 1)), order[...])
    first, second = which[0, 0] == 0, which[0, 0] == 1
    skeleton = jnp.where(first, skeleton_1[...], jnp.where(second, own[...], moved[:, :K]))
    redundant = jnp.where(first, redundant_1[...], jnp.where(second, redundant_2[...], moved[:, K:]))
    upper_ref[:, :K] = skeleton
    upper_ref[:, K:] = redundant[:, 256:]
    upper_rest_ref[...] = redundant[:, :256]
    pack(leaf, rest, got, payload_ref, rest_ref)


def local(a_matrix, omega, leaf_pivots, upper_pivots, ranks):
    z, core, y, x = (lax.axis_index(name) for name in ("z", "core", "y", "x"))
    row_index = z * 2 + core
    place = jnp.stack([x, y, core]).astype(jnp.int32)

    near = jnp.where(core == 0, 1, 3)
    far = 4 - near
    bit = [jnp.arange(16) >> i & 1 for i in (3, 2, 1, 0)]
    leaf_owners = ((y ^ bit[1] * near ^ bit[3] * far) * 4 + (x ^ bit[0] * near ^ bit[2] * far))
    upper_owners = ((y ^ bit[0] * near ^ bit[3] * far) * 4 + (x ^ bit[1] * near ^ bit[2] * far))
    position = jnp.arange(K)
    leaf_order = jnp.where(position < ranks[0, row_index], leaf_pivots[0, :K], -1)[None]
    leaf_rest = jnp.take(leaf_pivots[0, K:].reshape(16, 96), leaf_owners, axis=0)
    leaf_rest = jnp.pad(leaf_rest, ((0, 0), (0, 32)), constant_values=-1).reshape(1, LEAF)
    orders = []
    for level in (1, 2, 3):
        node, side = row_index >> level, row_index >> (level - 1) & 1
        pivots = upper_pivots[level - 1, node] ^ (side << 9)
        kept = jnp.where(position < ranks[level, node], pivots[:K], -1)
        rest = jnp.take(pivots[K:].reshape(16, 32), upper_owners, axis=0).reshape(K)
        orders.append(jnp.concatenate([kept, rest])[None])

    send = ordered_samples(place, omega, a_matrix, True)
    got = hop(send[0], "x", True), hop(send[1], "y", True)
    kept = ordered_samples(place, omega, a_matrix, False)
    for axes, first in (("xy", False), ("yx", True), ("yx", False)):
        send = added(kept, got, kept[0].shape[0] // 2, "add_sent")
        kept = added(kept, got, 0, "add_kept")
        got = hop(send[0], axes[0], first), hop(send[1], axes[1], first)
    leaf_skeleton, parts = finished(leaf_order, (kept[0], got[0]), (kept[1], got[1]))

    small = (32, K)
    sibling = swapped(leaf_skeleton, "core", 1)
    skeleton_1, redundant_1 = call(
        level_1_kernel, "level_1", (orders[0], leaf_skeleton, sibling), (small, small)
    )
    sibling = swapped(skeleton_1, "z", 1)
    leaf, rest = call(
        leaf_kernel,
        "leaf_redundant",
        (leaf_rest, parts, leaf_skeleton),
        ((32, 3 * K), (32, 2 * K)),
        (skeleton_1,),
    )
    got = hop(leaf, "x", True)
    skeleton_2, redundant_2, leaf, rest = call(
        level_2_kernel,
        "level_2",
        (orders[1], skeleton_1, sibling, leaf, rest, got),
        (small, small, (64, 2 * K), (64, K)),
    )
    inner = (z ^ z >> 1) & 1
    sibling = lax.ppermute(skeleton_2, "z", [(i, i ^ 3) for i in (1, 2, 5, 6)])
    got = hop(leaf, "y", True)
    which = jnp.broadcast_to(jnp.where(core == 0, 0, 1 + inner), (1, 128)).astype(jnp.int32)
    upper, upper_rest, leaf, rest = call(
        level_3_kernel,
        "level_3",
        (orders[2], skeleton_2, sibling, leaf, rest, got, which)
        + (skeleton_1, redundant_1, redundant_2),
        ((32, K + 256), (32, 256), (128, K + 256), (128, 256)),
    )
    upper_got = hop(upper, "y", True)
    got = hop(leaf, "x", False)
    upper, upper_rest = call(
        pack_kernel, "upper_2", (upper, upper_rest, upper_got), ((64, K + 128), (64, 128))
    )
    upper_got = hop(upper, "x", True)
    leaf, rest = call(pack_kernel, "leaf_4", (leaf, rest, got), ((256, K + 128), (256, 128)))
    got = hop(leaf, "y", False)
    (upper,) = call(pack_all_kernel, "upper_3", (upper, upper_rest, upper_got), ((128, K + 128),))
    upper_got = hop(upper, "x", False)
    (upper,) = call(stack_kernel, "upper_4", (upper, upper_got), ((256, K + 128),))
    upper_got = hop(upper, "y", False)
    leaf_interp = solve((leaf, rest, got), 96, False)
    upper_interp = solve((upper, upper_got), 32, True, (leaf_interp,))

    other = swapped(upper_interp, "core", 1)
    level_1 = jnp.where(core == 0, upper_interp, other)
    chip = jnp.where(core == 0, other, upper_interp)
    beside = swapped(chip, "z", 1)
    level_2 = jnp.where(inner == 0, chip, beside)
    level_3 = jnp.where(inner == 0, beside, chip)
    return (leaf_interp[None], jnp.stack([level_1, level_2, level_3])[:, None])


def solution(mesh):
    grid = Mesh(mesh.devices.reshape(8, 2, 4, 4), ("z", "core", "y", "x"))
    row, col = ("z", "core"), ("y", "x")
    return jax.shard_map(
        local,
        mesh=grid,
        in_specs=(P(row, col), P(col, None), P(row, None), P(), P()),
        out_specs=(P(row, col, None), P(None, row, col, None)),
        check_vma=False,
    )
```

time: 138 us -> 129 us (0.935)
  blocking collectives: 32.9 us -> 0 us
  waiting for transfers between devices: 19.5 us -> 43.1 us
  matrix products: 7.08 us -> 0 us
  Pallas kernels: 24.9 us -> 30.4 us
  starting transfers between devices: 33.1 us -> 36.7 us
    all_to_all x1 -> x0, blocking collectives: 32.9 us -> none  [local(): lax.all_to_all(spread, ('y', 'x'), 0, 0, tiled=False)]
    ppermute x8 -> x16, waiting for transfers between devices: 16.9 us -> 37 us  [hop(): return lax.ppermute(block, ('core', axis), route)]
    dot_general x4 -> x0, matrix products: 7.08 us -> none  [pick(): parts = jnp.dot(split3(value), chosen, preferred_element_type=F32)]
    unnamed x8 -> x22, local copies, waits for them, and re-layouts: 4.2 us -> 8.72 us
    pallas_call x2, Pallas kernels: 9.11 us -> 13.3 us  [ordered_samples(): pl.pallas_call(functools.partial(ordered_kernel, sent=sent), grid_spec=pl...]
    ppermute x5 -> x4, waiting for transfers between devices: 2.66 us -> 6.18 us  [swapped(): return lax.ppermute(block, axis, [(i, i ^ mask) for i in range(count)])]
    add x11 -> x0, other arithmetic: 2.81 us -> none  [the longest x2 1.48 us: local(): sum_a, sum_b = (keep_a + got_a, keep_b + got_b)]
    select_n x4 -> x7, other arithmetic: 0.11 us -> 2.7 us  [the longest x3 1.89 us: local(): kept = jnp.where(position < ranks[level, node], pivots[:K], -1)]
  transfers between devices with their start and end apart: 13 -> 21, of which waited for: 9 -> 16; matrix products, arithmetic and copies ran while one was open for 6% -> 5% of each run, Pallas kernels for 9% -> 11%
where the time goes in v1:
time: 129 us; the launch traced here: 128 us
  waiting for transfers between devices  43.1 us (33%)
  starting transfers between devices  36.7 us (28%)
  Pallas kernels  30.4 us (24%)
  local copies, waits for them, and re-layouts  12.2 us (9%)
  other arithmetic  4.95 us (4%)
    ppermute x16, waiting for transfers between devices, hop(): return lax.ppermute(block, ('core', axis), route)  37 us
    ppermute x4, starting transfers between devices, swapped(): return lax.ppermute(block, axis, [(i, i ^ mask) for i in range(count)])  21 us
    ppermute x16, starting transfers between devices, hop(): return lax.ppermute(block, ('core', axis), route)  15 us
    pallas_call x2, Pallas kernels, ordered_samples(): pl.pallas_call(functools.partial(ordered_kernel, sent=sent), grid_spec=pl...  13.3 us
    pallas_call x2, Pallas kernels, solve(): pl.pallas_call(functools.partial(solve_kernel, packed=packed), out_shape=...  12.3 us
    unnamed x22, local copies, waits for them, and re-layouts  8.72 us
    ppermute x4, waiting for transfers between devices, swapped(): return lax.ppermute(block, axis, [(i, i ^ mask) for i in range(count)])  6.18 us
    pallas_call x8, Pallas kernels, call(): pl.pallas_call(kernel, in_specs=[VMEM] * len(inputs) + [ANY] * len(after)...  3.02 us
  transfers between devices with their start and end apart: 21, of which 16 were waited for; matrix products, arithmetic and copies ran while one was open for 5% of the time, Pallas kernels for 11%

profile of v1, /device:TPU:1, one launch (start us, length us, event | category | flops | bytes accessed | tf_op | source)
XLA Modules:
  0.0 128.3 jit_solution(6200496421609006808)
XLA Ops:
  0.6 0.7 pad_add_fusion.3.place_ref
  1.3 6.6 %sent_samples.1 = (f32[128,2048]{1,0:T(8,128)}, f32[128,2048]{1,0:T(8,128)}) custom-call(s32[3]{0:T(128)} %pad_add_fusion.3.place_ref, bf16[1536,512]{1,0:T(8,128)(2,1)} %omega_ref.3, bf16[2048,1536]{1,0:T(8,128)(2,1)} %a_ref.3), custom_call_target="tpu_custom_call" | custom-call | flops 2013265920 | bytes 9961472 | tf_op jit(solution)/shard_map/sent_samples/pallas_call | solution.py:71
  7.9 3.3 %collective-permute-start = (f32[128,2048]{1,0:T(8,128)}, f32[128,2048]{1,0:T(8,128)S(1)}, u32[]{:S(2)}, u32[]{:S(2)}) collective-permute-start(f32[128,2048]{1,0:T(8,128)} %get-tuple-element.38), channel_id=1, source_target_pairs={{0,1},{1,0},{2,3},{3,2},{16,19},{17,18},{18,17},{19,16},{4,5},{5,4... | collective-permute-start | bytes 3145736 | tf_op jit(solution)/shard_map/ppermute | solution.py:27
  11.2 2.7 %collective-permute-start.1 = (f32[128,2048]{1,0:T(8,128)}, f32[128,2048]{1,0:T(8,128)S(1)}, u32[]{:S(2)}, u32[]{:S(2)}) collective-permute-start(f32[128,2048]{1,0:T(8,128)} %get-tuple-element.40), channel_id=1, source_target_pairs={{0,4},{4,0},{8,12},{12,8},{16,28},{20,24},{24,20},{28,16},{1,5},{5... | collective-permute-start | bytes 3145736 | tf_op jit(solution)/shard_map/ppermute | solution.py:27
  14.0 0.8 dynamic-slice_xor_fusion
  15.0 0.6 gather_fusion.2
  15.6 0.6 gather_fusion.1
  16.2 0.6 gather_fusion.3
  16.8 6.7 %kept_samples.1 = (f32[128,2048]{1,0:T(8,128)}, f32[128,2048]{1,0:T(8,128)}) custom-call(s32[3]{0:T(128)} %pad_add_fusion.3.place_ref, bf16[1536,512]{1,0:T(8,128)(2,1)} %omega_ref.3, bf16[2048,1536]{1,0:T(8,128)(2,1)} %a_ref.3), custom_call_target="tpu_custom_call" | custom-call | flops 2013265920 | bytes 9961472 | tf_op jit(solution)/shard_map/kept_samples/pallas_call | solution.py:71
  23.5 0.2 collective-permute-done.got_a
  23.6 2.7 %collective-permute-done.1.got_b = f32[128,2048]{1,0:T(8,128)S(1)} collective-permute-done((f32[128,2048]{1,0:T(8,128)}, f32[128,2048]{1,0:T(8,128)S(1)}, u32[]{:S(2)}, u32[]{:S(2)}) %collective-permute-start.1) | collective-permute-done | bytes 1048608 | tf_op jit(solution)/shard_map/ppermute | solution.py:27
  26.4 1.2 copy-done
  27.6 1.2 copy-done.2
  28.8 1.1 add_sent.3
  29.9 0.3 collective-permute-start.3
  30.4 0.6 gather_fusion
  31.0 1.2 copy-done.1
  32.3 1.2 copy-done.3
  33.5 0.1 add_kept.3
  33.6 4.9 %collective-permute-done.2.got_a = f32[64,2048]{1,0:T(8,128)S(1)} collective-permute-done((f32[64,2048]{1,0:T(8,128)}, f32[64,2048]{1,0:T(8,128)S(1)}, u32[]{:S(2)}, u32[]{:S(2)}) %collective-permute-start.2) | collective-permute-done | bytes 524320 | tf_op jit(solution)/shard_map/ppermute | solution.py:27
  38.6 0.8 copy-done.4
  39.4 2.7 %collective-permute-start.4 = (f32[32,2048]{1,0:T(8,128)S(1)}, f32[32,2048]{1,0:T(8,128)S(1)}, u32[]{:S(2)}, u32[]{:S(2)}) collective-permute-start(f32[32,2048]{1,0:T(8,128)S(1)} %get-tuple-element.46), channel_id=1, source_target_pairs={{0,4},{4,0},{8,12},{12,8},{16,28},{20,24},{24,20},{28,16},{1,5},{5... | collective-permute-start | bytes 786440 | tf_op jit(solution)/shard_map/ppermute | solution.py:27
  42.0 0.8 collective-permute-start.5
  43.0 0.6 constant_dynamic-slice_fusion
  43.6 0.6 compare_select_fusion.order_ref
  44.3 1.0 copy-done.5
  45.3 1.0 copy-done.7
  46.4 2.0 %collective-permute-done.5.got_b = f32[32,2048]{1,0:T(8,128)S(1)} collective-permute-done((f32[32,2048]{1,0:T(8,128)S(1)}, f32[32,2048]{1,0:T(8,128)S(1)}, u32[]{:S(2)}, u32[]{:S(2)}) %collective-permute-start.5) | collective-permute-done | bytes 262176 | tf_op jit(solution)/shard_map/ppermute | solution.py:27
  48.6 0.6 collective-permute-start.7
  49.2 0.6 fusion.2
  49.9 2.5 %collective-permute-done.6.refs_1_ = f32[16,2048]{1,0:T(8,128)S(1)} collective-permute-done((f32[16,2048]{1,0:T(8,128)S(1)}, f32[16,2048]{1,0:T(8,128)S(1)}, u32[]{:S(2)}, u32[]{:S(2)}) %collective-permute-start.6) | collective-permute-done | bytes 131104 | tf_op jit(solution)/shard_map/ppermute | solution.py:27
  52.4 0.1 collective-permute-done.7.refs_3_
  52.5 0.5 finish_samples.1
  53.0 6.7 %collective-permute-start.8 = (f32[32,512]{1,0:T(8,128)S(1)}, f32[32,512]{1,0:T(8,128)S(1)}, u32[]{:S(2)}, u32[]{:S(2)}) collective-permute-start(f32[32,512]{1,0:T(8,128)S(1)} %get-tuple-element.53.own.skeleton_ref), channel_id=1, source_target_pairs={{0,16},{16,0},{1,17},{17,1},{2,18},{18,2},{3,19},{19,3},{4,20},{20... | collective-permute-start | bytes 196616 | tf_op jit(solution)/shard_map/ppermute | solution.py:32
  59.7 0.9 collective-permute-done.8.sibling
  60.6 0.5 level_1.1
  61.1 1.5 %leaf_redundant.1 = (f32[32,1536]{1,0:T(8,128)S(1)}, f32[32,1024]{1,0:T(8,128)S(1)}) custom-call(s32[1,2048]{1,0:T(1,128)S(1)} %bitcast.27, bf16[96,2048]{1,0:T(8,128)(2,1)S(1)} %get-tuple-element.55.parts_ref, f32[32,512]{1,0:T(8,128)S(1)} %get-tuple-element.53.own.skeleton_ref, f32[32,512]{1,0:T(8,128)S(1)} %get-tuple-element.54._.own.skeleton_1), custom_call_target="tpu_custom_call" | custom-call | flops 1000000 | bytes 1000000 | tf_op jit(solution)/shard_map/leaf_redundant/pallas_call | solution.py:237
  62.5 1.0 collective-permute-start.10
  63.5 0.6 fusion.1
  64.3 1.7 %collective-permute-start.9 = (f32[32,512]{1,0:T(8,128)S(1)}, f32[32,512]{1,0:T(8,128)S(1)}, u32[]{:S(2)}, u32[]{:S(2)}) collective-permute-start(f32[32,512]{1,0:T(8,128)S(1)} %get-tuple-element.54._.own.skeleton_1), channel_id=1, source_target_pairs={{0,32},{32,0},{64,96},{96,64},{128,160},{160,128},{192,224},{224,1... | collective-permute-start | bytes 196616 | tf_op jit(solution)/shard_map/ppermute | solution.py:32
  66.0 2.2 %collective-permute-done.9.sibling = f32[32,512]{1,0:T(8,128)S(1)} collective-permute-done((f32[32,512]{1,0:T(8,128)S(1)}, f32[32,512]{1,0:T(8,128)S(1)}, u32[]{:S(2)}, u32[]{:S(2)}) %collective-permute-start.9) | collective-permute-done | bytes 65568 | tf_op jit(solution)/shard_map/ppermute | solution.py:32
  68.2 0.1 collective-permute-done.10.got
  68.3 0.5 level_2.1
  68.8 0.2 collective-permute-start.12
  68.9 0.6 fusion
  69.6 0.7 collective-permute-start.11
  70.3 5.1 %collective-permute-done.12.got = f32[64,1024]{1,0:T(8,128)S(1)} collective-permute-done((f32[64,1024]{1,0:T(8,128)S(1)}, f32[64,1024]{1,0:T(8,128)S(1)}, u32[]{:S(2)}, u32[]{:S(2)}) %collective-permute-start.12) | collective-permute-done | bytes 262176 | tf_op jit(solution)/shard_map/ppermute | solution.py:27
  75.4 0.5 level_3.1
  75.9 0.1 collective-permute-start.15
  76.0 6.8 %collective-permute-done.13.got = f32[128,768]{1,0:T(8,128)S(1)} collective-permute-done((f32[128,768]{1,0:T(8,128)S(1)}, f32[128,768]{1,0:T(8,128)S(1)}, u32[]{:S(2)}, u32[]{:S(2)}) %collective-permute-start.13) | collective-permute-done | bytes 393248 | tf_op jit(solution)/shard_map/ppermute | solution.py:27
  82.9 0.6 collective-permute-start.14
  83.5 1.2 collective-permute-start.16
  84.7 4.3 %collective-permute-done.16.got = f32[64,640]{1,0:T(8,128)S(1)} collective-permute-done((f32[64,640]{1,0:T(8,128)S(1)}, f32[64,640]{1,0:T(8,128)S(1)}, u32[]{:S(2)}, u32[]{:S(2)}) %collective-permute-start.16) | collective-permute-done | bytes 163872 | tf_op jit(solution)/shard_map/ppermute | solution.py:27
  89.1 6.2 %collective-permute-done.17.got = f32[128,640]{1,0:T(8,128)S(1)} collective-permute-done((f32[128,640]{1,0:T(8,128)S(1)}, f32[128,640]{1,0:T(8,128)S(1)}, u32[]{:S(2)}, u32[]{:S(2)}) %collective-permute-start.17) | collective-permute-done | bytes 327712 | tf_op jit(solution)/shard_map/ppermute | solution.py:27
  95.4 1.3 collective-permute-start.18
  96.6 6.7 %solve_leaf.1.refs_2_ = f32[96,512]{1,0:T(8,128)} custom-call(f32[256,640]{1,0:T(8,128)S(1)} %get-tuple-element.65.refs_0_, f32[256,128]{1,0:T(8,128)S(1)} %get-tuple-element.66.refs_1_, f32[256,640]{1,0:T(8,128)S(1)} %collective-permute-done.14.refs_2_), custom_call_target="tpu_custom_call" | custom-call | flops 5737807872 | bytes 1245184 | tf_op jit(solution)/shard_map/solve_leaf/pallas_call | solution.py:153
  103.4 2.0 %collective-permute-done.18.refs_1_ = f32[256,640]{1,0:T(8,128)S(1)} collective-permute-done((f32[256,640]{1,0:T(8,128)S(1)}, f32[256,640]{1,0:T(8,128)S(1)}, u32[]{:S(2)}, u32[]{:S(2)}) %collective-permute-start.18) | collective-permute-done | bytes 655392 | tf_op jit(solution)/shard_map/ppermute | solution.py:27
  105.4 0.9 copy-done.8
  106.3 5.5 %solve_upper.1 = f32[32,512]{1,0:T(8,128)S(1)} custom-call(f32[256,640]{1,0:T(8,128)S(1)} %upper_4.1.refs_0_, f32[256,640]{1,0:T(8,128)S(1)} %collective-permute-done.18.refs_1_, f32[96,512]{1,0:T(8,128)S(1)} %copy-done.8), custom_call_target="tpu_custom_call" | custom-call | flops 5133828096 | bytes 1114112 | tf_op jit(solution)/shard_map/solve_upper/pallas_call | solution.py:153
  111.8 6.5 %collective-permute-start.19 = (f32[32,512]{1,0:T(8,128)S(1)}, f32[32,512]{1,0:T(8,128)S(1)}, u32[]{:S(2)}, u32[]{:S(2)}) collective-permute-start(f32[32,512]{1,0:T(8,128)S(1)} %solve_upper.1), channel_id=1, source_target_pairs={{0,16},{16,0},{1,17},{17,1},{2,18},{18,2},{3,19},{19,3},{4,20},{20... | collective-permute-start | bytes 196616 | tf_op jit(solution)/shard_map/ppermute | solution.py:32
  118.3 0.9 collective-permute-done.19
  119.2 6.2 %collective-permute-start.20 = (f32[32,512]{1,0:T(8,128)S(1)}, f32[32,512]{1,0:T(8,128)S(1)}, u32[]{:S(2)}, u32[]{:S(2)}) collective-permute-start(f32[32,512]{1,0:T(8,128)S(1)} %get-tuple-element.76), channel_id=1, source_target_pairs={{0,32},{32,0},{64,96},{96,64},{128,160},{160,128},{192,224},{224,1... | collective-permute-start | bytes 196616 | tf_op jit(solution)/shard_map/ppermute | solution.py:32
  125.4 2.2 %collective-permute-done.20 = f32[32,512]{1,0:T(8,128)S(1)} collective-permute-done((f32[32,512]{1,0:T(8,128)S(1)}, f32[32,512]{1,0:T(8,128)S(1)}, u32[]{:S(2)}, u32[]{:S(2)}) %collective-permute-start.20) | collective-permute-done | bytes 65568 | tf_op jit(solution)/shard_map/ppermute | solution.py:32
  127.6 0.7 maximum_bitcast_fusion
  (54 shorter events, 1.4 us)
Async XLA Ops:
  7.9 22.3 %copy-start.9 = (s32[1,2048]{1,0:T(1,128)S(1)}, s32[1,2048]{1,0:T(1,128)}, u32[]{:S(2)}) copy-start(s32[1,2048]{1,0:T(1,128)} %param.9) | copy-start | bytes 24580
  7.9 15.7 %collective-permute-start = (f32[128,2048]{1,0:T(8,128)}, f32[128,2048]{1,0:T(8,128)S(1)}, u32[]{:S(2)}, u32[]{:S(2)}) collective-permute-start(f32[128,2048]{1,0:T(8,128)} %get-tuple-element.38), channel_id=1, source_target_pairs={{0,1},{1,0},{2,3},{3,2},{16,19},{17,18},{18,17},{19,16},{4,5},{5,4... | collective-permute-start | bytes 3145736 | tf_op jit(solution)/shard_map/ppermute | solution.py:27
  11.2 15.1 %collective-permute-start.1 = (f32[128,2048]{1,0:T(8,128)}, f32[128,2048]{1,0:T(8,128)S(1)}, u32[]{:S(2)}, u32[]{:S(2)}) collective-permute-start(f32[128,2048]{1,0:T(8,128)} %get-tuple-element.40), channel_id=1, source_target_pairs={{0,4},{4,0},{8,12},{12,8},{16,28},{20,24},{24,20},{28,16},{1,5},{5... | collective-permute-start | bytes 3145736 | tf_op jit(solution)/shard_map/ppermute | solution.py:27
  23.5 19.5 %copy-start.10 = (s32[4,16]{1,0:T(4,128)S(1)}, s32[4,16]{1,0:T(4,128)}, u32[]{:S(2)}) copy-start(s32[4,16]{1,0:T(4,128)} %param.11) | copy-start | bytes 772
  26.4 1.2 copy-start
  27.6 1.2 copy-start.2
  29.9 8.5 %collective-permute-start.2 = (f32[64,2048]{1,0:T(8,128)}, f32[64,2048]{1,0:T(8,128)S(1)}, u32[]{:S(2)}, u32[]{:S(2)}) collective-permute-start(f32[64,2048]{1,0:T(8,128)} %get-tuple-element.42), channel_id=1, source_target_pairs={{0,3},{1,2},{2,1},{3,0},{16,17},{17,16},{18,19},{19,18},{4,7},{5,6... | collective-permute-start | bytes 1572872 | tf_op jit(solution)/shard_map/ppermute | solution.py:27
  29.9 8.5 %collective-permute-start.3 = (f32[64,2048]{1,0:T(8,128)}, f32[64,2048]{1,0:T(8,128)S(1)}, u32[]{:S(2)}, u32[]{:S(2)}) collective-permute-start(f32[64,2048]{1,0:T(8,128)} %get-tuple-element.44), channel_id=1, source_target_pairs={{0,12},{4,8},{8,4},{12,0},{16,20},{20,16},{24,28},{28,24},{1,13},{... | collective-permute-start | bytes 1572872 | tf_op jit(solution)/shard_map/ppermute | solution.py:27
  31.0 1.2 copy-start.1
  32.3 1.2 copy-start.3
  33.6 5.0 %copy-start.6 = (f32[64,2048]{1,0:T(8,128)}, f32[64,2048]{1,0:T(8,128)S(1)}, u32[]{:S(2)}) copy-start(f32[64,2048]{1,0:T(8,128)S(1)} %get-tuple-element.43.kept_b) | copy-start | bytes 1572868
  38.5 0.8 copy-start.4
  39.4 7.1 %collective-permute-start.4 = (f32[32,2048]{1,0:T(8,128)S(1)}, f32[32,2048]{1,0:T(8,128)S(1)}, u32[]{:S(2)}, u32[]{:S(2)}) collective-permute-start(f32[32,2048]{1,0:T(8,128)S(1)} %get-tuple-element.46), channel_id=1, source_target_pairs={{0,4},{4,0},{8,12},{12,8},{16,28},{20,24},{24,20},{28,16},{1,5},{5... | collective-permute-start | bytes 786440 | tf_op jit(solution)/shard_map/ppermute | solution.py:27
  42.0 6.4 %collective-permute-start.5 = (f32[32,2048]{1,0:T(8,128)S(1)}, f32[32,2048]{1,0:T(8,128)S(1)}, u32[]{:S(2)}, u32[]{:S(2)}) collective-permute-start(f32[32,2048]{1,0:T(8,128)S(1)} %get-tuple-element.48), channel_id=1, source_target_pairs={{0,1},{1,0},{2,3},{3,2},{16,19},{17,18},{18,17},{19,16},{4,5},{5,4... | collective-permute-start | bytes 786440 | tf_op jit(solution)/shard_map/ppermute | solution.py:27
  44.3 1.0 copy-start.5
  45.3 1.0 copy-start.7
  48.5 3.9 %collective-permute-start.6 = (f32[16,2048]{1,0:T(8,128)S(1)}, f32[16,2048]{1,0:T(8,128)S(1)}, u32[]{:S(2)}, u32[]{:S(2)}) collective-permute-start(f32[16,2048]{1,0:T(8,128)S(1)} %get-tuple-element.50), channel_id=1, source_target_pairs={{0,12},{4,8},{8,4},{12,0},{16,20},{20,16},{24,28},{28,24},{1,13},{... | collective-permute-start | bytes 393224 | tf_op jit(solution)/shard_map/ppermute | solution.py:27
  48.6 3.9 %collective-permute-start.7 = (f32[16,2048]{1,0:T(8,128)S(1)}, f32[16,2048]{1,0:T(8,128)S(1)}, u32[]{:S(2)}, u32[]{:S(2)}) collective-permute-start(f32[16,2048]{1,0:T(8,128)S(1)} %get-tuple-element.52), channel_id=1, source_target_pairs={{0,3},{1,2},{2,1},{3,0},{16,17},{17,16},{18,19},{19,18},{4,7},{5,6... | collective-permute-start | bytes 393224 | tf_op jit(solution)/shard_map/ppermute | solution.py:27
  53.0 7.6 %collective-permute-start.8 = (f32[32,512]{1,0:T(8,128)S(1)}, f32[32,512]{1,0:T(8,128)S(1)}, u32[]{:S(2)}, u32[]{:S(2)}) collective-permute-start(f32[32,512]{1,0:T(8,128)S(1)} %get-tuple-element.53.own.skeleton_ref), channel_id=1, source_target_pairs={{0,16},{16,0},{1,17},{17,1},{2,18},{18,2},{3,19},{19,3},{4,20},{20... | collective-permute-start | bytes 196616 | tf_op jit(solution)/shard_map/ppermute | solution.py:32
  62.5 5.8 %collective-permute-start.10 = (f32[32,1536]{1,0:T(8,128)S(1)}, f32[32,1536]{1,0:T(8,128)S(1)}, u32[]{:S(2)}, u32[]{:S(2)}) collective-permute-start(f32[32,1536]{1,0:T(8,128)S(1)} %get-tuple-element.56.leaf), channel_id=1, source_target_pairs={{0,1},{1,0},{2,3},{3,2},{16,19},{17,18},{18,17},{19,16},{4,5},{5,4... | collective-permute-start | bytes 589832 | tf_op jit(solution)/shard_map/ppermute | solution.py:27
  64.3 3.9 %collective-permute-start.9 = (f32[32,512]{1,0:T(8,128)S(1)}, f32[32,512]{1,0:T(8,128)S(1)}, u32[]{:S(2)}, u32[]{:S(2)}) collective-permute-start(f32[32,512]{1,0:T(8,128)S(1)} %get-tuple-element.54._.own.skeleton_1), channel_id=1, source_target_pairs={{0,32},{32,0},{64,96},{96,64},{128,160},{160,128},{192,224},{224,1... | collective-permute-start | bytes 196616 | tf_op jit(solution)/shard_map/ppermute | solution.py:32
  68.8 6.6 %collective-permute-start.12 = (f32[64,1024]{1,0:T(8,128)S(1)}, f32[64,1024]{1,0:T(8,128)S(1)}, u32[]{:S(2)}, u32[]{:S(2)}) collective-permute-start(f32[64,1024]{1,0:T(8,128)S(1)} %get-tuple-element.59.leaf), channel_id=1, source_target_pairs={{0,4},{4,0},{8,12},{12,8},{16,28},{20,24},{24,20},{28,16},{1,5},{5... | collective-permute-start | bytes 786440 | tf_op jit(solution)/shard_map/ppermute | solution.py:27
  69.6 0.7 collective-permute-start.11
  75.9 7.0 %collective-permute-start.13 = (f32[128,768]{1,0:T(8,128)S(1)}, f32[128,768]{1,0:T(8,128)S(1)}, u32[]{:S(2)}, u32[]{:S(2)}) collective-permute-start(f32[128,768]{1,0:T(8,128)S(1)} %get-tuple-element.63.own), channel_id=1, source_target_pairs={{0,3},{1,2},{2,1},{3,0},{16,17},{17,16},{18,19},{19,18},{4,7},{5,6... | collective-permute-start | bytes 1179656 | tf_op jit(solution)/shard_map/ppermute | solution.py:27
  75.9 7.6 %collective-permute-start.15 = (f32[32,768]{1,0:T(8,128)S(1)}, f32[32,768]{1,0:T(8,128)S(1)}, u32[]{:S(2)}, u32[]{:S(2)}) collective-permute-start(f32[32,768]{1,0:T(8,128)S(1)} %get-tuple-element.67.own), channel_id=1, source_target_pairs={{0,4},{4,0},{8,12},{12,8},{16,28},{20,24},{24,20},{28,16},{1,5},{5... | collective-permute-start | bytes 294920 | tf_op jit(solution)/shard_map/ppermute | solution.py:27
  82.9 13.7 %collective-permute-start.14 = (f32[256,640]{1,0:T(8,128)S(1)}, f32[256,640]{1,0:T(8,128)S(1)}, u32[]{:S(2)}, u32[]{:S(2)}) collective-permute-start(f32[256,640]{1,0:T(8,128)S(1)} %get-tuple-element.65.refs_0_), channel_id=1, source_target_pairs={{0,12},{4,8},{8,4},{12,0},{16,20},{20,16},{24,28},{28,24},{1,13},{... | collective-permute-start | bytes 1966088 | tf_op jit(solution)/shard_map/ppermute | solution.py:27
  83.5 5.5 %collective-permute-start.16 = (f32[64,640]{1,0:T(8,128)S(1)}, f32[64,640]{1,0:T(8,128)S(1)}, u32[]{:S(2)}, u32[]{:S(2)}) collective-permute-start(f32[64,640]{1,0:T(8,128)S(1)} %get-tuple-element.69.own), channel_id=1, source_target_pairs={{0,1},{1,0},{2,3},{3,2},{16,19},{17,18},{18,17},{19,16},{4,5},{5,4... | collective-permute-start | bytes 491528 | tf_op jit(solution)/shard_map/ppermute | solution.py:27
  89.0 6.3 %collective-permute-start.17 = (f32[128,640]{1,0:T(8,128)S(1)}, f32[128,640]{1,0:T(8,128)S(1)}, u32[]{:S(2)}, u32[]{:S(2)}) collective-permute-start(f32[128,640]{1,0:T(8,128)S(1)} %upper_3.1.own), channel_id=1, source_target_pairs={{0,3},{1,2},{2,1},{3,0},{16,17},{17,16},{18,19},{19,18},{4,7},{5,6... | collective-permute-start | bytes 983048 | tf_op jit(solution)/shard_map/ppermute | solution.py:27
  95.4 10.0 %collective-permute-start.18 = (f32[256,640]{1,0:T(8,128)S(1)}, f32[256,640]{1,0:T(8,128)S(1)}, u32[]{:S(2)}, u32[]{:S(2)}) collective-permute-start(f32[256,640]{1,0:T(8,128)S(1)} %upper_4.1.refs_0_), channel_id=1, source_target_pairs={{0,12},{4,8},{8,4},{12,0},{16,20},{20,16},{24,28},{28,24},{1,13},{... | collective-permute-start | bytes 1966088 | tf_op jit(solution)/shard_map/ppermute | solution.py:27
  105.4 0.9 copy-start.8
  111.8 7.4 %collective-permute-start.19 = (f32[32,512]{1,0:T(8,128)S(1)}, f32[32,512]{1,0:T(8,128)S(1)}, u32[]{:S(2)}, u32[]{:S(2)}) collective-permute-start(f32[32,512]{1,0:T(8,128)S(1)} %solve_upper.1), channel_id=1, source_target_pairs={{0,16},{16,0},{1,17},{17,1},{2,18},{18,2},{3,19},{19,3},{4,20},{20... | collective-permute-start | bytes 196616 | tf_op jit(solution)/shard_map/ppermute | solution.py:32
  119.2 8.4 %collective-permute-start.20 = (f32[32,512]{1,0:T(8,128)S(1)}, f32[32,512]{1,0:T(8,128)S(1)}, u32[]{:S(2)}, u32[]{:S(2)}) collective-permute-start(f32[32,512]{1,0:T(8,128)S(1)} %get-tuple-element.76), channel_id=1, source_target_pairs={{0,32},{32,0},{64,96},{96,64},{128,160},{160,128},{192,224},{224,1... | collective-permute-start | bytes 196616 | tf_op jit(solution)/shard_map/ppermute | solution.py:32

commit v2 on v1

--- a/solution.py
+++ b/solution.py
@@ -32,10 +32,12 @@
     return lax.ppermute(block, axis, [(i, i ^ mask) for i in range(count)])
 
 
-def ordered_kernel(place_ref, omega_ref, a_ref, out_a_ref, out_b_ref, lhs_ref, *, sent):
+def ordered_kernel(omega_ref, a_ref, *refs, sent):
+    lhs_ref = refs[4]
+
     @pl.when(pl.program_id(0) == 0)
     def _():
-        x, y, core = place_ref[0], place_ref[1], place_ref[2]
+        x, y, core = (lax.axis_index(name) for name in ("x", "y", "core"))
         near = jnp.where(core == 0, 1, 3)
         far = jnp.where(core == 0, 3, 1)
         row = lax.broadcasted_iota(jnp.int32, (256, 1), 0)
@@ -60,35 +62,32 @@
     rows = lax.dot_general(
         lhs_ref[...], a_ref[...], (((1,), (1,)), ((), ())), preferred_element_type=F32
     )
-    out_a_ref[...] = rows[:128]
-    out_b_ref[...] = rows[128:]
-
-
-def ordered_samples(place, omega, a_matrix, sent):
+    for i in range(4):
+        refs[i][...] = rows[64 * i : 64 * i + 64]
+
+
+def ordered_samples(omega, a_matrix, sent):
     depth = a_matrix.shape[1]
     block = 1024
-    out = jax.ShapeDtypeStruct((128, LEAF), F32)
+    out = jax.ShapeDtypeStruct((64, LEAF), F32)
     return pl.pallas_call(
         functools.partial(ordered_kernel, sent=sent),
-        grid_spec=pltpu.PrefetchScalarGridSpec(
-            num_scalar_prefetch=1,
-            grid=(LEAF // block,),
-            in_specs=[
-                pl.BlockSpec((depth, S), lambda i, _: (0, 0)),
-                pl.BlockSpec((block, depth), lambda i, _: (i, 0)),
-            ],
-            out_specs=[pl.BlockSpec((128, block), lambda i, _: (0, i))] * 2,
-            scratch_shapes=[pltpu.VMEM((256, depth), BF16)],
-        ),
-        out_shape=[out, out],
-        compiler_params=pltpu.CompilerParams(vmem_limit_bytes=56 * 2**20),
+        grid=(LEAF // block,),
+        in_specs=[
+            pl.BlockSpec((depth, S), lambda i: (0, 0)),
+            pl.BlockSpec((block, depth), lambda i: (i, 0)),
+        ],
+        out_specs=[pl.BlockSpec((64, block), lambda i: (0, i))] * 4,
+        scratch_shapes=[pltpu.VMEM((256, depth), BF16)],
+        out_shape=[out] * 4,
+        compiler_params=pltpu.CompilerParams(vmem_limit_bytes=(56 if sent else 16) * 2**20),
         cost_estimate=pl.CostEstimate(
             flops=2 * 256 * depth * (LEAF + S),
             bytes_accessed=2 * depth * (LEAF + S) + 4 * 256 * LEAF,
             transcendentals=0,
         ),
         name="sent_samples" if sent else "kept_samples",
-    )(place, omega, a_matrix)
+    )(omega, a_matrix)
 
 
 def parts2(value):
@@ -101,11 +100,11 @@
 
 
 def solve_kernel(*refs, packed):
-    out_ref = refs[-1]
+    out_ref = refs[-2]
+    refs[-1][...] = jnp.zeros_like(refs[-1])
     if packed:
-        own_ref, got_ref = refs[:2]
-        skeleton = jnp.concatenate([own_ref[:, :K], got_ref[:, :K]], 0)
-        pieces = [own_ref[:128], own_ref[128:], got_ref[:128], got_ref[128:]]
+        pieces = refs[:4]
+        skeleton = jnp.concatenate([piece[:, :K] for piece in pieces], 0)
         redundant = jnp.concatenate(
             [
                 piece[:, K + 32 * slot : K + 32 * slot + 32]
@@ -152,9 +151,9 @@
 def solve(whole, rows, packed, after=()):
     return pl.pallas_call(
         functools.partial(solve_kernel, packed=packed),
-        out_shape=jax.ShapeDtypeStruct((rows, K), F32),
+        out_shape=[jax.ShapeDtypeStruct(shape, F32) for shape in ((rows, K), (8, 128))],
         in_specs=[VMEM] * len(whole) + [ANY] * len(after),
-        out_specs=VMEM,
+        out_specs=[VMEM] * 2,
         compiler_params=pltpu.CompilerParams(vmem_limit_bytes=24 * 2**20),
         cost_estimate=pl.CostEstimate(
             flops=6 * 6 * (K + rows) * K * K, bytes_accessed=4 * (S + rows) * K, transcendentals=0
@@ -170,8 +169,7 @@
     out_b[...] = kept_b[part] + got_b[part]
 
 
-def added(kept, got, first, name):
-    rows = kept[0].shape[0] // 2
+def added(kept, got, first, rows, name):
     out = jax.ShapeDtypeStruct((rows, LEAF), F32)
     return pl.pallas_call(
         functools.partial(add_kernel, first=first),
@@ -202,7 +200,7 @@
 
 
 def finish_kernel(order_ref, *refs):
-    terms, (skeleton_ref, parts_ref) = refs[:-2], refs[-2:]
+    terms, (skeleton_ref, parts_ref) = refs[:4], refs[-2:]
     half = len(terms) // 2
     totals = []
     for group in (terms[:half], terms[half:]):
@@ -215,11 +213,11 @@
     skeleton_ref[...] = picked(parts, order_ref[...])
 
 
-def finished(order, terms_a, terms_b):
+def finished(order, terms_a, terms_b, after):
     terms = [*terms_a, *terms_b]
     return pl.pallas_call(
         finish_kernel,
-        in_specs=[VMEM] * (1 + len(terms)),
+        in_specs=[VMEM] * (1 + len(terms)) + [ANY] * len(after),
         out_specs=[VMEM] * 2,
         out_shape=[
             jax.ShapeDtypeStruct((32, K), F32),
@@ -230,7 +228,7 @@
             flops=2 * 96 * LEAF * K, bytes_accessed=4 * 16 * len(terms) * LEAF, transcendentals=0
         ),
         name="finish_samples",
-    )(order, *terms)
+    )(order, *terms, *after)
 
 
 def call(kernel, name, inputs, shapes, after=(), flops=10**6):
@@ -245,7 +243,7 @@
     )(*inputs, *after)
 
 
-def leaf_kernel(order_ref, parts_ref, skeleton_ref, _, payload_ref, rest_ref):
+def leaf_kernel(order_ref, parts_ref, skeleton_ref, payload_ref, rest_ref):
     parts = parts_ref[...]
     payload_ref[:, :K] = skeleton_ref[...]
     for i in range(4):
@@ -267,8 +265,8 @@
     rest_ref[rows:] = got[:, K : K + half]
 
 
-def pack_kernel(own, rest, got, payload_ref, rest_ref):
-    pack(own, rest, got, payload_ref, rest_ref)
+def pack_kernel(own, rest, got, *refs):
+    pack(own, rest, got, *refs[-2:])
 
 
 def pack_all_kernel(own, rest, got, payload_ref):
@@ -278,23 +276,15 @@
     payload_ref[rows:] = got[...]
 
 
-def stack_kernel(own, got, payload_ref):
-    rows = own.shape[0]
-    payload_ref[:rows] = own[...]
-    payload_ref[rows:] = got[...]
-
-
 def level_1_kernel(order, own, sibling, skeleton_ref, redundant_ref):
     moved = picked(parts3(jnp.concatenate([own[...], sibling[...]], 1)), order[...])
     skeleton_ref[...] = moved[:, :K]
     redundant_ref[...] = moved[:, K:]
 
 
-def level_2_kernel(
-    order, own, sibling, leaf, rest, got, skeleton_ref, redundant_ref, payload_ref, rest_ref
-):
+def level_2_kernel(order, own, sibling, leaf, skeleton_ref, redundant_ref, payload_ref):
     level_1_kernel(order, own, sibling, skeleton_ref, redundant_ref)
-    pack(leaf, rest, got, payload_ref, rest_ref)
+    payload_ref[...] = leaf[...]
 
 
 def level_3_kernel(
@@ -314,13 +304,12 @@
 def local(a_matrix, omega, leaf_pivots, upper_pivots, ranks):
     z, core, y, x = (lax.axis_index(name) for name in ("z", "core", "y", "x"))
     row_index = z * 2 + core
-    place = jnp.stack([x, y, core]).astype(jnp.int32)
 
     near = jnp.where(core == 0, 1, 3)
     far = 4 - near
     bit = [jnp.arange(16) >> i & 1 for i in (3, 2, 1, 0)]
-    leaf_owners = ((y ^ bit[1] * near ^ bit[3] * far) * 4 + (x ^ bit[0] * near ^ bit[2] * far))
-    upper_owners = ((y ^ bit[0] * near ^ bit[3] * far) * 4 + (x ^ bit[1] * near ^ bit[2] * far))
+    leaf_owners = (y ^ bit[2] * near ^ bit[3] * far) * 4 + (x ^ bit[0] * near ^ bit[1] * far)
+    upper_owners = (y ^ bit[0] * near ^ bit[3] * far) * 4 + (x ^ bit[1] * near ^ bit[2] * far)
     position = jnp.arange(K)
     leaf_order = jnp.where(position < ranks[0, row_index], leaf_pivots[0, :K], -1)[None]
     leaf_rest = jnp.take(leaf_pivots[0, K:].reshape(16, 96), leaf_owners, axis=0)
@@ -329,18 +318,23 @@
     for level in (1, 2, 3):
         node, side = row_index >> level, row_index >> (level - 1) & 1
         pivots = upper_pivots[level - 1, node] ^ (side << 9)
-        kept = jnp.where(position < ranks[level, node], pivots[:K], -1)
+        head = jnp.where(position < ranks[level, node], pivots[:K], -1)
         rest = jnp.take(pivots[K:].reshape(16, 32), upper_owners, axis=0).reshape(K)
-        orders.append(jnp.concatenate([kept, rest])[None])
-
-    send = ordered_samples(place, omega, a_matrix, True)
-    got = hop(send[0], "x", True), hop(send[1], "y", True)
-    kept = ordered_samples(place, omega, a_matrix, False)
-    for axes, first in (("xy", False), ("yx", True), ("yx", False)):
-        send = added(kept, got, kept[0].shape[0] // 2, "add_sent")
-        kept = added(kept, got, 0, "add_kept")
-        got = hop(send[0], axes[0], first), hop(send[1], axes[1], first)
-    leaf_skeleton, parts = finished(leaf_order, (kept[0], got[0]), (kept[1], got[1]))
+        orders.append(jnp.concatenate([head, rest])[None])
+
+    near_a, both_a, near_b, both_b = ordered_samples(omega, a_matrix, True)
+    got_both = hop(both_a, "x", True), hop(both_b, "y", True)
+    got_near = hop(near_a, "x", True), hop(near_b, "y", True)
+    own_a, far_a, own_b, far_b = ordered_samples(omega, a_matrix, False)
+    send = added((far_a, far_b), got_both, 0, 64, "add_sent")
+    got = hop(send[0], "x", False), hop(send[1], "y", False)
+    kept = added((own_a, own_b), got_near, 0, 64, "add_kept")
+
+    for rows, first in ((32, True), (16, False)):
+        send = added(kept, got, rows, rows, "add_sent")
+        kept = added(kept, got, 0, rows, "add_kept")
+        got = hop(send[0], "y", first), hop(send[1], "x", first)
+    leaf_skeleton, parts = finished(leaf_order, (kept[0], got[0]), (kept[1], got[1]), orders)
 
     small = (32, K)
     sibling = swapped(leaf_skeleton, "core", 1)
@@ -353,25 +347,24 @@
         "leaf_redundant",
         (leaf_rest, parts, leaf_skeleton),
         ((32, 3 * K), (32, 2 * K)),
-        (skeleton_1,),
-    )
-    got = hop(leaf, "x", True)
-    skeleton_2, redundant_2, leaf, rest = call(
+        flops=2 * 96 * LEAF * LEAF,
+    )
+    skeleton_2, redundant_2, leaf = call(
         level_2_kernel,
         "level_2",
-        (orders[1], skeleton_1, sibling, leaf, rest, got),
-        (small, small, (64, 2 * K), (64, K)),
+        (orders[1], skeleton_1, sibling, leaf),
+        (small, small, (32, 3 * K)),
     )
     inner = (z ^ z >> 1) & 1
     sibling = lax.ppermute(skeleton_2, "z", [(i, i ^ 3) for i in (1, 2, 5, 6)])
-    got = hop(leaf, "y", True)
+    got = hop(leaf, "x", True)
     which = jnp.broadcast_to(jnp.where(core == 0, 0, 1 + inner), (1, 128)).astype(jnp.int32)
     upper, upper_rest, leaf, rest = call(
         level_3_kernel,
         "level_3",
         (orders[2], skeleton_2, sibling, leaf, rest, got, which)
         + (skeleton_1, redundant_1, redundant_2),
-        ((32, K + 256), (32, 256), (128, K + 256), (128, 256)),
+        ((32, K + 256), (32, 256), (64, 2 * K), (64, K)),
     )
     upper_got = hop(upper, "y", True)
     got = hop(leaf, "x", False)
@@ -379,14 +372,19 @@
         pack_kernel, "upper_2", (upper, upper_rest, upper_got), ((64, K + 128), (64, 128))
     )
     upper_got = hop(upper, "x", True)
-    leaf, rest = call(pack_kernel, "leaf_4", (leaf, rest, got), ((256, K + 128), (256, 128)))
+    leaf, rest = call(
+        pack_kernel, "leaf_3", (leaf, rest, got), ((128, K + 256), (128, 256)), (upper,)
+    )
+    got = hop(leaf, "y", True)
+    (upper,) = call(pack_all_kernel, "upper_3", (upper, upper_rest, upper_got), ((128, K + 128),))
+    upper_got, across = hop(upper, "x", False), hop(upper, "y", False)
+    leaf, rest = call(
+        pack_kernel, "leaf_4", (leaf, rest, got), ((256, K + 128), (256, 128)), (upper,)
+    )
     got = hop(leaf, "y", False)
-    (upper,) = call(pack_all_kernel, "upper_3", (upper, upper_rest, upper_got), ((128, K + 128),))
-    upper_got = hop(upper, "x", False)
-    (upper,) = call(stack_kernel, "upper_4", (upper, upper_got), ((256, K + 128),))
-    upper_got = hop(upper, "y", False)
-    leaf_interp = solve((leaf, rest, got), 96, False)
-    upper_interp = solve((upper, upper_got), 32, True, (leaf_interp,))
+    beyond = hop(upper_got, "y", False)
+    leaf_interp, done = solve((leaf, rest, got), 96, False, (upper_got,))
+    upper_interp, _ = solve((upper, upper_got, across, beyond), 32, True, (done,))
 
     other = swapped(upper_interp, "core", 1)
     level_1 = jnp.where(core == 0, upper_interp, other)

time: 129 us -> 115 us (0.89)
  local copies, waits for them, and re-layouts: 12.2 us -> 6.31 us
  Pallas kernels: 30.4 us -> 26.7 us
  starting transfers between devices: 36.7 us -> 34.5 us
  waiting for transfers between devices: 43.1 us -> 41.1 us
    unnamed x22 -> x8, local copies, waits for them, and re-layouts: 8.72 us -> 2.79 us
    pallas_call x3, Pallas kernels: 13.8 us -> 9.38 us  [the longest x2 8.9 us: ordered_samples(): pl.pallas_call(functools.partial(ordered_kernel, sent=sent), grid=(LEAF /...]
    ppermute x4, starting transfers between devices: 21 us -> 16.9 us  [swapped(): return lax.ppermute(block, axis, [(i, i ^ mask) for i in range(count)])]
    ppermute x16 -> x19, starting transfers between devices: 15 us -> 17 us  [hop(): return lax.ppermute(block, ('core', axis), route)]
    ppermute x4, waiting for transfers between devices: 6.18 us -> 4.55 us  [swapped(): return lax.ppermute(block, axis, [(i, i ^ mask) for i in range(count)])]
    ppermute x16 -> x19, waiting for transfers between devices: 37 us -> 36.5 us  [hop(): return lax.ppermute(block, ('core', axis), route)]
  transfers between devices with their start and end apart: 21 -> 24, of which waited for: 16 -> 18; matrix products, arithmetic and copies ran while one was open for 5% -> 6% of each run, Pallas kernels for 11% -> 11%
where the time goes in v2:
time: 115 us; the launch traced here: 114 us
  waiting for transfers between devices  41.1 us (36%)
  starting transfers between devices  34.5 us (30%)
  Pallas kernels  26.7 us (23%)
  local copies, waits for them, and re-layouts  6.31 us (5%)
  other arithmetic  4.22 us (4%)
    ppermute x19, waiting for transfers between devices, hop(): return lax.ppermute(block, ('core', axis), route)  36.5 us
    ppermute x19, starting transfers between devices, hop(): return lax.ppermute(block, ('core', axis), route)  17 us
    ppermute x4, starting transfers between devices, swapped(): return lax.ppermute(block, axis, [(i, i ^ mask) for i in range(count)])  16.9 us
    pallas_call x2, Pallas kernels, solve(): pl.pallas_call(functools.partial(solve_kernel, packed=packed), out_shape=...  12.3 us
    pallas_call x2, Pallas kernels, ordered_samples(): pl.pallas_call(functools.partial(ordered_kernel, sent=sent), grid=(LEAF /...  8.9 us
    ppermute x4, waiting for transfers between devices, swapped(): return lax.ppermute(block, axis, [(i, i ^ mask) for i in range(count)])  4.55 us
    pallas_call x8, Pallas kernels, call(): pl.pallas_call(kernel, in_specs=[VMEM] * len(inputs) + [ANY] * len(after)...  2.97 us
    unnamed x8, local copies, waits for them, and re-layouts  2.79 us
  transfers between devices with their start and end apart: 24, of which 18 were waited for; matrix products, arithmetic and copies ran while one was open for 6% of the time, Pallas kernels for 11%

profile of v2, /device:TPU:1, one launch (start us, length us, event | category | flops | bytes accessed | tf_op | source)
XLA Modules:
  0.0 113.8 jit_solution(15947886975272330192)
XLA Ops:
  0.7 6.1 %sent_samples.1 = (f32[64,2048]{1,0:T(8,128)}, f32[64,2048]{1,0:T(8,128)}, f32[64,2048]{1,0:T(8,128)}, f32[64,2048]{1,0:T(8,128)}) custom-call(bf16[1536,512]{1,0:T(8,128)(2,1)} %omega_ref.3, bf16[2048,1536]{1,0:T(8,128)(2,1)} %a_ref.3), custom_call_target="tpu_custom_call" | custom-call | flops 2013265920 | bytes 9961472 | tf_op jit(solution)/shard_map/sent_samples/pallas_call | solution.py:73
  6.8 3.3 %collective-permute-start.2 = (f32[64,2048]{1,0:T(8,128)}, f32[64,2048]{1,0:T(8,128)S(1)}, u32[]{:S(2)}, u32[]{:S(2)}) collective-permute-start(f32[64,2048]{1,0:T(8,128)} %get-tuple-element.51), channel_id=1, source_target_pairs={{0,1},{1,0},{2,3},{3,2},{16,19},{17,18},{18,17},{19,16},{4,5},{5,4... | collective-permute-start | bytes 1572872 | tf_op jit(solution)/shard_map/ppermute | solution.py:27
  10.1 2.7 %collective-permute-start.3 = (f32[64,2048]{1,0:T(8,128)}, f32[64,2048]{1,0:T(8,128)}, u32[]{:S(2)}, u32[]{:S(2)}) collective-permute-start(f32[64,2048]{1,0:T(8,128)} %get-tuple-element.53), channel_id=1, source_target_pairs={{0,4},{4,0},{8,12},{12,8},{16,28},{20,24},{24,20},{28,16},{1,5},{5... | collective-permute-start | bytes 1572872 | tf_op jit(solution)/shard_map/ppermute | solution.py:27
  12.8 0.2 collective-permute-start
  13.0 0.8 dynamic-slice_xor_fusion
  14.1 0.6 gather_fusion.2
  14.6 0.6 gather_fusion.1
  15.3 0.6 gather_fusion.3
  15.9 0.1 reshape.144
  16.0 0.7 constant_dynamic-slice_fusion
  16.7 2.8 %copy-done = bf16[2048,1536]{1,0:T(8,128)(2,1)S(1)} copy-done((bf16[2048,1536]{1,0:T(8,128)(2,1)S(1)}, bf16[2048,1536]{1,0:T(8,128)(2,1)}, u32[]{:S(2)}) %copy-start) | copy-done | bytes 6291480
  19.5 2.8 %kept_samples.1 = (f32[64,2048]{1,0:T(8,128)S(1)}, f32[64,2048]{1,0:T(8,128)S(1)}, f32[64,2048]{1,0:T(8,128)S(1)}, f32[64,2048]{1,0:T(8,128)S(1)}) custom-call(bf16[1536,512]{1,0:T(8,128)(2,1)S(1)} %copy-done.1, bf16[2048,1536]{1,0:T(8,128)(2,1)S(1)} %copy-done), custom_call_target="tpu_custom_call" | custom-call | flops 2013265920 | bytes 9961472 | tf_op jit(solution)/shard_map/kept_samples/pallas_call | solution.py:73
  22.3 0.7 compare_select_fusion.order_ref
  23.0 1.2 %add_sent.3 = (f32[64,2048]{1,0:T(8,128)S(1)}, f32[64,2048]{1,0:T(8,128)S(1)}) custom-call(f32[64,2048]{1,0:T(8,128)S(1)} %get-tuple-element.50.kept_a, f32[64,2048]{1,0:T(8,128)S(1)} %collective-permute-done.2.got_a, f32[64,2048]{1,0:T(8,128)S(1)} %get-tuple-element.52.kept_b, f32[64,2048]{1,0:T(8,128)} %collective-permute-done.3.got_b), custom_call_target="tpu_custom_call" | custom-call | flops 262144 | bytes 3145728 | tf_op jit(solution)/shard_map/add_sent/pallas_call | solution.py:174
  24.1 0.1 collective-permute-start.4
  24.2 0.1 collective-permute-start.5
  24.3 0.6 fusion.2
  25.0 0.7 fusion.1
  25.7 0.1 add_kept.3
  25.8 6.8 %collective-permute-done.4.got_a = f32[64,2048]{1,0:T(8,128)S(1)} collective-permute-done((f32[64,2048]{1,0:T(8,128)S(1)}, f32[64,2048]{1,0:T(8,128)S(1)}, u32[]{:S(2)}, u32[]{:S(2)}) %collective-permute-start.4) | collective-permute-done | bytes 524320 | tf_op jit(solution)/shard_map/ppermute | solution.py:27
  32.5 0.1 collective-permute-done.5.got_b
  32.6 0.7 add_sent.4
  33.4 2.7 %collective-permute-start.6 = (f32[32,2048]{1,0:T(8,128)}, f32[32,2048]{1,0:T(8,128)S(1)}, u32[]{:S(2)}, u32[]{:S(2)}) collective-permute-start(f32[32,2048]{1,0:T(8,128)} %get-tuple-element.58), channel_id=1, source_target_pairs={{0,4},{4,0},{8,12},{12,8},{16,28},{20,24},{24,20},{28,16},{1,5},{5... | collective-permute-start | bytes 786440 | tf_op jit(solution)/shard_map/ppermute | solution.py:27
  36.1 2.5 %collective-permute-start.7 = (f32[32,2048]{1,0:T(8,128)S(1)}, f32[32,2048]{1,0:T(8,128)S(1)}, u32[]{:S(2)}, u32[]{:S(2)}) collective-permute-start(f32[32,2048]{1,0:T(8,128)S(1)} %get-tuple-element.60), channel_id=1, source_target_pairs={{0,1},{1,0},{2,3},{3,2},{16,19},{17,18},{18,17},{19,16},{4,5},{5,4... | collective-permute-start | bytes 786440 | tf_op jit(solution)/shard_map/ppermute | solution.py:27
  38.6 0.6 fusion
  39.3 0.8 collective-permute-done.6.got_a
  40.0 2.5 %collective-permute-done.7.got_b = f32[32,2048]{1,0:T(8,128)S(1)} collective-permute-done((f32[32,2048]{1,0:T(8,128)S(1)}, f32[32,2048]{1,0:T(8,128)S(1)}, u32[]{:S(2)}, u32[]{:S(2)}) %collective-permute-start.7) | collective-permute-done | bytes 262176 | tf_op jit(solution)/shard_map/ppermute | solution.py:27
  42.5 0.1 collective-permute-start.8
  42.6 0.9 collective-permute-start.9
  43.7 0.6 gather_fusion
  44.4 2.1 %collective-permute-done.8.refs_1_ = f32[16,2048]{1,0:T(8,128)S(1)} collective-permute-done((f32[16,2048]{1,0:T(8,128)S(1)}, f32[16,2048]{1,0:T(8,128)S(1)}, u32[]{:S(2)}, u32[]{:S(2)}) %collective-permute-start.8) | collective-permute-done | bytes 131104 | tf_op jit(solution)/shard_map/ppermute | solution.py:27
  46.4 0.1 collective-permute-done.9.refs_3_
  46.5 0.5 finish_samples.1
  47.0 7.5 %collective-permute-start.10 = (f32[32,512]{1,0:T(8,128)S(1)}, f32[32,512]{1,0:T(8,128)S(1)}, u32[]{:S(2)}, u32[]{:S(2)}) collective-permute-start(f32[32,512]{1,0:T(8,128)S(1)} %get-tuple-element.65.own.skeleton_ref), channel_id=1, source_target_pairs={{0,16},{16,0},{1,17},{17,1},{2,18},{18,2},{3,19},{19,3},{4,20},{20... | collective-permute-start | bytes 196616 | tf_op jit(solution)/shard_map/ppermute | solution.py:32
  54.6 0.8 collective-permute-done.10.sibling
  55.5 0.5 level_1.1
  55.9 1.8 %collective-permute-start.11 = (f32[32,512]{1,0:T(8,128)S(1)}, f32[32,512]{1,0:T(8,128)S(1)}, u32[]{:S(2)}, u32[]{:S(2)}) collective-permute-start(f32[32,512]{1,0:T(8,128)S(1)} %get-tuple-element.66.own.skeleton_1), channel_id=1, source_target_pairs={{0,32},{32,0},{64,96},{96,64},{128,160},{160,128},{192,224},{224,1... | collective-permute-start | bytes 196616 | tf_op jit(solution)/shard_map/ppermute | solution.py:32
  57.8 1.5 %leaf_redundant.1 = (f32[32,1536]{1,0:T(8,128)S(1)}, f32[32,1024]{1,0:T(8,128)S(1)}) custom-call(s32[1,2048]{1,0:T(1,128)S(1)} %bitcast.30, bf16[96,2048]{1,0:T(8,128)(2,1)S(1)} %get-tuple-element.67.parts_ref, f32[32,512]{1,0:T(8,128)S(1)} %get-tuple-element.65.own.skeleton_ref), custom_call_target="tpu_custom_call" | custom-call | flops 805306368 | bytes 1000000 | tf_op jit(solution)/shard_map/leaf_redundant/pallas_call | solution.py:235
  59.2 0.6 collective-permute-done.11.sibling
  59.9 0.5 level_2.1
  60.3 0.7 collective-permute-start.12
  61.0 5.0 %collective-permute-done.13.got = f32[32,1536]{1,0:T(8,128)S(1)} collective-permute-done((f32[32,1536]{1,0:T(8,128)S(1)}, f32[32,1536]{1,0:T(8,128)S(1)}, u32[]{:S(2)}, u32[]{:S(2)}) %collective-permute-start.13) | collective-permute-done | bytes 196640 | tf_op jit(solution)/shard_map/ppermute | solution.py:27
  66.1 0.5 level_3.1
  66.6 0.1 collective-permute-start.15
  66.7 4.7 %collective-permute-done.15.got = f32[32,768]{1,0:T(8,128)S(1)} collective-permute-done((f32[32,768]{1,0:T(8,128)S(1)}, f32[32,768]{1,0:T(8,128)S(1)}, u32[]{:S(2)}, u32[]{:S(2)}) %collective-permute-start.15) | collective-permute-done | bytes 98336 | tf_op jit(solution)/shard_map/ppermute | solution.py:27
  71.4 0.7 collective-permute-done.14.got
  72.2 0.1 collective-permute-start.16
  72.3 0.2 collective-permute-start.17
  72.5 5.3 %collective-permute-done.17.got = f32[64,640]{1,0:T(8,128)S(1)} collective-permute-done((f32[64,640]{1,0:T(8,128)S(1)}, f32[64,640]{1,0:T(8,128)S(1)}, u32[]{:S(2)}, u32[]{:S(2)}) %collective-permute-start.17) | collective-permute-done | bytes 163872 | tf_op jit(solution)/shard_map/ppermute | solution.py:27
  77.8 2.3 %collective-permute-done.16.got = f32[128,768]{1,0:T(8,128)S(1)} collective-permute-done((f32[128,768]{1,0:T(8,128)S(1)}, f32[128,768]{1,0:T(8,128)S(1)}, u32[]{:S(2)}, u32[]{:S(2)}) %collective-permute-start.16) | collective-permute-done | bytes 393248 | tf_op jit(solution)/shard_map/ppermute | solution.py:27
  80.1 0.2 collective-permute-start.18
  80.3 0.7 collective-permute-start.19
  81.0 1.4 %collective-permute-start.20 = (f32[128,640]{1,0:T(8,128)S(1)}, f32[128,640]{1,0:T(8,128)S(1)}, u32[]{:S(2)}, u32[]{:S(2)}) collective-permute-start(f32[128,640]{1,0:T(8,128)S(1)} %upper_3.1.refs_0_), channel_id=1, source_target_pairs={{0,12},{4,8},{8,4},{12,0},{16,20},{20,16},{24,28},{28,24},{1,13},{... | collective-permute-start | bytes 983048 | tf_op jit(solution)/shard_map/ppermute | solution.py:27
  82.4 3.9 %collective-permute-done.19.refs_3_.refs_1_ = f32[128,640]{1,0:T(8,128)S(1)} collective-permute-done((f32[128,640]{1,0:T(8,128)S(1)}, f32[128,640]{1,0:T(8,128)S(1)}, u32[]{:S(2)}, u32[]{:S(2)}) %collective-permute-start.19) | collective-permute-done | bytes 327712 | tf_op jit(solution)/shard_map/ppermute | solution.py:27
  86.3 1.7 %collective-permute-start.21 = (f32[128,640]{1,0:T(8,128)S(1)}, f32[128,640]{1,0:T(8,128)S(1)}, u32[]{:S(2)}, u32[]{:S(2)}) collective-permute-start(f32[128,640]{1,0:T(8,128)S(1)} %collective-permute-done.19.refs_3_.refs_1_), channel_id=1, source_target_pairs={{0,12},{4,8},{8,4},{12,0},{16,20},{20,16},{24,28},{28,24},{1,13},{... | collective-permute-start | bytes 983048 | tf_op jit(solution)/shard_map/ppermute | solution.py:27
  87.9 2.0 %collective-permute-done.18.refs_2_ = f32[256,640]{1,0:T(8,128)S(1)} collective-permute-done((f32[256,640]{1,0:T(8,128)S(1)}, f32[256,640]{1,0:T(8,128)S(1)}, u32[]{:S(2)}, u32[]{:S(2)}) %collective-permute-start.18) | collective-permute-done | bytes 655392 | tf_op jit(solution)/shard_map/ppermute | solution.py:27
  90.0 6.7 %solve_leaf.1 = (f32[96,512]{1,0:T(8,128)}, f32[8,128]{1,0:T(8,128)S(1)}) custom-call(f32[256,640]{1,0:T(8,128)S(1)} %get-tuple-element.82.refs_0_, f32[256,128]{1,0:T(8,128)S(1)} %get-tuple-element.83.refs_1_, f32[256,640]{1,0:T(8,128)S(1)} %collective-permute-done.18.refs_2_, f32[128,640]{1,0:T(8,128)S(1)} %collective-permute-done.19.refs_3_.refs_1_), custom_call_target="tpu_custom_call" | custom-call | flops 5737807872 | bytes 1245184 | tf_op jit(solution)/shard_map/solve_leaf/pallas_call | solution.py:152
  96.7 0.3 collective-permute-done.21.refs_3_
  97.0 5.6 %solve_upper.1 = (f32[32,512]{1,0:T(8,128)S(1)}, f32[8,128]{1,0:T(8,128)}) custom-call(f32[128,640]{1,0:T(8,128)S(1)} %upper_3.1.refs_0_, f32[128,640]{1,0:T(8,128)S(1)} %collective-permute-done.19.refs_3_.refs_1_, f32[128,640]{1,0:T(8,128)S(1)} %collective-permute-done.20.refs_2_, f32[128,640]{1,0:T(8,128)S(1)} %collective-permute-done.21.refs_3_, ...), custom_call_target="tpu_custom_call" | custom-call | flops 5133828096 | bytes 1114112 | tf_op jit(solution)/shard_map/solve_upper/pallas_call | solution.py:152
  102.5 5.0 %collective-permute-start.22 = (f32[32,512]{1,0:T(8,128)S(1)}, f32[32,512]{1,0:T(8,128)S(1)}, u32[]{:S(2)}, u32[]{:S(2)}) collective-permute-start(f32[32,512]{1,0:T(8,128)S(1)} %get-tuple-element.86), channel_id=1, source_target_pairs={{0,16},{16,0},{1,17},{17,1},{2,18},{18,2},{3,19},{19,3},{4,20},{20... | collective-permute-start | bytes 196616 | tf_op jit(solution)/shard_map/ppermute | solution.py:32
  107.6 0.9 collective-permute-done.22
  108.5 2.4 %collective-permute-start.23 = (f32[32,512]{1,0:T(8,128)S(1)}, f32[32,512]{1,0:T(8,128)S(1)}, u32[]{:S(2)}, u32[]{:S(2)}) collective-permute-start(f32[32,512]{1,0:T(8,128)S(1)} %get-tuple-element.92), channel_id=1, source_target_pairs={{0,32},{32,0},{64,96},{96,64},{128,160},{160,128},{192,224},{224,1... | collective-permute-start | bytes 196616 | tf_op jit(solution)/shard_map/ppermute | solution.py:32
  110.9 2.2 %collective-permute-done.23 = f32[32,512]{1,0:T(8,128)S(1)} collective-permute-done((f32[32,512]{1,0:T(8,128)S(1)}, f32[32,512]{1,0:T(8,128)S(1)}, u32[]{:S(2)}, u32[]{:S(2)}) %collective-permute-start.23) | collective-permute-done | bytes 65568 | tf_op jit(solution)/shard_map/ppermute | solution.py:32
  113.1 0.7 maximum_bitcast_fusion
  (45 shorter events, 1.1 us)
Async XLA Ops:
  0.6 16.1 %copy-start.1 = (bf16[1536,512]{1,0:T(8,128)(2,1)S(1)}, bf16[1536,512]{1,0:T(8,128)(2,1)}, u32[]{:S(2)}) copy-start(bf16[1536,512]{1,0:T(8,128)(2,1)} %omega_ref.3) | copy-start | bytes 4718596
  0.6 15.3 %copy-start.2 = (s32[1,2048]{1,0:T(1,128)S(1)}, s32[1,2048]{1,0:T(1,128)}, u32[]{:S(2)}) copy-start(s32[1,2048]{1,0:T(1,128)} %param.9) | copy-start | bytes 24580
  0.7 15.4 %copy-start.3 = (s32[4,16]{1,0:T(4,128)S(1)}, s32[4,16]{1,0:T(4,128)}, u32[]{:S(2)}) copy-start(s32[4,16]{1,0:T(4,128)} %param.11) | copy-start | bytes 772
  6.8 16.2 %collective-permute-start.2 = (f32[64,2048]{1,0:T(8,128)}, f32[64,2048]{1,0:T(8,128)S(1)}, u32[]{:S(2)}, u32[]{:S(2)}) collective-permute-start(f32[64,2048]{1,0:T(8,128)} %get-tuple-element.51), channel_id=1, source_target_pairs={{0,1},{1,0},{2,3},{3,2},{16,19},{17,18},{18,17},{19,16},{4,5},{5,4... | collective-permute-start | bytes 1572872 | tf_op jit(solution)/shard_map/ppermute | solution.py:27
  10.1 12.9 %collective-permute-start.3 = (f32[64,2048]{1,0:T(8,128)}, f32[64,2048]{1,0:T(8,128)}, u32[]{:S(2)}, u32[]{:S(2)}) collective-permute-start(f32[64,2048]{1,0:T(8,128)} %get-tuple-element.53), channel_id=1, source_target_pairs={{0,4},{4,0},{8,12},{12,8},{16,28},{20,24},{24,20},{28,16},{1,5},{5... | collective-permute-start | bytes 1572872 | tf_op jit(solution)/shard_map/ppermute | solution.py:27
  12.8 12.8 %collective-permute-start = (f32[64,2048]{1,0:T(8,128)}, f32[64,2048]{1,0:T(8,128)S(1)}, u32[]{:S(2)}, u32[]{:S(2)}) collective-permute-start(f32[64,2048]{1,0:T(8,128)} %get-tuple-element.46), channel_id=1, source_target_pairs={{0,1},{1,0},{2,3},{3,2},{16,19},{17,18},{18,17},{19,16},{4,5},{5,4... | collective-permute-start | bytes 1572872 | tf_op jit(solution)/shard_map/ppermute | solution.py:27
  13.0 12.6 %collective-permute-start.1 = (f32[64,2048]{1,0:T(8,128)}, f32[64,2048]{1,0:T(8,128)S(1)}, u32[]{:S(2)}, u32[]{:S(2)}) collective-permute-start(f32[64,2048]{1,0:T(8,128)} %get-tuple-element.48), channel_id=1, source_target_pairs={{0,4},{4,0},{8,12},{12,8},{16,28},{20,24},{24,20},{28,16},{1,5},{5... | collective-permute-start | bytes 1572872 | tf_op jit(solution)/shard_map/ppermute | solution.py:27
  16.7 2.8 %copy-start = (bf16[2048,1536]{1,0:T(8,128)(2,1)S(1)}, bf16[2048,1536]{1,0:T(8,128)(2,1)}, u32[]{:S(2)}) copy-start(bf16[2048,1536]{1,0:T(8,128)(2,1)} %a_ref.3) | copy-start | bytes 18874372
  24.1 8.4 %collective-permute-start.4 = (f32[64,2048]{1,0:T(8,128)S(1)}, f32[64,2048]{1,0:T(8,128)S(1)}, u32[]{:S(2)}, u32[]{:S(2)}) collective-permute-start(f32[64,2048]{1,0:T(8,128)S(1)} %get-tuple-element.54), channel_id=1, source_target_pairs={{0,3},{1,2},{2,1},{3,0},{16,17},{17,16},{18,19},{19,18},{4,7},{5,6... | collective-permute-start | bytes 1572872 | tf_op jit(solution)/shard_map/ppermute | solution.py:27
  24.2 8.4 %collective-permute-start.5 = (f32[64,2048]{1,0:T(8,128)S(1)}, f32[64,2048]{1,0:T(8,128)S(1)}, u32[]{:S(2)}, u32[]{:S(2)}) collective-permute-start(f32[64,2048]{1,0:T(8,128)S(1)} %get-tuple-element.56), channel_id=1, source_target_pairs={{0,12},{4,8},{8,4},{12,0},{16,20},{20,16},{24,28},{28,24},{1,13},{... | collective-permute-start | bytes 1572872 | tf_op jit(solution)/shard_map/ppermute | solution.py:27
  33.4 6.6 %collective-permute-start.6 = (f32[32,2048]{1,0:T(8,128)}, f32[32,2048]{1,0:T(8,128)S(1)}, u32[]{:S(2)}, u32[]{:S(2)}) collective-permute-start(f32[32,2048]{1,0:T(8,128)} %get-tuple-element.58), channel_id=1, source_target_pairs={{0,4},{4,0},{8,12},{12,8},{16,28},{20,24},{24,20},{28,16},{1,5},{5... | collective-permute-start | bytes 786440 | tf_op jit(solution)/shard_map/ppermute | solution.py:27
  36.1 6.4 %collective-permute-start.7 = (f32[32,2048]{1,0:T(8,128)S(1)}, f32[32,2048]{1,0:T(8,128)S(1)}, u32[]{:S(2)}, u32[]{:S(2)}) collective-permute-start(f32[32,2048]{1,0:T(8,128)S(1)} %get-tuple-element.60), channel_id=1, source_target_pairs={{0,1},{1,0},{2,3},{3,2},{16,19},{17,18},{18,17},{19,16},{4,5},{5,4... | collective-permute-start | bytes 786440 | tf_op jit(solution)/shard_map/ppermute | solution.py:27
  42.5 3.9 %collective-permute-start.8 = (f32[16,2048]{1,0:T(8,128)S(1)}, f32[16,2048]{1,0:T(8,128)S(1)}, u32[]{:S(2)}, u32[]{:S(2)}) collective-permute-start(f32[16,2048]{1,0:T(8,128)S(1)} %get-tuple-element.62), channel_id=1, source_target_pairs={{0,12},{4,8},{8,4},{12,0},{16,20},{20,16},{24,28},{28,24},{1,13},{... | collective-permute-start | bytes 393224 | tf_op jit(solution)/shard_map/ppermute | solution.py:27
  42.6 3.9 %collective-permute-start.9 = (f32[16,2048]{1,0:T(8,128)S(1)}, f32[16,2048]{1,0:T(8,128)S(1)}, u32[]{:S(2)}, u32[]{:S(2)}) collective-permute-start(f32[16,2048]{1,0:T(8,128)S(1)} %get-tuple-element.64), channel_id=1, source_target_pairs={{0,3},{1,2},{2,1},{3,0},{16,17},{17,16},{18,19},{19,18},{4,7},{5,6... | collective-permute-start | bytes 393224 | tf_op jit(solution)/shard_map/ppermute | solution.py:27
  47.0 8.4 %collective-permute-start.10 = (f32[32,512]{1,0:T(8,128)S(1)}, f32[32,512]{1,0:T(8,128)S(1)}, u32[]{:S(2)}, u32[]{:S(2)}) collective-permute-start(f32[32,512]{1,0:T(8,128)S(1)} %get-tuple-element.65.own.skeleton_ref), channel_id=1, source_target_pairs={{0,16},{16,0},{1,17},{17,1},{2,18},{18,2},{3,19},{19,3},{4,20},{20... | collective-permute-start | bytes 196616 | tf_op jit(solution)/shard_map/ppermute | solution.py:32
  55.9 3.9 %collective-permute-start.11 = (f32[32,512]{1,0:T(8,128)S(1)}, f32[32,512]{1,0:T(8,128)S(1)}, u32[]{:S(2)}, u32[]{:S(2)}) collective-permute-start(f32[32,512]{1,0:T(8,128)S(1)} %get-tuple-element.66.own.skeleton_1), channel_id=1, source_target_pairs={{0,32},{32,0},{64,96},{96,64},{128,160},{160,128},{192,224},{224,1... | collective-permute-start | bytes 196616 | tf_op jit(solution)/shard_map/ppermute | solution.py:32
  60.3 5.7 %collective-permute-start.13 = (f32[32,1536]{1,0:T(8,128)S(1)}, f32[32,1536]{1,0:T(8,128)S(1)}, u32[]{:S(2)}, u32[]{:S(2)}) collective-permute-start(f32[32,1536]{1,0:T(8,128)S(1)} %get-tuple-element.70.leaf), channel_id=1, source_target_pairs={{0,1},{1,0},{2,3},{3,2},{16,19},{17,18},{18,17},{19,16},{4,5},{5,4... | collective-permute-start | bytes 589832 | tf_op jit(solution)/shard_map/ppermute | solution.py:27
  60.3 0.7 collective-permute-start.12
  66.5 5.6 %collective-permute-start.14 = (f32[64,1024]{1,0:T(8,128)S(1)}, f32[64,1024]{1,0:T(8,128)S(1)}, u32[]{:S(2)}, u32[]{:S(2)}) collective-permute-start(f32[64,1024]{1,0:T(8,128)S(1)} %get-tuple-element.74.own), channel_id=1, source_target_pairs={{0,3},{1,2},{2,1},{3,0},{16,17},{17,16},{18,19},{19,18},{4,7},{5,6... | collective-permute-start | bytes 786440 | tf_op jit(solution)/shard_map/ppermute | solution.py:27
  66.6 4.8 %collective-permute-start.15 = (f32[32,768]{1,0:T(8,128)S(1)}, f32[32,768]{1,0:T(8,128)S(1)}, u32[]{:S(2)}, u32[]{:S(2)}) collective-permute-start(f32[32,768]{1,0:T(8,128)S(1)} %get-tuple-element.76.own), channel_id=1, source_target_pairs={{0,4},{4,0},{8,12},{12,8},{16,28},{20,24},{24,20},{28,16},{1,5},{5... | collective-permute-start | bytes 294920 | tf_op jit(solution)/shard_map/ppermute | solution.py:27
  72.2 7.9 %collective-permute-start.16 = (f32[128,768]{1,0:T(8,128)S(1)}, f32[128,768]{1,0:T(8,128)S(1)}, u32[]{:S(2)}, u32[]{:S(2)}) collective-permute-start(f32[128,768]{1,0:T(8,128)S(1)} %get-tuple-element.79.own), channel_id=1, source_target_pairs={{0,4},{4,0},{8,12},{12,8},{16,28},{20,24},{24,20},{28,16},{1,5},{5... | collective-permute-start | bytes 1179656 | tf_op jit(solution)/shard_map/ppermute | solution.py:27
  72.3 5.5 %collective-permute-start.17 = (f32[64,640]{1,0:T(8,128)S(1)}, f32[64,640]{1,0:T(8,128)S(1)}, u32[]{:S(2)}, u32[]{:S(2)}) collective-permute-start(f32[64,640]{1,0:T(8,128)S(1)} %get-tuple-element.78.refs_0_.own), channel_id=1, source_target_pairs={{0,1},{1,0},{2,3},{3,2},{16,19},{17,18},{18,17},{19,16},{4,5},{5,4... | collective-permute-start | bytes 491528 | tf_op jit(solution)/shard_map/ppermute | solution.py:27
  80.1 9.8 %collective-permute-start.18 = (f32[256,640]{1,0:T(8,128)S(1)}, f32[256,640]{1,0:T(8,128)S(1)}, u32[]{:S(2)}, u32[]{:S(2)}) collective-permute-start(f32[256,640]{1,0:T(8,128)S(1)} %get-tuple-element.82.refs_0_), channel_id=1, source_target_pairs={{0,12},{4,8},{8,4},{12,0},{16,20},{20,16},{24,28},{28,24},{1,13},{... | collective-permute-start | bytes 1966088 | tf_op jit(solution)/shard_map/ppermute | solution.py:27
  80.3 5.9 %collective-permute-start.19 = (f32[128,640]{1,0:T(8,128)S(1)}, f32[128,640]{1,0:T(8,128)S(1)}, u32[]{:S(2)}, u32[]{:S(2)}) collective-permute-start(f32[128,640]{1,0:T(8,128)S(1)} %upper_3.1.refs_0_), channel_id=1, source_target_pairs={{0,3},{1,2},{2,1},{3,0},{16,17},{17,16},{18,19},{19,18},{4,7},{5,6... | collective-permute-start | bytes 983048 | tf_op jit(solution)/shard_map/ppermute | solution.py:27
  81.0 15.7 %collective-permute-start.20 = (f32[128,640]{1,0:T(8,128)S(1)}, f32[128,640]{1,0:T(8,128)S(1)}, u32[]{:S(2)}, u32[]{:S(2)}) collective-permute-start(f32[128,640]{1,0:T(8,128)S(1)} %upper_3.1.refs_0_), channel_id=1, source_target_pairs={{0,12},{4,8},{8,4},{12,0},{16,20},{20,16},{24,28},{28,24},{1,13},{... | collective-permute-start | bytes 983048 | tf_op jit(solution)/shard_map/ppermute | solution.py:27
  86.3 10.7 %collective-permute-start.21 = (f32[128,640]{1,0:T(8,128)S(1)}, f32[128,640]{1,0:T(8,128)S(1)}, u32[]{:S(2)}, u32[]{:S(2)}) collective-permute-start(f32[128,640]{1,0:T(8,128)S(1)} %collective-permute-done.19.refs_3_.refs_1_), channel_id=1, source_target_pairs={{0,12},{4,8},{8,4},{12,0},{16,20},{20,16},{24,28},{28,24},{1,13},{... | collective-permute-start | bytes 983048 | tf_op jit(solution)/shard_map/ppermute | solution.py:27
  102.5 5.9 %collective-permute-start.22 = (f32[32,512]{1,0:T(8,128)S(1)}, f32[32,512]{1,0:T(8,128)S(1)}, u32[]{:S(2)}, u32[]{:S(2)}) collective-permute-start(f32[32,512]{1,0:T(8,128)S(1)} %get-tuple-element.86), channel_id=1, source_target_pairs={{0,16},{16,0},{1,17},{17,1},{2,18},{18,2},{3,19},{19,3},{4,20},{20... | collective-permute-start | bytes 196616 | tf_op jit(solution)/shard_map/ppermute | solution.py:32
  108.5 4.6 %collective-permute-start.23 = (f32[32,512]{1,0:T(8,128)S(1)}, f32[32,512]{1,0:T(8,128)S(1)}, u32[]{:S(2)}, u32[]{:S(2)}) collective-permute-start(f32[32,512]{1,0:T(8,128)S(1)} %get-tuple-element.92), channel_id=1, source_target_pairs={{0,32},{32,0},{64,96},{96,64},{128,160},{160,128},{192,224},{224,1... | collective-permute-start | bytes 196616 | tf_op jit(solution)/shard_map/ppermute | solution.py:32

commit v3 on v2

--- a/solution.py
+++ b/solution.py
@@ -113,9 +113,11 @@
             0,
         )
     else:
-        own_ref, rest_ref, got_ref = refs[:3]
-        skeleton = jnp.concatenate([own_ref[:, :K], got_ref[:, :K]], 0)
-        redundant = jnp.concatenate([rest_ref[:, :96], got_ref[:, K : K + 96]], 0)
+        rest_ref, *pieces = refs[:5]
+        skeleton = jnp.concatenate([piece[:, :K] for piece in pieces], 0)
+        redundant = jnp.concatenate(
+            [rest_ref[:, :96]] + [piece[:, K : K + 96] for piece in pieces[1:]], 0
+        )
     count = redundant.shape[1]
     identity = jnp.where(
         lax.broadcasted_iota(jnp.int32, (K, K), 0) == lax.broadcasted_iota(jnp.int32, (K, K), 1),
@@ -269,6 +271,26 @@
     pack(own, rest, got, *refs[-2:])
 
 
+def fork_kernel(own, rest, got, *refs):
+    payload_ref, ahead_ref, rest_ref = refs[-3:]
+    rows = own.shape[0]
+    payload_ref[:rows, :K] = own[:, :K]
+    payload_ref[rows:, :K] = got[:, :K]
+    payload_ref[:rows, K:] = rest[:, 256:]
+    payload_ref[rows:, K:] = got[:, K + 256 :]
+    ahead_ref[:rows, :K] = own[:, :K]
+    ahead_ref[rows:, :K] = got[:, :K]
+    ahead_ref[:rows, K:] = rest[:, 128:256]
+    ahead_ref[rows:, K:] = got[:, K + 128 : K + 256]
+    rest_ref[:rows] = rest[:, :128]
+    rest_ref[rows:] = got[:, K : K + 128]
+
+
+def onward_kernel(got, *refs):
+    refs[-1][:, :K] = got[:, :K]
+    refs[-1][:, K:] = got[:, K + 128 :]
+
+
 def pack_all_kernel(own, rest, got, payload_ref):
     rows = own.shape[0]
     payload_ref[:rows, :K] = own[:, :K]
@@ -372,21 +394,23 @@
         pack_kernel, "upper_2", (upper, upper_rest, upper_got), ((64, K + 128), (64, 128))
     )
     upper_got = hop(upper, "x", True)
-    leaf, rest = call(
-        pack_kernel, "leaf_3", (leaf, rest, got), ((128, K + 256), (128, 256)), (upper,)
-    )
-    got = hop(leaf, "y", True)
+    leaf, ahead, rest = call(
+        fork_kernel,
+        "leaf_3",
+        (leaf, rest, got),
+        ((128, K + 256), (128, K + 128), (128, 128)),
+        (upper_got,),
+    )
     (upper,) = call(pack_all_kernel, "upper_3", (upper, upper_rest, upper_got), ((128, K + 128),))
     upper_got, across = hop(upper, "x", False), hop(upper, "y", False)
-    leaf, rest = call(
-        pack_kernel, "leaf_4", (leaf, rest, got), ((256, K + 128), (256, 128)), (upper,)
-    )
-    got = hop(leaf, "y", False)
+    got, leaf_across = hop(leaf, "y", True), hop(ahead, "y", False)
     beyond = hop(upper_got, "y", False)
-    leaf_interp, done = solve((leaf, rest, got), 96, False, (upper_got,))
-    upper_interp, _ = solve((upper, upper_got, across, beyond), 32, True, (done,))
-
+    (onward,) = call(onward_kernel, "leaf_4", (got,), ((128, K + 128),), (upper_got,))
+    leaf_beyond = hop(onward, "y", False)
+    upper_interp, _ = solve((upper, upper_got, across, beyond), 32, True)
     other = swapped(upper_interp, "core", 1)
+    leaf_interp, _ = solve((rest, leaf, got, leaf_across, leaf_beyond), 96, False, (other,))
+
     level_1 = jnp.where(core == 0, upper_interp, other)
     chip = jnp.where(core == 0, other, upper_interp)
     beside = swapped(chip, "z", 1)

time: 115 us -> 112 us (0.974)
  starting transfers between devices: 34.5 us -> 30.2 us
  waiting for transfers between devices: 41.1 us -> 43.5 us
    ppermute x19 -> x20, waiting for transfers between devices: 36.5 us -> 41.1 us  [hop(): return lax.ppermute(block, ('core', axis), route)]
    ppermute x4, starting transfers between devices: 16.9 us -> 14.1 us  [swapped(): return lax.ppermute(block, axis, [(i, i ^ mask) for i in range(count)])]
    ppermute x4, waiting for transfers between devices: 4.55 us -> 2.37 us  [swapped(): return lax.ppermute(block, axis, [(i, i ^ mask) for i in range(count)])]
    ppermute x19 -> x20, starting transfers between devices: 17 us -> 15.4 us  [hop(): return lax.ppermute(block, ('core', axis), route)]
  transfers between devices with their start and end apart: 24 -> 25, of which waited for: 18 -> 16; matrix products, arithmetic and copies ran while one was open for 6% -> 6% of each run, Pallas kernels for 11% -> 16%
where the time goes in v3:
time: 112 us
  waiting for transfers between devices  43.5 us (39%)
  starting transfers between devices  30.2 us (27%)
  Pallas kernels  26.7 us (24%)
  local copies, waits for them, and re-layouts  6.31 us (6%)
  other arithmetic  4.22 us (4%)
    ppermute x20, waiting for transfers between devices, hop(): return lax.ppermute(block, ('core', axis), route)  41.1 us
    ppermute x20, starting transfers between devices, hop(): return lax.ppermute(block, ('core', axis), route)  15.4 us
    ppermute x4, starting transfers between devices, swapped(): return lax.ppermute(block, axis, [(i, i ^ mask) for i in range(count)])  14.1 us
    pallas_call x2, Pallas kernels, solve(): pl.pallas_call(functools.partial(solve_kernel, packed=packed), out_shape=...  12.3 us
    pallas_call x2, Pallas kernels, ordered_samples(): pl.pallas_call(functools.partial(ordered_kernel, sent=sent), grid=(LEAF /...  8.9 us
    pallas_call x8, Pallas kernels, call(): pl.pallas_call(kernel, in_specs=[VMEM] * len(inputs) + [ANY] * len(after)...  2.96 us
    unnamed x8, local copies, waits for them, and re-layouts  2.79 us
    ppermute x4, waiting for transfers between devices, swapped(): return lax.ppermute(block, axis, [(i, i ^ mask) for i in range(count)])  2.37 us
  transfers between devices with their start and end apart: 25, of which 16 were waited for; matrix products, arithmetic and copies ran while one was open for 6% of the time, Pallas kernels for 16%

profile of v3, /device:TPU:1, one launch (start us, length us, event | category | flops | bytes accessed | tf_op | source)
XLA Modules:
  0.0 111.8 jit_solution(14805155513441962455)
XLA Ops:
  0.7 6.1 %sent_samples.1 = (f32[64,2048]{1,0:T(8,128)}, f32[64,2048]{1,0:T(8,128)}, f32[64,2048]{1,0:T(8,128)}, f32[64,2048]{1,0:T(8,128)}) custom-call(bf16[1536,512]{1,0:T(8,128)(2,1)} %omega_ref.3, bf16[2048,1536]{1,0:T(8,128)(2,1)} %a_ref.3), custom_call_target="tpu_custom_call" | custom-call | flops 2013265920 | bytes 9961472 | tf_op jit(solution)/shard_map/sent_samples/pallas_call | solution.py:73
  6.8 3.3 %collective-permute-start.2 = (f32[64,2048]{1,0:T(8,128)}, f32[64,2048]{1,0:T(8,128)S(1)}, u32[]{:S(2)}, u32[]{:S(2)}) collective-permute-start(f32[64,2048]{1,0:T(8,128)} %get-tuple-element.49), channel_id=1, source_target_pairs={{0,1},{1,0},{2,3},{3,2},{16,19},{17,18},{18,17},{19,16},{4,5},{5,4... | collective-permute-start | bytes 1572872 | tf_op jit(solution)/shard_map/ppermute | solution.py:27
  10.1 2.7 %collective-permute-start.3 = (f32[64,2048]{1,0:T(8,128)}, f32[64,2048]{1,0:T(8,128)}, u32[]{:S(2)}, u32[]{:S(2)}) collective-permute-start(f32[64,2048]{1,0:T(8,128)} %get-tuple-element.51), channel_id=1, source_target_pairs={{0,4},{4,0},{8,12},{12,8},{16,28},{20,24},{24,20},{28,16},{1,5},{5... | collective-permute-start | bytes 1572872 | tf_op jit(solution)/shard_map/ppermute | solution.py:27
  12.8 0.2 collective-permute-start
  13.0 0.8 dynamic-slice_xor_fusion
  13.9 0.1 slice.52
  14.0 0.1 slice.48
  14.1 0.6 gather_fusion.2
  14.6 0.6 gather_fusion.1
  15.3 0.6 gather_fusion.3
  15.9 0.1 reshape.144
  16.0 0.7 constant_dynamic-slice_fusion
  16.7 2.8 %copy-done = bf16[2048,1536]{1,0:T(8,128)(2,1)S(1)} copy-done((bf16[2048,1536]{1,0:T(8,128)(2,1)S(1)}, bf16[2048,1536]{1,0:T(8,128)(2,1)}, u32[]{:S(2)}) %copy-start) | copy-done | bytes 6291480
  19.5 2.8 %kept_samples.1 = (f32[64,2048]{1,0:T(8,128)S(1)}, f32[64,2048]{1,0:T(8,128)S(1)}, f32[64,2048]{1,0:T(8,128)S(1)}, f32[64,2048]{1,0:T(8,128)S(1)}) custom-call(bf16[1536,512]{1,0:T(8,128)(2,1)S(1)} %copy-done.1, bf16[2048,1536]{1,0:T(8,128)(2,1)S(1)} %copy-done), custom_call_target="tpu_custom_call" | custom-call | flops 2013265920 | bytes 9961472 | tf_op jit(solution)/shard_map/kept_samples/pallas_call | solution.py:73
  22.3 0.7 compare_select_fusion.order_ref
  23.0 1.2 %add_sent.3 = (f32[64,2048]{1,0:T(8,128)S(1)}, f32[64,2048]{1,0:T(8,128)S(1)}) custom-call(f32[64,2048]{1,0:T(8,128)S(1)} %get-tuple-element.48.kept_a, f32[64,2048]{1,0:T(8,128)S(1)} %collective-permute-done.2.got_a, f32[64,2048]{1,0:T(8,128)S(1)} %get-tuple-element.50.kept_b, f32[64,2048]{1,0:T(8,128)} %collective-permute-done.3.got_b), custom_call_target="tpu_custom_call" | custom-call | flops 262144 | bytes 3145728 | tf_op jit(solution)/shard_map/add_sent/pallas_call | solution.py:176
  24.1 0.1 collective-permute-start.4
  24.2 0.1 collective-permute-start.5
  24.3 0.6 fusion.2
  25.0 0.7 fusion.1
  25.7 0.1 add_kept.3
  25.8 6.8 %collective-permute-done.4.got_a = f32[64,2048]{1,0:T(8,128)S(1)} collective-permute-done((f32[64,2048]{1,0:T(8,128)S(1)}, f32[64,2048]{1,0:T(8,128)S(1)}, u32[]{:S(2)}, u32[]{:S(2)}) %collective-permute-start.4) | collective-permute-done | bytes 524320 | tf_op jit(solution)/shard_map/ppermute | solution.py:27
  32.5 0.1 collective-permute-done.5.got_b
  32.6 0.7 add_sent.4
  33.4 2.7 %collective-permute-start.6 = (f32[32,2048]{1,0:T(8,128)}, f32[32,2048]{1,0:T(8,128)S(1)}, u32[]{:S(2)}, u32[]{:S(2)}) collective-permute-start(f32[32,2048]{1,0:T(8,128)} %get-tuple-element.56), channel_id=1, source_target_pairs={{0,4},{4,0},{8,12},{12,8},{16,28},{20,24},{24,20},{28,16},{1,5},{5... | collective-permute-start | bytes 786440 | tf_op jit(solution)/shard_map/ppermute | solution.py:27
  36.1 2.5 %collective-permute-start.7 = (f32[32,2048]{1,0:T(8,128)S(1)}, f32[32,2048]{1,0:T(8,128)S(1)}, u32[]{:S(2)}, u32[]{:S(2)}) collective-permute-start(f32[32,2048]{1,0:T(8,128)S(1)} %get-tuple-element.58), channel_id=1, source_target_pairs={{0,1},{1,0},{2,3},{3,2},{16,19},{17,18},{18,17},{19,16},{4,5},{5,4... | collective-permute-start | bytes 786440 | tf_op jit(solution)/shard_map/ppermute | solution.py:27
  38.6 0.1 reshape.143
  38.6 0.6 fusion
  39.3 0.8 collective-permute-done.6.got_a
  40.0 2.5 %collective-permute-done.7.got_b = f32[32,2048]{1,0:T(8,128)S(1)} collective-permute-done((f32[32,2048]{1,0:T(8,128)S(1)}, f32[32,2048]{1,0:T(8,128)S(1)}, u32[]{:S(2)}, u32[]{:S(2)}) %collective-permute-start.7) | collective-permute-done | bytes 262176 | tf_op jit(solution)/shard_map/ppermute | solution.py:27
  42.5 0.1 collective-permute-start.8
  42.6 0.9 collective-permute-start.9
  43.7 0.6 gather_fusion
  44.4 2.1 %collective-permute-done.8.refs_1_ = f32[16,2048]{1,0:T(8,128)S(1)} collective-permute-done((f32[16,2048]{1,0:T(8,128)S(1)}, f32[16,2048]{1,0:T(8,128)S(1)}, u32[]{:S(2)}, u32[]{:S(2)}) %collective-permute-start.8) | collective-permute-done | bytes 131104 | tf_op jit(solution)/shard_map/ppermute | solution.py:27
  46.4 0.1 collective-permute-done.9.refs_3_
  46.5 0.5 finish_samples.1
  47.0 7.5 %collective-permute-start.10 = (f32[32,512]{1,0:T(8,128)S(1)}, f32[32,512]{1,0:T(8,128)S(1)}, u32[]{:S(2)}, u32[]{:S(2)}) collective-permute-start(f32[32,512]{1,0:T(8,128)S(1)} %get-tuple-element.63.own.skeleton_ref), channel_id=1, source_target_pairs={{0,16},{16,0},{1,17},{17,1},{2,18},{18,2},{3,19},{19,3},{4,20},{20... | collective-permute-start | bytes 196616 | tf_op jit(solution)/shard_map/ppermute | solution.py:32
  54.6 0.8 collective-permute-done.10.sibling
  55.5 0.5 level_1.1
  55.9 1.8 %collective-permute-start.11 = (f32[32,512]{1,0:T(8,128)S(1)}, f32[32,512]{1,0:T(8,128)S(1)}, u32[]{:S(2)}, u32[]{:S(2)}) collective-permute-start(f32[32,512]{1,0:T(8,128)S(1)} %get-tuple-element.64.own.skeleton_1), channel_id=1, source_target_pairs={{0,32},{32,0},{64,96},{96,64},{128,160},{160,128},{192,224},{224,1... | collective-permute-start | bytes 196616 | tf_op jit(solution)/shard_map/ppermute | solution.py:32
  57.8 1.5 %leaf_redundant.1 = (f32[32,1536]{1,0:T(8,128)S(1)}, f32[32,1024]{1,0:T(8,128)S(1)}) custom-call(s32[1,2048]{1,0:T(1,128)S(1)} %bitcast.30, bf16[96,2048]{1,0:T(8,128)(2,1)S(1)} %get-tuple-element.65.parts_ref, f32[32,512]{1,0:T(8,128)S(1)} %get-tuple-element.63.own.skeleton_ref), custom_call_target="tpu_custom_call" | custom-call | flops 805306368 | bytes 1000000 | tf_op jit(solution)/shard_map/leaf_redundant/pallas_call | solution.py:237
  59.2 0.6 collective-permute-done.11.sibling
  59.9 0.5 level_2.1
  60.3 0.7 collective-permute-start.12
  61.0 5.0 %collective-permute-done.13.got = f32[32,1536]{1,0:T(8,128)S(1)} collective-permute-done((f32[32,1536]{1,0:T(8,128)S(1)}, f32[32,1536]{1,0:T(8,128)S(1)}, u32[]{:S(2)}, u32[]{:S(2)}) %collective-permute-start.13) | collective-permute-done | bytes 196640 | tf_op jit(solution)/shard_map/ppermute | solution.py:27
  66.1 0.5 level_3.1
  66.6 4.7 %collective-permute-done.15.got = f32[32,768]{1,0:T(8,128)S(1)} collective-permute-done((f32[32,768]{1,0:T(8,128)S(1)}, f32[32,768]{1,0:T(8,128)S(1)}, u32[]{:S(2)}, u32[]{:S(2)}) %collective-permute-start.15) | collective-permute-done | bytes 98336 | tf_op jit(solution)/shard_map/ppermute | solution.py:27
  71.3 0.1 collective-permute-start.16
  71.4 0.1 collective-permute-start.14
  71.5 5.9 %collective-permute-done.16.refs_0_.got = f32[64,640]{1,0:T(8,128)S(1)} collective-permute-done((f32[64,640]{1,0:T(8,128)S(1)}, f32[64,640]{1,0:T(8,128)S(1)}, u32[]{:S(2)}, u32[]{:S(2)}) %collective-permute-start.16) | collective-permute-done | bytes 163872 | tf_op jit(solution)/shard_map/ppermute | solution.py:27
  77.4 0.1 collective-permute-start.19
  77.5 1.1 collective-permute-done.14.got
  78.7 0.7 collective-permute-start.17
  79.3 4.4 %collective-permute-done.19.refs_0_.refs_1_ = f32[128,640]{1,0:T(8,128)S(1)} collective-permute-done((f32[128,640]{1,0:T(8,128)S(1)}, f32[128,640]{1,0:T(8,128)S(1)}, u32[]{:S(2)}, u32[]{:S(2)}) %collective-permute-start.19) | collective-permute-done | bytes 327712 | tf_op jit(solution)/shard_map/ppermute | solution.py:27
  83.7 1.5 %collective-permute-start.18 = (f32[128,640]{1,0:T(8,128)S(1)}, f32[128,640]{1,0:T(8,128)S(1)}, u32[]{:S(2)}, u32[]{:S(2)}) collective-permute-start(f32[128,640]{1,0:T(8,128)S(1)} %get-tuple-element.79), channel_id=1, source_target_pairs={{0,12},{4,8},{8,4},{12,0},{16,20},{20,16},{24,28},{28,24},{1,13},{... | collective-permute-start | bytes 983048 | tf_op jit(solution)/shard_map/ppermute | solution.py:27
  85.2 2.8 %collective-permute-done.17.got.refs_2_ = f32[128,768]{1,0:T(8,128)S(1)} collective-permute-done((f32[128,768]{1,0:T(8,128)S(1)}, f32[128,768]{1,0:T(8,128)S(1)}, u32[]{:S(2)}, u32[]{:S(2)}) %collective-permute-start.17) | collective-permute-done | bytes 393248 | tf_op jit(solution)/shard_map/ppermute | solution.py:27
  88.0 0.3 collective-permute-start.20
  88.3 4.9 %collective-permute-done.22.refs_3_ = f32[128,640]{1,0:T(8,128)S(1)} collective-permute-done((f32[128,640]{1,0:T(8,128)S(1)}, f32[128,640]{1,0:T(8,128)S(1)}, u32[]{:S(2)}, u32[]{:S(2)}) %collective-permute-start.22) | collective-permute-done | bytes 327712 | tf_op jit(solution)/shard_map/ppermute | solution.py:27
  93.3 5.5 %solve_upper.1 = (f32[32,512]{1,0:T(8,128)S(1)}, f32[8,128]{1,0:T(8,128)}) custom-call(f32[128,640]{1,0:T(8,128)S(1)} %upper_3.1.refs_0_, f32[128,640]{1,0:T(8,128)S(1)} %collective-permute-done.19.refs_0_.refs_1_, f32[128,640]{1,0:T(8,128)S(1)} %collective-permute-done.21.refs_2_, f32[128,640]{1,0:T(8,128)S(1)} %collective-permute-done.22.refs_3_), custom_call_target="tpu_custom_call" | custom-call | flops 5133828096 | bytes 1114112 | tf_op jit(solution)/shard_map/solve_upper/pallas_call | solution.py:154
  98.8 2.7 %collective-permute-start.23 = (f32[32,512]{1,0:T(8,128)S(1)}, f32[32,512]{1,0:T(8,128)S(1)}, u32[]{:S(2)}, u32[]{:S(2)}) collective-permute-start(f32[32,512]{1,0:T(8,128)S(1)} %get-tuple-element.81), channel_id=1, source_target_pairs={{0,16},{16,0},{1,17},{17,1},{2,18},{18,2},{3,19},{19,3},{4,20},{20... | collective-permute-start | bytes 196616 | tf_op jit(solution)/shard_map/ppermute | solution.py:32
  101.5 0.9 collective-permute-done.23.refs_5_
  102.4 2.0 %collective-permute-start.24 = (f32[32,512]{1,0:T(8,128)S(1)}, f32[32,512]{1,0:T(8,128)S(1)}, u32[]{:S(2)}, u32[]{:S(2)}) collective-permute-start(f32[32,512]{1,0:T(8,128)S(1)} %get-tuple-element.88), channel_id=1, source_target_pairs={{0,32},{32,0},{64,96},{96,64},{128,160},{160,128},{192,224},{224,1... | collective-permute-start | bytes 196616 | tf_op jit(solution)/shard_map/ppermute | solution.py:32
  104.4 6.7 %solve_leaf.1 = (f32[96,512]{1,0:T(8,128)}, f32[8,128]{1,0:T(8,128)}) custom-call(f32[128,128]{1,0:T(8,128)S(1)} %get-tuple-element.77.refs_0_, f32[128,768]{1,0:T(8,128)S(1)} %get-tuple-element.78.refs_1_, f32[128,768]{1,0:T(8,128)S(1)} %collective-permute-done.17.got.refs_2_, f32[128,640]{1,0:T(8,128)S(1)} %collective-permute-done.18.refs_3_, ...), custom_call_target="tpu_custom_call" | custom-call | flops 5737807872 | bytes 1245184 | tf_op jit(solution)/shard_map/solve_leaf/pallas_call | solution.py:154
  111.1 0.7 maximum_bitcast_fusion
  (47 shorter events, 0.9 us)
Async XLA Ops:
  0.6 16.1 %copy-start.1 = (bf16[1536,512]{1,0:T(8,128)(2,1)S(1)}, bf16[1536,512]{1,0:T(8,128)(2,1)}, u32[]{:S(2)}) copy-start(bf16[1536,512]{1,0:T(8,128)(2,1)} %omega_ref.3) | copy-start | bytes 4718596
  0.6 15.3 %copy-start.2 = (s32[1,2048]{1,0:T(1,128)S(1)}, s32[1,2048]{1,0:T(1,128)}, u32[]{:S(2)}) copy-start(s32[1,2048]{1,0:T(1,128)} %param.9) | copy-start | bytes 24580
  0.7 15.4 %copy-start.3 = (s32[4,16]{1,0:T(4,128)S(1)}, s32[4,16]{1,0:T(4,128)}, u32[]{:S(2)}) copy-start(s32[4,16]{1,0:T(4,128)} %param.11) | copy-start | bytes 772
  6.8 16.2 %collective-permute-start.2 = (f32[64,2048]{1,0:T(8,128)}, f32[64,2048]{1,0:T(8,128)S(1)}, u32[]{:S(2)}, u32[]{:S(2)}) collective-permute-start(f32[64,2048]{1,0:T(8,128)} %get-tuple-element.49), channel_id=1, source_target_pairs={{0,1},{1,0},{2,3},{3,2},{16,19},{17,18},{18,17},{19,16},{4,5},{5,4... | collective-permute-start | bytes 1572872 | tf_op jit(solution)/shard_map/ppermute | solution.py:27
  10.1 12.9 %collective-permute-start.3 = (f32[64,2048]{1,0:T(8,128)}, f32[64,2048]{1,0:T(8,128)}, u32[]{:S(2)}, u32[]{:S(2)}) collective-permute-start(f32[64,2048]{1,0:T(8,128)} %get-tuple-element.51), channel_id=1, source_target_pairs={{0,4},{4,0},{8,12},{12,8},{16,28},{20,24},{24,20},{28,16},{1,5},{5... | collective-permute-start | bytes 1572872 | tf_op jit(solution)/shard_map/ppermute | solution.py:27
  12.8 12.8 %collective-permute-start = (f32[64,2048]{1,0:T(8,128)}, f32[64,2048]{1,0:T(8,128)S(1)}, u32[]{:S(2)}, u32[]{:S(2)}) collective-permute-start(f32[64,2048]{1,0:T(8,128)} %get-tuple-element.44), channel_id=1, source_target_pairs={{0,1},{1,0},{2,3},{3,2},{16,19},{17,18},{18,17},{19,16},{4,5},{5,4... | collective-permute-start | bytes 1572872 | tf_op jit(solution)/shard_map/ppermute | solution.py:27
  13.0 12.6 %collective-permute-start.1 = (f32[64,2048]{1,0:T(8,128)}, f32[64,2048]{1,0:T(8,128)S(1)}, u32[]{:S(2)}, u32[]{:S(2)}) collective-permute-start(f32[64,2048]{1,0:T(8,128)} %get-tuple-element.46), channel_id=1, source_target_pairs={{0,4},{4,0},{8,12},{12,8},{16,28},{20,24},{24,20},{28,16},{1,5},{5... | collective-permute-start | bytes 1572872 | tf_op jit(solution)/shard_map/ppermute | solution.py:27
  16.7 2.8 %copy-start = (bf16[2048,1536]{1,0:T(8,128)(2,1)S(1)}, bf16[2048,1536]{1,0:T(8,128)(2,1)}, u32[]{:S(2)}) copy-start(bf16[2048,1536]{1,0:T(8,128)(2,1)} %a_ref.3) | copy-start | bytes 18874372
  24.1 8.4 %collective-permute-start.4 = (f32[64,2048]{1,0:T(8,128)S(1)}, f32[64,2048]{1,0:T(8,128)S(1)}, u32[]{:S(2)}, u32[]{:S(2)}) collective-permute-start(f32[64,2048]{1,0:T(8,128)S(1)} %get-tuple-element.52), channel_id=1, source_target_pairs={{0,3},{1,2},{2,1},{3,0},{16,17},{17,16},{18,19},{19,18},{4,7},{5,6... | collective-permute-start | bytes 1572872 | tf_op jit(solution)/shard_map/ppermute | solution.py:27
  24.2 8.4 %collective-permute-start.5 = (f32[64,2048]{1,0:T(8,128)S(1)}, f32[64,2048]{1,0:T(8,128)S(1)}, u32[]{:S(2)}, u32[]{:S(2)}) collective-permute-start(f32[64,2048]{1,0:T(8,128)S(1)} %get-tuple-element.54), channel_id=1, source_target_pairs={{0,12},{4,8},{8,4},{12,0},{16,20},{20,16},{24,28},{28,24},{1,13},{... | collective-permute-start | bytes 1572872 | tf_op jit(solution)/shard_map/ppermute | solution.py:27
  33.4 6.6 %collective-permute-start.6 = (f32[32,2048]{1,0:T(8,128)}, f32[32,2048]{1,0:T(8,128)S(1)}, u32[]{:S(2)}, u32[]{:S(2)}) collective-permute-start(f32[32,2048]{1,0:T(8,128)} %get-tuple-element.56), channel_id=1, source_target_pairs={{0,4},{4,0},{8,12},{12,8},{16,28},{20,24},{24,20},{28,16},{1,5},{5... | collective-permute-start | bytes 786440 | tf_op jit(solution)/shard_map/ppermute | solution.py:27
  36.1 6.4 %collective-permute-start.7 = (f32[32,2048]{1,0:T(8,128)S(1)}, f32[32,2048]{1,0:T(8,128)S(1)}, u32[]{:S(2)}, u32[]{:S(2)}) collective-permute-start(f32[32,2048]{1,0:T(8,128)S(1)} %get-tuple-element.58), channel_id=1, source_target_pairs={{0,1},{1,0},{2,3},{3,2},{16,19},{17,18},{18,17},{19,16},{4,5},{5,4... | collective-permute-start | bytes 786440 | tf_op jit(solution)/shard_map/ppermute | solution.py:27
  42.5 3.9 %collective-permute-start.8 = (f32[16,2048]{1,0:T(8,128)S(1)}, f32[16,2048]{1,0:T(8,128)S(1)}, u32[]{:S(2)}, u32[]{:S(2)}) collective-permute-start(f32[16,2048]{1,0:T(8,128)S(1)} %get-tuple-element.60), channel_id=1, source_target_pairs={{0,12},{4,8},{8,4},{12,0},{16,20},{20,16},{24,28},{28,24},{1,13},{... | collective-permute-start | bytes 393224 | tf_op jit(solution)/shard_map/ppermute | solution.py:27
  42.6 3.9 %collective-permute-start.9 = (f32[16,2048]{1,0:T(8,128)S(1)}, f32[16,2048]{1,0:T(8,128)S(1)}, u32[]{:S(2)}, u32[]{:S(2)}) collective-permute-start(f32[16,2048]{1,0:T(8,128)S(1)} %get-tuple-element.62), channel_id=1, source_target_pairs={{0,3},{1,2},{2,1},{3,0},{16,17},{17,16},{18,19},{19,18},{4,7},{5,6... | collective-permute-start | bytes 393224 | tf_op jit(solution)/shard_map/ppermute | solution.py:27
  47.0 8.4 %collective-permute-start.10 = (f32[32,512]{1,0:T(8,128)S(1)}, f32[32,512]{1,0:T(8,128)S(1)}, u32[]{:S(2)}, u32[]{:S(2)}) collective-permute-start(f32[32,512]{1,0:T(8,128)S(1)} %get-tuple-element.63.own.skeleton_ref), channel_id=1, source_target_pairs={{0,16},{16,0},{1,17},{17,1},{2,18},{18,2},{3,19},{19,3},{4,20},{20... | collective-permute-start | bytes 196616 | tf_op jit(solution)/shard_map/ppermute | solution.py:32
  55.9 3.9 %collective-permute-start.11 = (f32[32,512]{1,0:T(8,128)S(1)}, f32[32,512]{1,0:T(8,128)S(1)}, u32[]{:S(2)}, u32[]{:S(2)}) collective-permute-start(f32[32,512]{1,0:T(8,128)S(1)} %get-tuple-element.64.own.skeleton_1), channel_id=1, source_target_pairs={{0,32},{32,0},{64,96},{96,64},{128,160},{160,128},{192,224},{224,1... | collective-permute-start | bytes 196616 | tf_op jit(solution)/shard_map/ppermute | solution.py:32
  60.3 5.7 %collective-permute-start.13 = (f32[32,1536]{1,0:T(8,128)S(1)}, f32[32,1536]{1,0:T(8,128)S(1)}, u32[]{:S(2)}, u32[]{:S(2)}) collective-permute-start(f32[32,1536]{1,0:T(8,128)S(1)} %get-tuple-element.68.leaf), channel_id=1, source_target_pairs={{0,1},{1,0},{2,3},{3,2},{16,19},{17,18},{18,17},{19,16},{4,5},{5,4... | collective-permute-start | bytes 589832 | tf_op jit(solution)/shard_map/ppermute | solution.py:27
  60.3 0.7 collective-permute-start.12
  66.5 4.7 %collective-permute-start.15 = (f32[32,768]{1,0:T(8,128)S(1)}, f32[32,768]{1,0:T(8,128)S(1)}, u32[]{:S(2)}, u32[]{:S(2)}) collective-permute-start(f32[32,768]{1,0:T(8,128)S(1)} %get-tuple-element.74.own), channel_id=1, source_target_pairs={{0,4},{4,0},{8,12},{12,8},{16,28},{20,24},{24,20},{28,16},{1,5},{5... | collective-permute-start | bytes 294920 | tf_op jit(solution)/shard_map/ppermute | solution.py:27
  71.3 6.1 %collective-permute-start.16 = (f32[64,640]{1,0:T(8,128)S(1)}, f32[64,640]{1,0:T(8,128)S(1)}, u32[]{:S(2)}, u32[]{:S(2)}) collective-permute-start(f32[64,640]{1,0:T(8,128)S(1)} %get-tuple-element.76.own), channel_id=1, source_target_pairs={{0,1},{1,0},{2,3},{3,2},{16,19},{17,18},{18,17},{19,16},{4,5},{5,4... | collective-permute-start | bytes 491528 | tf_op jit(solution)/shard_map/ppermute | solution.py:27
  71.4 7.2 %collective-permute-start.14 = (f32[64,1024]{1,0:T(8,128)S(1)}, f32[64,1024]{1,0:T(8,128)S(1)}, u32[]{:S(2)}, u32[]{:S(2)}) collective-permute-start(f32[64,1024]{1,0:T(8,128)S(1)} %get-tuple-element.72.own), channel_id=1, source_target_pairs={{0,3},{1,2},{2,1},{3,0},{16,17},{17,16},{18,19},{19,18},{4,7},{5,6... | collective-permute-start | bytes 786440 | tf_op jit(solution)/shard_map/ppermute | solution.py:27
  77.4 6.3 %collective-permute-start.19 = (f32[128,640]{1,0:T(8,128)S(1)}, f32[128,640]{1,0:T(8,128)S(1)}, u32[]{:S(2)}, u32[]{:S(2)}) collective-permute-start(f32[128,640]{1,0:T(8,128)S(1)} %upper_3.1.refs_0_), channel_id=1, source_target_pairs={{0,3},{1,2},{2,1},{3,0},{16,17},{17,16},{18,19},{19,18},{4,7},{5,6... | collective-permute-start | bytes 983048 | tf_op jit(solution)/shard_map/ppermute | solution.py:27
  78.7 9.3 %collective-permute-start.17 = (f32[128,768]{1,0:T(8,128)S(1)}, f32[128,768]{1,0:T(8,128)S(1)}, u32[]{:S(2)}, u32[]{:S(2)}) collective-permute-start(f32[128,768]{1,0:T(8,128)S(1)} %get-tuple-element.78.refs_1_), channel_id=1, source_target_pairs={{0,4},{4,0},{8,12},{12,8},{16,28},{20,24},{24,20},{28,16},{1,5},{5... | collective-permute-start | bytes 1179656 | tf_op jit(solution)/shard_map/ppermute | solution.py:27
  79.3 9.0 %collective-permute-start.21 = (f32[128,640]{1,0:T(8,128)S(1)}, f32[128,640]{1,0:T(8,128)S(1)}, u32[]{:S(2)}, u32[]{:S(2)}) collective-permute-start(f32[128,640]{1,0:T(8,128)S(1)} %upper_3.1.refs_0_), channel_id=1, source_target_pairs={{0,12},{4,8},{8,4},{12,0},{16,20},{20,16},{24,28},{28,24},{1,13},{... | collective-permute-start | bytes 983048 | tf_op jit(solution)/shard_map/ppermute | solution.py:27
  83.7 9.5 %collective-permute-start.22 = (f32[128,640]{1,0:T(8,128)S(1)}, f32[128,640]{1,0:T(8,128)S(1)}, u32[]{:S(2)}, u32[]{:S(2)}) collective-permute-start(f32[128,640]{1,0:T(8,128)S(1)} %collective-permute-done.19.refs_0_.refs_1_), channel_id=1, source_target_pairs={{0,12},{4,8},{8,4},{12,0},{16,20},{20,16},{24,28},{28,24},{1,13},{... | collective-permute-start | bytes 983048 | tf_op jit(solution)/shard_map/ppermute | solution.py:27
  83.7 20.7 %collective-permute-start.18 = (f32[128,640]{1,0:T(8,128)S(1)}, f32[128,640]{1,0:T(8,128)S(1)}, u32[]{:S(2)}, u32[]{:S(2)}) collective-permute-start(f32[128,640]{1,0:T(8,128)S(1)} %get-tuple-element.79), channel_id=1, source_target_pairs={{0,12},{4,8},{8,4},{12,0},{16,20},{20,16},{24,28},{28,24},{1,13},{... | collective-permute-start | bytes 983048 | tf_op jit(solution)/shard_map/ppermute | solution.py:27
  88.0 16.4 %collective-permute-start.20 = (f32[128,640]{1,0:T(8,128)S(1)}, f32[128,640]{1,0:T(8,128)S(1)}, u32[]{:S(2)}, u32[]{:S(2)}) collective-permute-start(f32[128,640]{1,0:T(8,128)S(1)} %leaf_4.1), channel_id=1, source_target_pairs={{0,12},{4,8},{8,4},{12,0},{16,20},{20,16},{24,28},{28,24},{1,13},{... | collective-permute-start | bytes 983048 | tf_op jit(solution)/shard_map/ppermute | solution.py:27
  98.8 3.6 %collective-permute-start.23 = (f32[32,512]{1,0:T(8,128)S(1)}, f32[32,512]{1,0:T(8,128)S(1)}, u32[]{:S(2)}, u32[]{:S(2)}) collective-permute-start(f32[32,512]{1,0:T(8,128)S(1)} %get-tuple-element.81), channel_id=1, source_target_pairs={{0,16},{16,0},{1,17},{17,1},{2,18},{18,2},{3,19},{19,3},{4,20},{20... | collective-permute-start | bytes 196616 | tf_op jit(solution)/shard_map/ppermute | solution.py:32
  102.4 8.8 %collective-permute-start.24 = (f32[32,512]{1,0:T(8,128)S(1)}, f32[32,512]{1,0:T(8,128)S(1)}, u32[]{:S(2)}, u32[]{:S(2)}) collective-permute-start(f32[32,512]{1,0:T(8,128)S(1)} %get-tuple-element.88), channel_id=1, source_target_pairs={{0,32},{32,0},{64,96},{96,64},{128,160},{160,128},{192,224},{224,1... | collective-permute-start | bytes 196616 | tf_op jit(solution)/shard_map/ppermute | solution.py:32

commit v4 on v3

--- a/solution.py
+++ b/solution.py
@@ -125,17 +125,21 @@
         0.0,
     )
 
+    half = K // 2
+
     def times(square, rows, high, low):
         rows_high, rows_low = parts2(rows)
-        left = [rows_high, rows_low] if square is None else [square, rows_high, rows_low]
-        first = product(jnp.concatenate(left, 0), high)
-        second = product(jnp.concatenate(left[:-1], 0), low)
-        start = 0 if square is None else K
-        moved = (second[start:] + first[start + count :]) + first[start : start + count]
         if square is None:
-            return None, moved
+            first = product(jnp.concatenate([rows_high, rows_low], 0), high)
+            return None, (product(rows_high, low) + first[count:]) + first[:count]
+        first = product(jnp.concatenate([square[:half], rows_high, rows_low], 0), high)
+        corner = product(square[half:], high[:, half:])
+        second = product(jnp.concatenate([square, rows_high], 0), low)
+        moved = (second[K:] + first[half + count :]) + first[half : half + count]
+        top = first[:half]
+        main = jnp.concatenate([top, jnp.concatenate([top[:, half:].T, corner], 1)], 0)
         mixed = second[:K]
-        return first[:K] + (mixed + mixed.T), moved
+        return main + (mixed + mixed.T), moved
 
     high, low = parts2(skeleton)
     gram, cross = times(parts2(skeleton.T)[0], redundant.T, high, low)
@@ -323,26 +327,55 @@
     pack(leaf, rest, got, payload_ref, rest_ref)
 
 
+def orders_kernel(
+    ranks_ref, leaf_ref, upper_ref, head_ref, rest_ref, one_ref, two_ref, three_ref, leaf_slots, slots
+):
+    z, core, y, x = (lax.axis_index(name) for name in ("z", "core", "y", "x"))
+    row_index = z * 2 + core
+    near = jnp.where(core == 0, 1, 3)
+    far = 4 - near
+    position = lax.broadcasted_iota(jnp.int32, (1, K), 1)
+    head_ref[...] = jnp.where(position < ranks_ref[0, row_index], leaf_ref[:, :K], -1)
+    orders = (one_ref, two_ref, three_ref)
+    rests = []
+    for level in (1, 2, 3):
+        node, side = row_index >> level, row_index >> (level - 1) & 1
+        pivots = upper_ref[level - 1, pl.ds(node, 1), :] ^ (side << 9)
+        head = jnp.where(position < ranks_ref[level, node], pivots[:, :K], -1)
+        orders[level - 1][:, :K] = head
+        rests.append(pivots[:, K:])
+    rests = jnp.concatenate(rests, 0)
+    leaf_slots[...] = jnp.full_like(leaf_slots, -1)
+    for i in range(16):
+        leaf_slots[:, i * 128 : i * 128 + 96] = leaf_ref[:, K + i * 96 : K + i * 96 + 96]
+        slots[:, i * 128 : i * 128 + 32] = rests[:, i * 32 : i * 32 + 32]
+    for i in range(16):
+        bit = [i >> shift & 1 for shift in (3, 2, 1, 0)]
+        owner = (y ^ bit[2] * near ^ bit[3] * far) * 4 + (x ^ bit[0] * near ^ bit[1] * far)
+        rest_ref[:, i * 128 : i * 128 + 128] = leaf_slots[:, pl.ds(pl.multiple_of(owner * 128, 128), 128)]
+        owner = (y ^ bit[0] * near ^ bit[3] * far) * 4 + (x ^ bit[1] * near ^ bit[2] * far)
+        block = slots[:, pl.ds(pl.multiple_of(owner * 128, 128), 128)]
+        for level in range(3):
+            orders[level][:, K + i * 32 : K + i * 32 + 32] = block[level : level + 1, :32]
+
+
+def pivot_orders(ranks, leaf_pivots, upper_pivots):
+    shapes = (K, LEAF, 2 * K, 2 * K, 2 * K)
+    return pl.pallas_call(
+        orders_kernel,
+        in_specs=[pl.BlockSpec(memory_space=pltpu.SMEM), VMEM, VMEM],
+        out_specs=[VMEM] * 5,
+        out_shape=[jax.ShapeDtypeStruct((1, size), jnp.int32) for size in shapes],
+        scratch_shapes=[pltpu.VMEM((1, LEAF), jnp.int32), pltpu.VMEM((3, LEAF), jnp.int32)],
+        compiler_params=pltpu.CompilerParams(vmem_limit_bytes=16 * 2**20),
+        cost_estimate=pl.CostEstimate(flops=10**6, bytes_accessed=10**5, transcendentals=0),
+        name="pivot_orders",
+    )(ranks, leaf_pivots, upper_pivots)
+
+
 def local(a_matrix, omega, leaf_pivots, upper_pivots, ranks):
     z, core, y, x = (lax.axis_index(name) for name in ("z", "core", "y", "x"))
-    row_index = z * 2 + core
-
-    near = jnp.where(core == 0, 1, 3)
-    far = 4 - near
-    bit = [jnp.arange(16) >> i & 1 for i in (3, 2, 1, 0)]
-    leaf_owners = (y ^ bit[2] * near ^ bit[3] * far) * 4 + (x ^ bit[0] * near ^ bit[1] * far)
-    upper_owners = (y ^ bit[0] * near ^ bit[3] * far) * 4 + (x ^ bit[1] * near ^ bit[2] * far)
-    position = jnp.arange(K)
-    leaf_order = jnp.where(position < ranks[0, row_index], leaf_pivots[0, :K], -1)[None]
-    leaf_rest = jnp.take(leaf_pivots[0, K:].reshape(16, 96), leaf_owners, axis=0)
-    leaf_rest = jnp.pad(leaf_rest, ((0, 0), (0, 32)), constant_values=-1).reshape(1, LEAF)
-    orders = []
-    for level in (1, 2, 3):
-        node, side = row_index >> level, row_index >> (level - 1) & 1
-        pivots = upper_pivots[level - 1, node] ^ (side << 9)
-        head = jnp.where(position < ranks[level, node], pivots[:K], -1)
-        rest = jnp.take(pivots[K:].reshape(16, 32), upper_owners, axis=0).reshape(K)
-        orders.append(jnp.concatenate([head, rest])[None])
+    leaf_order, leaf_rest, *orders = pivot_orders(ranks, leaf_pivots, upper_pivots)
 
     near_a, both_a, near_b, both_b = ordered_samples(omega, a_matrix, True)
     got_both = hop(both_a, "x", True), hop(both_b, "y", True)

time: 112 us -> 107 us (0.955)
  waiting for transfers between devices: 43.5 us -> 52 us
  local copies, waits for them, and re-layouts: 6.31 us -> 0.03 us
  other arithmetic: 4.22 us -> 0.72 us
  starting transfers between devices: 30.2 us -> 26.8 us
    ppermute x20, waiting for transfers between devices: 41.1 us -> 49.6 us  [hop(): return lax.ppermute(block, ('core', axis), route)]
    ppermute x4, starting transfers between devices: 14.1 us -> 10.6 us  [swapped(): return lax.ppermute(block, axis, [(i, i ^ mask) for i in range(count)])]
    unnamed x8 -> x10, local copies, waits for them, and re-layouts: 2.79 us -> 0.03 us
    select_n x7 -> x0, other arithmetic: 2.65 us -> none  [the longest x3 1.84 us: local(): head = jnp.where(position < ranks[level, node], pivots[:K], -1)]
    gather x4 -> x0, local copies, waits for them, and re-layouts: 2.25 us -> none  [the longest x3 1.69 us: local(): rest = jnp.take(pivots[K:].reshape(16, 32), upper_owners, axis=0).reshape(K)]
    pallas_call x6, Pallas kernels: 2.12 us -> 0.38 us  [added(): pl.pallas_call(functools.partial(add_kernel, first=first), in_specs=[VMEM...]
  transfers between devices with their start and end apart: 25 -> 25, of which waited for: 16 -> 20; matrix products, arithmetic and copies ran while one was open for 6% -> 0% of each run, Pallas kernels for 16% -> 17%
where the time goes in v4:
time: 107 us; the launch traced here: 106 us
  waiting for transfers between devices  52 us (49%)
  starting transfers between devices  26.8 us (25%)
  Pallas kernels  26.1 us (24%)
    ppermute x20, waiting for transfers between devices, hop(): return lax.ppermute(block, ('core', axis), route)  49.6 us
    ppermute x20, starting transfers between devices, hop(): return lax.ppermute(block, ('core', axis), route)  15.6 us
    pallas_call x2, Pallas kernels, solve(): pl.pallas_call(functools.partial(solve_kernel, packed=packed), out_shape=...  12.5 us
    ppermute x4, starting transfers between devices, swapped(): return lax.ppermute(block, axis, [(i, i ^ mask) for i in range(count)])  10.6 us
    pallas_call x2, Pallas kernels, ordered_samples(): pl.pallas_call(functools.partial(ordered_kernel, sent=sent), grid=(LEAF /...  8.95 us
    pallas_call x8, Pallas kernels, call(): pl.pallas_call(kernel, in_specs=[VMEM] * len(inputs) + [ANY] * len(after)...  2.96 us
    ppermute x4, waiting for transfers between devices, swapped(): return lax.ppermute(block, axis, [(i, i ^ mask) for i in range(count)])  2.41 us
  transfers between devices with their start and end apart: 25, of which 20 were waited for; matrix products, arithmetic and copies ran while one was open for 0% of the time, Pallas kernels for 17%

profile of v4, /device:TPU:1, one launch (start us, length us, event | category | flops | bytes accessed | tf_op | source)
XLA Modules:
  0.0 106.5 jit_solution(5979281209148247378)
XLA Ops:
  0.6 6.1 %sent_samples.1 = (f32[64,2048]{1,0:T(8,128)}, f32[64,2048]{1,0:T(8,128)}, f32[64,2048]{1,0:T(8,128)}, f32[64,2048]{1,0:T(8,128)}) custom-call(bf16[1536,512]{1,0:T(8,128)(2,1)} %omega_ref.3, bf16[2048,1536]{1,0:T(8,128)(2,1)} %a_ref.3), custom_call_target="tpu_custom_call" | custom-call | flops 2013265920 | bytes 9961472 | tf_op jit(solution)/shard_map/sent_samples/pallas_call | solution.py:73
  6.8 3.3 %collective-permute-start.2 = (f32[64,2048]{1,0:T(8,128)}, f32[64,2048]{1,0:T(8,128)S(1)}, u32[]{:S(2)}, u32[]{:S(2)}) collective-permute-start(f32[64,2048]{1,0:T(8,128)} %get-tuple-element.57), channel_id=1, source_target_pairs={{0,1},{1,0},{2,3},{3,2},{16,19},{17,18},{18,17},{19,16},{4,5},{5,4... | collective-permute-start | bytes 1572872 | tf_op jit(solution)/shard_map/ppermute | solution.py:27
  10.1 2.7 %collective-permute-start.3 = (f32[64,2048]{1,0:T(8,128)}, f32[64,2048]{1,0:T(8,128)S(1)}, u32[]{:S(2)}, u32[]{:S(2)}) collective-permute-start(f32[64,2048]{1,0:T(8,128)} %get-tuple-element.59), channel_id=1, source_target_pairs={{0,4},{4,0},{8,12},{12,8},{16,28},{20,24},{24,20},{28,16},{1,5},{5... | collective-permute-start | bytes 1572872 | tf_op jit(solution)/shard_map/ppermute | solution.py:27
  12.8 0.2 collective-permute-start
  13.0 0.0 collective-permute-start.1
  13.0 2.8 %kept_samples.1 = (f32[64,2048]{1,0:T(8,128)S(1)}, f32[64,2048]{1,0:T(8,128)S(1)}, f32[64,2048]{1,0:T(8,128)S(1)}, f32[64,2048]{1,0:T(8,128)S(1)}) custom-call(bf16[1536,512]{1,0:T(8,128)(2,1)S(1)} %copy-done.1, bf16[2048,1536]{1,0:T(8,128)(2,1)S(1)} %copy-done), custom_call_target="tpu_custom_call" | custom-call | flops 2013265920 | bytes 9961472 | tf_op jit(solution)/shard_map/kept_samples/pallas_call | solution.py:73
  15.9 0.0 copy-start.2
  15.9 0.0 copy-start.3
  15.9 0.0 copy-start.4
  15.9 1.0 collective-permute-done.2.got_a
  16.9 2.7 %collective-permute-done.3.got_b = f32[64,2048]{1,0:T(8,128)S(1)} collective-permute-done((f32[64,2048]{1,0:T(8,128)}, f32[64,2048]{1,0:T(8,128)S(1)}, u32[]{:S(2)}, u32[]{:S(2)}) %collective-permute-start.3) | collective-permute-done | bytes 524320 | tf_op jit(solution)/shard_map/ppermute | solution.py:27
  19.6 0.1 add_sent.3
  19.7 0.1 collective-permute-start.4
  19.8 0.4 collective-permute-start.5
  20.2 2.3 %collective-permute-done.got_a = f32[64,2048]{1,0:T(8,128)S(1)} collective-permute-done((f32[64,2048]{1,0:T(8,128)}, f32[64,2048]{1,0:T(8,128)S(1)}, u32[]{:S(2)}, u32[]{:S(2)}) %collective-permute-start) | collective-permute-done | bytes 524320 | tf_op jit(solution)/shard_map/ppermute | solution.py:27
  22.5 3.0 %collective-permute-done.1.got_b = f32[64,2048]{1,0:T(8,128)S(1)} collective-permute-done((f32[64,2048]{1,0:T(8,128)}, f32[64,2048]{1,0:T(8,128)S(1)}, u32[]{:S(2)}, u32[]{:S(2)}) %collective-permute-start.1) | collective-permute-done | bytes 524320 | tf_op jit(solution)/shard_map/ppermute | solution.py:27
  25.5 0.1 add_kept.3
  25.6 4.6 %collective-permute-done.4.got_a = f32[64,2048]{1,0:T(8,128)S(1)} collective-permute-done((f32[64,2048]{1,0:T(8,128)S(1)}, f32[64,2048]{1,0:T(8,128)S(1)}, u32[]{:S(2)}, u32[]{:S(2)}) %collective-permute-start.4) | collective-permute-done | bytes 524320 | tf_op jit(solution)/shard_map/ppermute | solution.py:27
  30.2 0.1 collective-permute-done.5.got_b
  30.3 0.1 add_sent.4
  30.4 2.5 %collective-permute-start.6 = (f32[32,2048]{1,0:T(8,128)S(1)}, f32[32,2048]{1,0:T(8,128)S(1)}, u32[]{:S(2)}, u32[]{:S(2)}) collective-permute-start(f32[32,2048]{1,0:T(8,128)S(1)} %get-tuple-element.64), channel_id=1, source_target_pairs={{0,4},{4,0},{8,12},{12,8},{16,28},{20,24},{24,20},{28,16},{1,5},{5... | collective-permute-start | bytes 786440 | tf_op jit(solution)/shard_map/ppermute | solution.py:27
  32.9 1.8 %collective-permute-start.7 = (f32[32,2048]{1,0:T(8,128)S(1)}, f32[32,2048]{1,0:T(8,128)S(1)}, u32[]{:S(2)}, u32[]{:S(2)}) collective-permute-start(f32[32,2048]{1,0:T(8,128)S(1)} %get-tuple-element.66), channel_id=1, source_target_pairs={{0,1},{1,0},{2,3},{3,2},{16,19},{17,18},{18,17},{19,16},{4,5},{5,4... | collective-permute-start | bytes 786440 | tf_op jit(solution)/shard_map/ppermute | solution.py:27
  34.7 0.1 add_kept.4
  34.8 2.1 %collective-permute-done.6.got_a = f32[32,2048]{1,0:T(8,128)S(1)} collective-permute-done((f32[32,2048]{1,0:T(8,128)S(1)}, f32[32,2048]{1,0:T(8,128)S(1)}, u32[]{:S(2)}, u32[]{:S(2)}) %collective-permute-start.6) | collective-permute-done | bytes 262176 | tf_op jit(solution)/shard_map/ppermute | solution.py:27
  36.9 2.4 %collective-permute-done.7.got_b = f32[32,2048]{1,0:T(8,128)S(1)} collective-permute-done((f32[32,2048]{1,0:T(8,128)S(1)}, f32[32,2048]{1,0:T(8,128)S(1)}, u32[]{:S(2)}, u32[]{:S(2)}) %collective-permute-start.7) | collective-permute-done | bytes 262176 | tf_op jit(solution)/shard_map/ppermute | solution.py:27
  39.4 0.1 collective-permute-start.8
  39.5 0.1 collective-permute-start.9
  39.6 0.8 pivot_orders.1
  40.4 3.1 %collective-permute-done.8.refs_1_ = f32[16,2048]{1,0:T(8,128)S(1)} collective-permute-done((f32[16,2048]{1,0:T(8,128)S(1)}, f32[16,2048]{1,0:T(8,128)S(1)}, u32[]{:S(2)}, u32[]{:S(2)}) %collective-permute-start.8) | collective-permute-done | bytes 131104 | tf_op jit(solution)/shard_map/ppermute | solution.py:27
  43.6 0.1 collective-permute-done.9.refs_3_
  43.7 0.5 finish_samples.1
  44.1 4.2 %collective-permute-start.10 = (f32[32,512]{1,0:T(8,128)S(1)}, f32[32,512]{1,0:T(8,128)S(1)}, u32[]{:S(2)}, u32[]{:S(2)}) collective-permute-start(f32[32,512]{1,0:T(8,128)S(1)} %get-tuple-element.71.own.skeleton_ref), channel_id=1, source_target_pairs={{0,16},{16,0},{1,17},{17,1},{2,18},{18,2},{3,19},{19,3},{4,20},{20... | collective-permute-start | bytes 196616 | tf_op jit(solution)/shard_map/ppermute | solution.py:32
  48.3 0.9 collective-permute-done.10.sibling
  49.2 0.5 level_1.1
  49.6 1.7 %collective-permute-start.11 = (f32[32,512]{1,0:T(8,128)S(1)}, f32[32,512]{1,0:T(8,128)S(1)}, u32[]{:S(2)}, u32[]{:S(2)}) collective-permute-start(f32[32,512]{1,0:T(8,128)S(1)} %get-tuple-element.72.own.skeleton_1), channel_id=1, source_target_pairs={{0,32},{32,0},{64,96},{96,64},{128,160},{160,128},{192,224},{224,1... | collective-permute-start | bytes 196616 | tf_op jit(solution)/shard_map/ppermute | solution.py:32
  51.3 1.5 %leaf_redundant.1 = (f32[32,1536]{1,0:T(8,128)S(1)}, f32[32,1024]{1,0:T(8,128)S(1)}) custom-call(s32[1,2048]{1,0:T(1,128)S(1)} %get-tuple-element.73.order_ref, bf16[96,2048]{1,0:T(8,128)(2,1)S(1)} %get-tuple-element.74.parts_ref, f32[32,512]{1,0:T(8,128)S(1)} %get-tuple-element.71.own.skeleton_ref), custom_call_target="tpu_custom_call" | custom-call | flops 805306368 | bytes 1000000 | tf_op jit(solution)/shard_map/leaf_redundant/pallas_call | solution.py:241
  52.8 0.6 collective-permute-done.11.sibling
  53.4 0.5 level_2.1
  53.8 1.0 collective-permute-start.13
  54.9 0.7 collective-permute-start.12
  55.5 0.0 collective-permute-done.12.sibling
  55.6 4.2 %collective-permute-done.13.got = f32[32,1536]{1,0:T(8,128)S(1)} collective-permute-done((f32[32,1536]{1,0:T(8,128)S(1)}, f32[32,1536]{1,0:T(8,128)S(1)}, u32[]{:S(2)}, u32[]{:S(2)}) %collective-permute-start.13) | collective-permute-done | bytes 196640 | tf_op jit(solution)/shard_map/ppermute | solution.py:27
  59.7 0.5 level_3.1
  60.2 0.3 collective-permute-start.15
  60.5 4.5 %collective-permute-done.15.got = f32[32,768]{1,0:T(8,128)S(1)} collective-permute-done((f32[32,768]{1,0:T(8,128)S(1)}, f32[32,768]{1,0:T(8,128)S(1)}, u32[]{:S(2)}, u32[]{:S(2)}) %collective-permute-start.15) | collective-permute-done | bytes 98336 | tf_op jit(solution)/shard_map/ppermute | solution.py:27
  65.0 0.9 collective-permute-start.16
  65.9 0.0 collective-permute-start.14
  65.9 5.1 %collective-permute-done.16.refs_0_.got = f32[64,640]{1,0:T(8,128)S(1)} collective-permute-done((f32[64,640]{1,0:T(8,128)S(1)}, f32[64,640]{1,0:T(8,128)S(1)}, u32[]{:S(2)}, u32[]{:S(2)}) %collective-permute-start.16) | collective-permute-done | bytes 163872 | tf_op jit(solution)/shard_map/ppermute | solution.py:27
  71.0 0.1 collective-permute-start.19
  71.2 2.0 %collective-permute-done.14.got = f32[64,1024]{1,0:T(8,128)S(1)} collective-permute-done((f32[64,1024]{1,0:T(8,128)S(1)}, f32[64,1024]{1,0:T(8,128)S(1)}, u32[]{:S(2)}, u32[]{:S(2)}) %collective-permute-start.14) | collective-permute-done | bytes 262176 | tf_op jit(solution)/shard_map/ppermute | solution.py:27
  73.2 0.1 leaf_3.1
  73.3 0.4 collective-permute-start.17
  73.6 3.7 %collective-permute-done.19.refs_0_.refs_1_ = f32[128,640]{1,0:T(8,128)S(1)} collective-permute-done((f32[128,640]{1,0:T(8,128)S(1)}, f32[128,640]{1,0:T(8,128)S(1)}, u32[]{:S(2)}, u32[]{:S(2)}) %collective-permute-start.19) | collective-permute-done | bytes 327712 | tf_op jit(solution)/shard_map/ppermute | solution.py:27
  77.4 1.5 %collective-permute-start.18 = (f32[128,640]{1,0:T(8,128)S(1)}, f32[128,640]{1,0:T(8,128)S(1)}, u32[]{:S(2)}, u32[]{:S(2)}) collective-permute-start(f32[128,640]{1,0:T(8,128)S(1)} %get-tuple-element.88), channel_id=1, source_target_pairs={{0,12},{4,8},{8,4},{12,0},{16,20},{20,16},{24,28},{28,24},{1,13},{... | collective-permute-start | bytes 983048 | tf_op jit(solution)/shard_map/ppermute | solution.py:27
  78.8 4.0 %collective-permute-done.17.got.refs_2_ = f32[128,768]{1,0:T(8,128)S(1)} collective-permute-done((f32[128,768]{1,0:T(8,128)S(1)}, f32[128,768]{1,0:T(8,128)S(1)}, u32[]{:S(2)}, u32[]{:S(2)}) %collective-permute-start.17) | collective-permute-done | bytes 393248 | tf_op jit(solution)/shard_map/ppermute | solution.py:27
  82.9 0.1 collective-permute-start.20
  83.0 0.0 collective-permute-done.21.refs_2_
  83.0 4.6 %collective-permute-done.22.refs_3_ = f32[128,640]{1,0:T(8,128)S(1)} collective-permute-done((f32[128,640]{1,0:T(8,128)S(1)}, f32[128,640]{1,0:T(8,128)S(1)}, u32[]{:S(2)}, u32[]{:S(2)}) %collective-permute-start.22) | collective-permute-done | bytes 327712 | tf_op jit(solution)/shard_map/ppermute | solution.py:27
  87.6 5.6 %solve_upper.1 = (f32[32,512]{1,0:T(8,128)S(1)}, f32[8,128]{1,0:T(8,128)}) custom-call(f32[128,640]{1,0:T(8,128)S(1)} %upper_3.1.refs_0_, f32[128,640]{1,0:T(8,128)S(1)} %collective-permute-done.19.refs_0_.refs_1_, f32[128,640]{1,0:T(8,128)S(1)} %collective-permute-done.21.refs_2_, f32[128,640]{1,0:T(8,128)S(1)} %collective-permute-done.22.refs_3_), custom_call_target="tpu_custom_call" | custom-call | flops 5133828096 | bytes 1114112 | tf_op jit(solution)/shard_map/solve_upper/pallas_call | solution.py:158
  93.2 2.1 %collective-permute-start.23 = (f32[32,512]{1,0:T(8,128)S(1)}, f32[32,512]{1,0:T(8,128)S(1)}, u32[]{:S(2)}, u32[]{:S(2)}) collective-permute-start(f32[32,512]{1,0:T(8,128)S(1)} %get-tuple-element.90), channel_id=1, source_target_pairs={{0,16},{16,0},{1,17},{17,1},{2,18},{18,2},{3,19},{19,3},{4,20},{20... | collective-permute-start | bytes 196616 | tf_op jit(solution)/shard_map/ppermute | solution.py:32
  95.3 0.9 collective-permute-done.23.refs_5_
  96.2 2.7 %collective-permute-start.24 = (f32[32,512]{1,0:T(8,128)S(1)}, f32[32,512]{1,0:T(8,128)S(1)}, u32[]{:S(2)}, u32[]{:S(2)}) collective-permute-start(f32[32,512]{1,0:T(8,128)S(1)} %get-tuple-element.95), channel_id=1, source_target_pairs={{0,32},{32,0},{64,96},{96,64},{128,160},{160,128},{192,224},{224,1... | collective-permute-start | bytes 196616 | tf_op jit(solution)/shard_map/ppermute | solution.py:32
  98.9 6.9 %solve_leaf.1 = (f32[96,512]{1,0:T(8,128)}, f32[8,128]{1,0:T(8,128)}) custom-call(f32[128,128]{1,0:T(8,128)S(1)} %get-tuple-element.86.refs_0_, f32[128,768]{1,0:T(8,128)S(1)} %get-tuple-element.87.refs_1_, f32[128,768]{1,0:T(8,128)S(1)} %collective-permute-done.17.got.refs_2_, f32[128,640]{1,0:T(8,128)S(1)} %collective-permute-done.18.refs_3_, ...), custom_call_target="tpu_custom_call" | custom-call | flops 5737807872 | bytes 1245184 | tf_op jit(solution)/shard_map/solve_leaf/pallas_call | solution.py:158
  105.8 0.7 maximum_bitcast_fusion
  (20 shorter events, 0.2 us)
Async XLA Ops:
  0.6 12.4 %copy-start = (bf16[2048,1536]{1,0:T(8,128)(2,1)S(1)}, bf16[2048,1536]{1,0:T(8,128)(2,1)}, u32[]{:S(2)}) copy-start(bf16[2048,1536]{1,0:T(8,128)(2,1)} %a_ref.3) | copy-start | bytes 18874372
  0.6 12.4 %copy-start.1 = (bf16[1536,512]{1,0:T(8,128)(2,1)S(1)}, bf16[1536,512]{1,0:T(8,128)(2,1)}, u32[]{:S(2)}) copy-start(bf16[1536,512]{1,0:T(8,128)(2,1)} %omega_ref.3) | copy-start | bytes 4718596
  6.8 10.1 %collective-permute-start.2 = (f32[64,2048]{1,0:T(8,128)}, f32[64,2048]{1,0:T(8,128)S(1)}, u32[]{:S(2)}, u32[]{:S(2)}) collective-permute-start(f32[64,2048]{1,0:T(8,128)} %get-tuple-element.57), channel_id=1, source_target_pairs={{0,1},{1,0},{2,3},{3,2},{16,19},{17,18},{18,17},{19,16},{4,5},{5,4... | collective-permute-start | bytes 1572872 | tf_op jit(solution)/shard_map/ppermute | solution.py:27
  10.1 9.5 %collective-permute-start.3 = (f32[64,2048]{1,0:T(8,128)}, f32[64,2048]{1,0:T(8,128)S(1)}, u32[]{:S(2)}, u32[]{:S(2)}) collective-permute-start(f32[64,2048]{1,0:T(8,128)} %get-tuple-element.59), channel_id=1, source_target_pairs={{0,4},{4,0},{8,12},{12,8},{16,28},{20,24},{24,20},{28,16},{1,5},{5... | collective-permute-start | bytes 1572872 | tf_op jit(solution)/shard_map/ppermute | solution.py:27
  12.8 9.7 %collective-permute-start = (f32[64,2048]{1,0:T(8,128)}, f32[64,2048]{1,0:T(8,128)S(1)}, u32[]{:S(2)}, u32[]{:S(2)}) collective-permute-start(f32[64,2048]{1,0:T(8,128)} %get-tuple-element.52), channel_id=1, source_target_pairs={{0,1},{1,0},{2,3},{3,2},{16,19},{17,18},{18,17},{19,16},{4,5},{5,4... | collective-permute-start | bytes 1572872 | tf_op jit(solution)/shard_map/ppermute | solution.py:27
  13.0 12.5 %collective-permute-start.1 = (f32[64,2048]{1,0:T(8,128)}, f32[64,2048]{1,0:T(8,128)S(1)}, u32[]{:S(2)}, u32[]{:S(2)}) collective-permute-start(f32[64,2048]{1,0:T(8,128)} %get-tuple-element.54), channel_id=1, source_target_pairs={{0,4},{4,0},{8,12},{12,8},{16,28},{20,24},{24,20},{28,16},{1,5},{5... | collective-permute-start | bytes 1572872 | tf_op jit(solution)/shard_map/ppermute | solution.py:27
  15.9 23.7 %copy-start.2 = (s32[3,8,1024]{2,1,0:T(8,128)S(1)}, s32[3,8,1024]{2,1,0:T(8,128)}, u32[]{:S(2)}) copy-start(s32[3,8,1024]{2,1,0:T(8,128)} %upper_ref.1) | copy-start | bytes 294916
  15.9 23.7 %copy-start.3 = (s32[1,2048]{1,0:T(1,128)S(1)}, s32[1,2048]{1,0:T(1,128)}, u32[]{:S(2)}) copy-start(s32[1,2048]{1,0:T(1,128)} %leaf_ref.1) | copy-start | bytes 24580
  15.9 23.7 %copy-start.4 = (s32[4,16]{1,0:T(4,128)S(1)}, s32[4,16]{1,0:T(4,128)}, u32[]{:S(2)}) copy-start(s32[4,16]{1,0:T(4,128)} %ranks_ref.1) | copy-start | bytes 772
  19.7 10.5 %collective-permute-start.4 = (f32[64,2048]{1,0:T(8,128)S(1)}, f32[64,2048]{1,0:T(8,128)S(1)}, u32[]{:S(2)}, u32[]{:S(2)}) collective-permute-start(f32[64,2048]{1,0:T(8,128)S(1)} %get-tuple-element.60), channel_id=1, source_target_pairs={{0,3},{1,2},{2,1},{3,0},{16,17},{17,16},{18,19},{19,18},{4,7},{5,6... | collective-permute-start | bytes 1572872 | tf_op jit(solution)/shard_map/ppermute | solution.py:27
  19.8 10.5 %collective-permute-start.5 = (f32[64,2048]{1,0:T(8,128)S(1)}, f32[64,2048]{1,0:T(8,128)S(1)}, u32[]{:S(2)}, u32[]{:S(2)}) collective-permute-start(f32[64,2048]{1,0:T(8,128)S(1)} %get-tuple-element.62), channel_id=1, source_target_pairs={{0,12},{4,8},{8,4},{12,0},{16,20},{20,16},{24,28},{28,24},{1,13},{... | collective-permute-start | bytes 1572872 | tf_op jit(solution)/shard_map/ppermute | solution.py:27
  30.4 6.5 %collective-permute-start.6 = (f32[32,2048]{1,0:T(8,128)S(1)}, f32[32,2048]{1,0:T(8,128)S(1)}, u32[]{:S(2)}, u32[]{:S(2)}) collective-permute-start(f32[32,2048]{1,0:T(8,128)S(1)} %get-tuple-element.64), channel_id=1, source_target_pairs={{0,4},{4,0},{8,12},{12,8},{16,28},{20,24},{24,20},{28,16},{1,5},{5... | collective-permute-start | bytes 786440 | tf_op jit(solution)/shard_map/ppermute | solution.py:27
  32.9 6.4 %collective-permute-start.7 = (f32[32,2048]{1,0:T(8,128)S(1)}, f32[32,2048]{1,0:T(8,128)S(1)}, u32[]{:S(2)}, u32[]{:S(2)}) collective-permute-start(f32[32,2048]{1,0:T(8,128)S(1)} %get-tuple-element.66), channel_id=1, source_target_pairs={{0,1},{1,0},{2,3},{3,2},{16,19},{17,18},{18,17},{19,16},{4,5},{5,4... | collective-permute-start | bytes 786440 | tf_op jit(solution)/shard_map/ppermute | solution.py:27
  39.4 4.2 %collective-permute-start.8 = (f32[16,2048]{1,0:T(8,128)S(1)}, f32[16,2048]{1,0:T(8,128)S(1)}, u32[]{:S(2)}, u32[]{:S(2)}) collective-permute-start(f32[16,2048]{1,0:T(8,128)S(1)} %get-tuple-element.68), channel_id=1, source_target_pairs={{0,12},{4,8},{8,4},{12,0},{16,20},{20,16},{24,28},{28,24},{1,13},{... | collective-permute-start | bytes 393224 | tf_op jit(solution)/shard_map/ppermute | solution.py:27
  39.5 4.2 %collective-permute-start.9 = (f32[16,2048]{1,0:T(8,128)S(1)}, f32[16,2048]{1,0:T(8,128)S(1)}, u32[]{:S(2)}, u32[]{:S(2)}) collective-permute-start(f32[16,2048]{1,0:T(8,128)S(1)} %get-tuple-element.70), channel_id=1, source_target_pairs={{0,3},{1,2},{2,1},{3,0},{16,17},{17,16},{18,19},{19,18},{4,7},{5,6... | collective-permute-start | bytes 393224 | tf_op jit(solution)/shard_map/ppermute | solution.py:27
  44.1 5.1 %collective-permute-start.10 = (f32[32,512]{1,0:T(8,128)S(1)}, f32[32,512]{1,0:T(8,128)S(1)}, u32[]{:S(2)}, u32[]{:S(2)}) collective-permute-start(f32[32,512]{1,0:T(8,128)S(1)} %get-tuple-element.71.own.skeleton_ref), channel_id=1, source_target_pairs={{0,16},{16,0},{1,17},{17,1},{2,18},{18,2},{3,19},{19,3},{4,20},{20... | collective-permute-start | bytes 196616 | tf_op jit(solution)/shard_map/ppermute | solution.py:32
  49.6 3.7 %collective-permute-start.11 = (f32[32,512]{1,0:T(8,128)S(1)}, f32[32,512]{1,0:T(8,128)S(1)}, u32[]{:S(2)}, u32[]{:S(2)}) collective-permute-start(f32[32,512]{1,0:T(8,128)S(1)} %get-tuple-element.72.own.skeleton_1), channel_id=1, source_target_pairs={{0,32},{32,0},{64,96},{96,64},{128,160},{160,128},{192,224},{224,1... | collective-permute-start | bytes 196616 | tf_op jit(solution)/shard_map/ppermute | solution.py:32
  53.8 5.9 %collective-permute-start.13 = (f32[32,1536]{1,0:T(8,128)S(1)}, f32[32,1536]{1,0:T(8,128)S(1)}, u32[]{:S(2)}, u32[]{:S(2)}) collective-permute-start(f32[32,1536]{1,0:T(8,128)S(1)} %get-tuple-element.77.leaf), channel_id=1, source_target_pairs={{0,1},{1,0},{2,3},{3,2},{16,19},{17,18},{18,17},{19,16},{4,5},{5,4... | collective-permute-start | bytes 589832 | tf_op jit(solution)/shard_map/ppermute | solution.py:27
  54.9 0.7 collective-permute-start.12
  60.2 4.7 %collective-permute-start.15 = (f32[32,768]{1,0:T(8,128)S(1)}, f32[32,768]{1,0:T(8,128)S(1)}, u32[]{:S(2)}, u32[]{:S(2)}) collective-permute-start(f32[32,768]{1,0:T(8,128)S(1)} %get-tuple-element.83.own), channel_id=1, source_target_pairs={{0,4},{4,0},{8,12},{12,8},{16,28},{20,24},{24,20},{28,16},{1,5},{5... | collective-permute-start | bytes 294920 | tf_op jit(solution)/shard_map/ppermute | solution.py:27
  65.0 6.0 %collective-permute-start.16 = (f32[64,640]{1,0:T(8,128)S(1)}, f32[64,640]{1,0:T(8,128)S(1)}, u32[]{:S(2)}, u32[]{:S(2)}) collective-permute-start(f32[64,640]{1,0:T(8,128)S(1)} %get-tuple-element.85.own), channel_id=1, source_target_pairs={{0,1},{1,0},{2,3},{3,2},{16,19},{17,18},{18,17},{19,16},{4,5},{5,4... | collective-permute-start | bytes 491528 | tf_op jit(solution)/shard_map/ppermute | solution.py:27
  65.9 7.3 %collective-permute-start.14 = (f32[64,1024]{1,0:T(8,128)S(1)}, f32[64,1024]{1,0:T(8,128)S(1)}, u32[]{:S(2)}, u32[]{:S(2)}) collective-permute-start(f32[64,1024]{1,0:T(8,128)S(1)} %get-tuple-element.81.own), channel_id=1, source_target_pairs={{0,3},{1,2},{2,1},{3,0},{16,17},{17,16},{18,19},{19,18},{4,7},{5,6... | collective-permute-start | bytes 786440 | tf_op jit(solution)/shard_map/ppermute | solution.py:27
  71.0 6.3 %collective-permute-start.19 = (f32[128,640]{1,0:T(8,128)S(1)}, f32[128,640]{1,0:T(8,128)S(1)}, u32[]{:S(2)}, u32[]{:S(2)}) collective-permute-start(f32[128,640]{1,0:T(8,128)S(1)} %upper_3.1.refs_0_), channel_id=1, source_target_pairs={{0,3},{1,2},{2,1},{3,0},{16,17},{17,16},{18,19},{19,18},{4,7},{5,6... | collective-permute-start | bytes 983048 | tf_op jit(solution)/shard_map/ppermute | solution.py:27
  73.3 9.6 %collective-permute-start.17 = (f32[128,768]{1,0:T(8,128)S(1)}, f32[128,768]{1,0:T(8,128)S(1)}, u32[]{:S(2)}, u32[]{:S(2)}) collective-permute-start(f32[128,768]{1,0:T(8,128)S(1)} %get-tuple-element.87.refs_1_), channel_id=1, source_target_pairs={{0,4},{4,0},{8,12},{12,8},{16,28},{20,24},{24,20},{28,16},{1,5},{5... | collective-permute-start | bytes 1179656 | tf_op jit(solution)/shard_map/ppermute | solution.py:27
  73.6 9.3 %collective-permute-start.21 = (f32[128,640]{1,0:T(8,128)S(1)}, f32[128,640]{1,0:T(8,128)S(1)}, u32[]{:S(2)}, u32[]{:S(2)}) collective-permute-start(f32[128,640]{1,0:T(8,128)S(1)} %upper_3.1.refs_0_), channel_id=1, source_target_pairs={{0,12},{4,8},{8,4},{12,0},{16,20},{20,16},{24,28},{28,24},{1,13},{... | collective-permute-start | bytes 983048 | tf_op jit(solution)/shard_map/ppermute | solution.py:27
  77.4 10.2 %collective-permute-start.22 = (f32[128,640]{1,0:T(8,128)S(1)}, f32[128,640]{1,0:T(8,128)S(1)}, u32[]{:S(2)}, u32[]{:S(2)}) collective-permute-start(f32[128,640]{1,0:T(8,128)S(1)} %collective-permute-done.19.refs_0_.refs_1_), channel_id=1, source_target_pairs={{0,12},{4,8},{8,4},{12,0},{16,20},{20,16},{24,28},{28,24},{1,13},{... | collective-permute-start | bytes 983048 | tf_op jit(solution)/shard_map/ppermute | solution.py:27
  77.4 21.5 %collective-permute-start.18 = (f32[128,640]{1,0:T(8,128)S(1)}, f32[128,640]{1,0:T(8,128)S(1)}, u32[]{:S(2)}, u32[]{:S(2)}) collective-permute-start(f32[128,640]{1,0:T(8,128)S(1)} %get-tuple-element.88), channel_id=1, source_target_pairs={{0,12},{4,8},{8,4},{12,0},{16,20},{20,16},{24,28},{28,24},{1,13},{... | collective-permute-start | bytes 983048 | tf_op jit(solution)/shard_map/ppermute | solution.py:27
  82.9 16.0 %collective-permute-start.20 = (f32[128,640]{1,0:T(8,128)S(1)}, f32[128,640]{1,0:T(8,128)S(1)}, u32[]{:S(2)}, u32[]{:S(2)}) collective-permute-start(f32[128,640]{1,0:T(8,128)S(1)} %leaf_4.1), channel_id=1, source_target_pairs={{0,12},{4,8},{8,4},{12,0},{16,20},{20,16},{24,28},{28,24},{1,13},{... | collective-permute-start | bytes 983048 | tf_op jit(solution)/shard_map/ppermute | solution.py:27
  93.2 3.0 %collective-permute-start.23 = (f32[32,512]{1,0:T(8,128)S(1)}, f32[32,512]{1,0:T(8,128)S(1)}, u32[]{:S(2)}, u32[]{:S(2)}) collective-permute-start(f32[32,512]{1,0:T(8,128)S(1)} %get-tuple-element.90), channel_id=1, source_target_pairs={{0,16},{16,0},{1,17},{17,1},{2,18},{18,2},{3,19},{19,3},{4,20},{20... | collective-permute-start | bytes 196616 | tf_op jit(solution)/shard_map/ppermute | solution.py:32
  96.2 9.6 %collective-permute-start.24 = (f32[32,512]{1,0:T(8,128)S(1)}, f32[32,512]{1,0:T(8,128)S(1)}, u32[]{:S(2)}, u32[]{:S(2)}) collective-permute-start(f32[32,512]{1,0:T(8,128)S(1)} %get-tuple-element.95), channel_id=1, source_target_pairs={{0,32},{32,0},{64,96},{96,64},{128,160},{160,128},{192,224},{224,1... | collective-permute-start | bytes 196616 | tf_op jit(solution)/shard_map/ppermute | solution.py:32

commit v5 on v4

--- a/solution.py
+++ b/solution.py
@@ -381,14 +381,18 @@
     got_both = hop(both_a, "x", True), hop(both_b, "y", True)
     got_near = hop(near_a, "x", True), hop(near_b, "y", True)
     own_a, far_a, own_b, far_b = ordered_samples(omega, a_matrix, False)
-    send = added((far_a, far_b), got_both, 0, 64, "add_sent")
+    send = added((far_a, far_b), got_both, 32, 32, "add_sent")
+    got_ahead = hop(send[0], "x", False), hop(send[1], "y", False)
+    send = added((far_a, far_b), got_both, 0, 32, "add_sent")
     got = hop(send[0], "x", False), hop(send[1], "y", False)
-    kept = added((own_a, own_b), got_near, 0, 64, "add_kept")
-
-    for rows, first in ((32, True), (16, False)):
-        send = added(kept, got, rows, rows, "add_sent")
-        kept = added(kept, got, 0, rows, "add_kept")
-        got = hop(send[0], "y", first), hop(send[1], "x", first)
+    send = added((own_a, own_b), got_near, 32, 32, "add_kept")
+    kept = added((own_a, own_b), got_near, 0, 32, "add_kept")
+    send = added(send, got_ahead, 0, 32, "add_sent")
+    kept = added(kept, got, 0, 32, "add_kept")
+    got = hop(send[0], "y", True), hop(send[1], "x", True)
+    send = added(kept, got, 16, 16, "add_sent")
+    kept = added(kept, got, 0, 16, "add_kept")
+    got = hop(send[0], "y", False), hop(send[1], "x", False)
     leaf_skeleton, parts = finished(leaf_order, (kept[0], got[0]), (kept[1], got[1]), orders)
 
     small = (32, K)

time: 107 us -> 103 us (0.963)
  waiting for transfers between devices: 52 us -> 42.5 us
  starting transfers between devices: 26.8 us -> 33 us
    ppermute x20 -> x22, waiting for transfers between devices: 49.6 us -> 40.1 us  [hop(): return lax.ppermute(block, ('core', axis), route)]
    ppermute x20 -> x22, starting transfers between devices: 15.6 us -> 23.8 us  [hop(): return lax.ppermute(block, ('core', axis), route)]
    ppermute x4, starting transfers between devices: 10.6 us -> 8.58 us  [swapped(): return lax.ppermute(block, axis, [(i, i ^ mask) for i in range(count)])]
  transfers between devices with their start and end apart: 25 -> 27, of which waited for: 20 -> 19; matrix products, arithmetic and copies ran while one was open for 0% -> 0% of each run, Pallas kernels for 17% -> 17%
where the time goes in v5:
time: 103 us
  waiting for transfers between devices  42.5 us (41%)
  starting transfers between devices  33 us (32%)
  Pallas kernels  26 us (25%)
    ppermute x22, waiting for transfers between devices, hop(): return lax.ppermute(block, ('core', axis), route)  40.1 us
    ppermute x22, starting transfers between devices, hop(): return lax.ppermute(block, ('core', axis), route)  23.8 us
    pallas_call x2, Pallas kernels, solve(): pl.pallas_call(functools.partial(solve_kernel, packed=packed), out_shape=...  12.4 us
    pallas_call x2, Pallas kernels, ordered_samples(): pl.pallas_call(functools.partial(ordered_kernel, sent=sent), grid=(LEAF /...  8.95 us
    ppermute x4, starting transfers between devices, swapped(): return lax.ppermute(block, axis, [(i, i ^ mask) for i in range(count)])  8.58 us
    pallas_call x8, Pallas kernels, call(): pl.pallas_call(kernel, in_specs=[VMEM] * len(inputs) + [ANY] * len(after)...  2.96 us
    ppermute x4, waiting for transfers between devices, swapped(): return lax.ppermute(block, axis, [(i, i ^ mask) for i in range(count)])  2.41 us
  transfers between devices with their start and end apart: 27, of which 19 were waited for; matrix products, arithmetic and copies ran while one was open for 0% of the time, Pallas kernels for 17%

profile of v5, /device:TPU:1, one launch (start us, length us, event | category | flops | bytes accessed | tf_op | source)
XLA Modules:
  0.0 103.2 jit_solution(2668755520344591780)
XLA Ops:
  0.6 6.1 %sent_samples.1 = (f32[64,2048]{1,0:T(8,128)}, f32[64,2048]{1,0:T(8,128)}, f32[64,2048]{1,0:T(8,128)}, f32[64,2048]{1,0:T(8,128)}) custom-call(bf16[1536,512]{1,0:T(8,128)(2,1)} %omega_ref.3, bf16[2048,1536]{1,0:T(8,128)(2,1)} %a_ref.3), custom_call_target="tpu_custom_call" | custom-call | flops 2013265920 | bytes 9961472 | tf_op jit(solution)/shard_map/sent_samples/pallas_call | solution.py:73
  6.8 3.3 %collective-permute-start.2 = (f32[64,2048]{1,0:T(8,128)}, f32[64,2048]{1,0:T(8,128)S(1)}, u32[]{:S(2)}, u32[]{:S(2)}) collective-permute-start(f32[64,2048]{1,0:T(8,128)} %get-tuple-element.61), channel_id=1, source_target_pairs={{0,1},{1,0},{2,3},{3,2},{16,19},{17,18},{18,17},{19,16},{4,5},{5,4... | collective-permute-start | bytes 1572872 | tf_op jit(solution)/shard_map/ppermute | solution.py:27
  10.1 2.7 %collective-permute-start.3 = (f32[64,2048]{1,0:T(8,128)}, f32[64,2048]{1,0:T(8,128)S(1)}, u32[]{:S(2)}, u32[]{:S(2)}) collective-permute-start(f32[64,2048]{1,0:T(8,128)} %get-tuple-element.63), channel_id=1, source_target_pairs={{0,4},{4,0},{8,12},{12,8},{16,28},{20,24},{24,20},{28,16},{1,5},{5... | collective-permute-start | bytes 1572872 | tf_op jit(solution)/shard_map/ppermute | solution.py:27
  12.8 0.2 collective-permute-start
  13.0 0.0 collective-permute-start.1
  13.0 2.8 %kept_samples.1 = (f32[64,2048]{1,0:T(8,128)S(1)}, f32[64,2048]{1,0:T(8,128)S(1)}, f32[64,2048]{1,0:T(8,128)S(1)}, f32[64,2048]{1,0:T(8,128)S(1)}) custom-call(bf16[1536,512]{1,0:T(8,128)(2,1)S(1)} %copy-done.1, bf16[2048,1536]{1,0:T(8,128)(2,1)S(1)} %copy-done), custom_call_target="tpu_custom_call" | custom-call | flops 2013265920 | bytes 9961472 | tf_op jit(solution)/shard_map/kept_samples/pallas_call | solution.py:73
  15.9 0.0 copy-start.2
  15.9 0.0 copy-start.3
  15.9 0.0 copy-start.4
  15.9 1.0 collective-permute-done.2.got_a
  16.9 2.7 %collective-permute-done.3.got_b = f32[64,2048]{1,0:T(8,128)S(1)} collective-permute-done((f32[64,2048]{1,0:T(8,128)}, f32[64,2048]{1,0:T(8,128)S(1)}, u32[]{:S(2)}, u32[]{:S(2)}) %collective-permute-start.3) | collective-permute-done | bytes 524320 | tf_op jit(solution)/shard_map/ppermute | solution.py:27
  19.6 0.1 add_sent.5
  19.7 0.1 collective-permute-start.6
  19.8 0.4 collective-permute-start.7
  20.2 0.1 add_sent.4
  20.2 1.5 %collective-permute-start.4 = (f32[32,2048]{1,0:T(8,128)S(1)}, f32[32,2048]{1,0:T(8,128)S(1)}, u32[]{:S(2)}, u32[]{:S(2)}) collective-permute-start(f32[32,2048]{1,0:T(8,128)S(1)} %get-tuple-element.64), channel_id=1, source_target_pairs={{0,3},{1,2},{2,1},{3,0},{16,17},{17,16},{18,19},{19,18},{4,7},{5,6... | collective-permute-start | bytes 786440 | tf_op jit(solution)/shard_map/ppermute | solution.py:27
  21.7 0.8 collective-permute-done.got_a
  22.5 1.5 %collective-permute-start.5 = (f32[32,2048]{1,0:T(8,128)S(1)}, f32[32,2048]{1,0:T(8,128)S(1)}, u32[]{:S(2)}, u32[]{:S(2)}) collective-permute-start(f32[32,2048]{1,0:T(8,128)S(1)} %get-tuple-element.66), channel_id=1, source_target_pairs={{0,12},{4,8},{8,4},{12,0},{16,20},{20,16},{24,28},{28,24},{1,13},{... | collective-permute-start | bytes 786440 | tf_op jit(solution)/shard_map/ppermute | solution.py:27
  24.0 1.5 %collective-permute-done.1.got_b = f32[64,2048]{1,0:T(8,128)S(1)} collective-permute-done((f32[64,2048]{1,0:T(8,128)}, f32[64,2048]{1,0:T(8,128)S(1)}, u32[]{:S(2)}, u32[]{:S(2)}) %collective-permute-start.1) | collective-permute-done | bytes 524320 | tf_op jit(solution)/shard_map/ppermute | solution.py:27
  25.5 0.1 add_kept.6
  25.6 1.9 %collective-permute-done.6.got_a = f32[32,2048]{1,0:T(8,128)S(1)} collective-permute-done((f32[32,2048]{1,0:T(8,128)S(1)}, f32[32,2048]{1,0:T(8,128)S(1)}, u32[]{:S(2)}, u32[]{:S(2)}) %collective-permute-start.6) | collective-permute-done | bytes 262176 | tf_op jit(solution)/shard_map/ppermute | solution.py:27
  27.4 0.1 collective-permute-done.7.got_b
  27.5 0.1 add_sent.6
  27.6 2.5 %collective-permute-start.8 = (f32[32,2048]{1,0:T(8,128)S(1)}, f32[32,2048]{1,0:T(8,128)S(1)}, u32[]{:S(2)}, u32[]{:S(2)}) collective-permute-start(f32[32,2048]{1,0:T(8,128)S(1)} %get-tuple-element.72), channel_id=1, source_target_pairs={{0,4},{4,0},{8,12},{12,8},{16,28},{20,24},{24,20},{28,16},{1,5},{5... | collective-permute-start | bytes 786440 | tf_op jit(solution)/shard_map/ppermute | solution.py:27
  30.1 1.7 %collective-permute-start.9 = (f32[32,2048]{1,0:T(8,128)S(1)}, f32[32,2048]{1,0:T(8,128)S(1)}, u32[]{:S(2)}, u32[]{:S(2)}) collective-permute-start(f32[32,2048]{1,0:T(8,128)S(1)} %get-tuple-element.74), channel_id=1, source_target_pairs={{0,1},{1,0},{2,3},{3,2},{16,19},{17,18},{18,17},{19,16},{4,5},{5,4... | collective-permute-start | bytes 786440 | tf_op jit(solution)/shard_map/ppermute | solution.py:27
  31.8 0.1 add_kept.4
  31.8 0.1 add_kept.5
  31.9 5.2 %collective-permute-done.8.got_a = f32[32,2048]{1,0:T(8,128)S(1)} collective-permute-done((f32[32,2048]{1,0:T(8,128)S(1)}, f32[32,2048]{1,0:T(8,128)S(1)}, u32[]{:S(2)}, u32[]{:S(2)}) %collective-permute-start.8) | collective-permute-done | bytes 262176 | tf_op jit(solution)/shard_map/ppermute | solution.py:27
  37.1 0.1 collective-permute-start.10
  37.2 0.1 collective-permute-start.11
  37.4 0.8 pivot_orders.1
  38.2 2.8 %collective-permute-done.10.refs_1_ = f32[16,2048]{1,0:T(8,128)S(1)} collective-permute-done((f32[16,2048]{1,0:T(8,128)S(1)}, f32[16,2048]{1,0:T(8,128)S(1)}, u32[]{:S(2)}, u32[]{:S(2)}) %collective-permute-start.10) | collective-permute-done | bytes 131104 | tf_op jit(solution)/shard_map/ppermute | solution.py:27
  41.0 0.1 collective-permute-done.11.refs_3_
  41.1 0.5 finish_samples.1
  41.6 4.1 %collective-permute-start.12 = (f32[32,512]{1,0:T(8,128)S(1)}, f32[32,512]{1,0:T(8,128)S(1)}, u32[]{:S(2)}, u32[]{:S(2)}) collective-permute-start(f32[32,512]{1,0:T(8,128)S(1)} %get-tuple-element.79.own.skeleton_ref), channel_id=1, source_target_pairs={{0,16},{16,0},{1,17},{17,1},{2,18},{18,2},{3,19},{19,3},{4,20},{20... | collective-permute-start | bytes 196616 | tf_op jit(solution)/shard_map/ppermute | solution.py:32
  45.8 0.9 collective-permute-done.12.sibling
  46.7 0.5 level_1.1
  47.1 1.8 %collective-permute-start.13 = (f32[32,512]{1,0:T(8,128)S(1)}, f32[32,512]{1,0:T(8,128)S(1)}, u32[]{:S(2)}, u32[]{:S(2)}) collective-permute-start(f32[32,512]{1,0:T(8,128)S(1)} %get-tuple-element.80.own.skeleton_1), channel_id=1, source_target_pairs={{0,32},{32,0},{64,96},{96,64},{128,160},{160,128},{192,224},{224,1... | collective-permute-start | bytes 196616 | tf_op jit(solution)/shard_map/ppermute | solution.py:32
  48.9 1.5 %leaf_redundant.1 = (f32[32,1536]{1,0:T(8,128)S(1)}, f32[32,1024]{1,0:T(8,128)S(1)}) custom-call(s32[1,2048]{1,0:T(1,128)S(1)} %get-tuple-element.81.order_ref, bf16[96,2048]{1,0:T(8,128)(2,1)S(1)} %get-tuple-element.82.parts_ref, f32[32,512]{1,0:T(8,128)S(1)} %get-tuple-element.79.own.skeleton_ref), custom_call_target="tpu_custom_call" | custom-call | flops 805306368 | bytes 1000000 | tf_op jit(solution)/shard_map/leaf_redundant/pallas_call | solution.py:241
  50.4 0.6 collective-permute-done.13.sibling
  51.0 0.5 level_2.1
  51.5 3.0 %collective-permute-start.15 = (f32[32,1536]{1,0:T(8,128)S(1)}, f32[32,1536]{1,0:T(8,128)S(1)}, u32[]{:S(2)}, u32[]{:S(2)}) collective-permute-start(f32[32,1536]{1,0:T(8,128)S(1)} %get-tuple-element.85.leaf), channel_id=1, source_target_pairs={{0,1},{1,0},{2,3},{3,2},{16,19},{17,18},{18,17},{19,16},{4,5},{5,4... | collective-permute-start | bytes 589832 | tf_op jit(solution)/shard_map/ppermute | solution.py:27
  54.4 0.7 collective-permute-start.14
  55.1 2.4 %collective-permute-done.15.got = f32[32,1536]{1,0:T(8,128)S(1)} collective-permute-done((f32[32,1536]{1,0:T(8,128)S(1)}, f32[32,1536]{1,0:T(8,128)S(1)}, u32[]{:S(2)}, u32[]{:S(2)}) %collective-permute-start.15) | collective-permute-done | bytes 196640 | tf_op jit(solution)/shard_map/ppermute | solution.py:27
  57.5 0.5 level_3.1
  58.0 0.8 collective-permute-start.17
  58.7 4.0 %collective-permute-done.17.got = f32[32,768]{1,0:T(8,128)S(1)} collective-permute-done((f32[32,768]{1,0:T(8,128)S(1)}, f32[32,768]{1,0:T(8,128)S(1)}, u32[]{:S(2)}, u32[]{:S(2)}) %collective-permute-start.17) | collective-permute-done | bytes 98336 | tf_op jit(solution)/shard_map/ppermute | solution.py:27
  62.7 2.8 %collective-permute-start.18 = (f32[64,640]{1,0:T(8,128)S(1)}, f32[64,640]{1,0:T(8,128)S(1)}, u32[]{:S(2)}, u32[]{:S(2)}) collective-permute-start(f32[64,640]{1,0:T(8,128)S(1)} %get-tuple-element.93.own), channel_id=1, source_target_pairs={{0,1},{1,0},{2,3},{3,2},{16,19},{17,18},{18,17},{19,16},{4,5},{5,4... | collective-permute-start | bytes 491528 | tf_op jit(solution)/shard_map/ppermute | solution.py:27
  65.5 3.6 %collective-permute-done.18.refs_0_.got = f32[64,640]{1,0:T(8,128)S(1)} collective-permute-done((f32[64,640]{1,0:T(8,128)S(1)}, f32[64,640]{1,0:T(8,128)S(1)}, u32[]{:S(2)}, u32[]{:S(2)}) %collective-permute-start.18) | collective-permute-done | bytes 163872 | tf_op jit(solution)/shard_map/ppermute | solution.py:27
  69.1 0.1 collective-permute-start.21
  69.2 1.9 %collective-permute-done.16.got = f32[64,1024]{1,0:T(8,128)S(1)} collective-permute-done((f32[64,1024]{1,0:T(8,128)S(1)}, f32[64,1024]{1,0:T(8,128)S(1)}, u32[]{:S(2)}, u32[]{:S(2)}) %collective-permute-start.16) | collective-permute-done | bytes 262176 | tf_op jit(solution)/shard_map/ppermute | solution.py:27
  71.1 0.1 leaf_3.1
  71.2 1.3 %collective-permute-start.19 = (f32[128,768]{1,0:T(8,128)S(1)}, f32[128,768]{1,0:T(8,128)S(1)}, u32[]{:S(2)}, u32[]{:S(2)}) collective-permute-start(f32[128,768]{1,0:T(8,128)S(1)} %get-tuple-element.95.refs_1_), channel_id=1, source_target_pairs={{0,4},{4,0},{8,12},{12,8},{16,28},{20,24},{24,20},{28,16},{1,5},{5... | collective-permute-start | bytes 1179656 | tf_op jit(solution)/shard_map/ppermute | solution.py:27
  72.5 2.9 %collective-permute-done.21.refs_0_.refs_1_ = f32[128,640]{1,0:T(8,128)S(1)} collective-permute-done((f32[128,640]{1,0:T(8,128)S(1)}, f32[128,640]{1,0:T(8,128)S(1)}, u32[]{:S(2)}, u32[]{:S(2)}) %collective-permute-start.21) | collective-permute-done | bytes 327712 | tf_op jit(solution)/shard_map/ppermute | solution.py:27
  75.4 1.5 %collective-permute-start.20 = (f32[128,640]{1,0:T(8,128)S(1)}, f32[128,640]{1,0:T(8,128)S(1)}, u32[]{:S(2)}, u32[]{:S(2)}) collective-permute-start(f32[128,640]{1,0:T(8,128)S(1)} %get-tuple-element.96), channel_id=1, source_target_pairs={{0,12},{4,8},{8,4},{12,0},{16,20},{20,16},{24,28},{28,24},{1,13},{... | collective-permute-start | bytes 983048 | tf_op jit(solution)/shard_map/ppermute | solution.py:27
  76.9 3.4 %collective-permute-done.19.got.refs_2_ = f32[128,768]{1,0:T(8,128)S(1)} collective-permute-done((f32[128,768]{1,0:T(8,128)S(1)}, f32[128,768]{1,0:T(8,128)S(1)}, u32[]{:S(2)}, u32[]{:S(2)}) %collective-permute-start.19) | collective-permute-done | bytes 393248 | tf_op jit(solution)/shard_map/ppermute | solution.py:27
  80.3 0.3 collective-permute-start.22
  80.7 5.8 %collective-permute-done.24.refs_3_ = f32[128,640]{1,0:T(8,128)S(1)} collective-permute-done((f32[128,640]{1,0:T(8,128)S(1)}, f32[128,640]{1,0:T(8,128)S(1)}, u32[]{:S(2)}, u32[]{:S(2)}) %collective-permute-start.24) | collective-permute-done | bytes 327712 | tf_op jit(solution)/shard_map/ppermute | solution.py:27
  86.4 5.6 %solve_upper.1 = (f32[32,512]{1,0:T(8,128)S(1)}, f32[8,128]{1,0:T(8,128)}) custom-call(f32[128,640]{1,0:T(8,128)S(1)} %upper_3.1.refs_0_, f32[128,640]{1,0:T(8,128)S(1)} %collective-permute-done.21.refs_0_.refs_1_, f32[128,640]{1,0:T(8,128)S(1)} %collective-permute-done.23.refs_2_, f32[128,640]{1,0:T(8,128)S(1)} %collective-permute-done.24.refs_3_), custom_call_target="tpu_custom_call" | custom-call | flops 5133828096 | bytes 1114112 | tf_op jit(solution)/shard_map/solve_upper/pallas_call | solution.py:158
  92.0 0.6 collective-permute-start.25
  92.7 0.9 collective-permute-done.25.refs_5_
  93.6 2.0 %collective-permute-start.26 = (f32[32,512]{1,0:T(8,128)S(1)}, f32[32,512]{1,0:T(8,128)S(1)}, u32[]{:S(2)}, u32[]{:S(2)}) collective-permute-start(f32[32,512]{1,0:T(8,128)S(1)} %get-tuple-element.103), channel_id=1, source_target_pairs={{0,32},{32,0},{64,96},{96,64},{128,160},{160,128},{192,224},{224,1... | collective-permute-start | bytes 196616 | tf_op jit(solution)/shard_map/ppermute | solution.py:32
  95.6 6.8 %solve_leaf.1 = (f32[96,512]{1,0:T(8,128)}, f32[8,128]{1,0:T(8,128)}) custom-call(f32[128,128]{1,0:T(8,128)S(1)} %get-tuple-element.94.refs_0_, f32[128,768]{1,0:T(8,128)S(1)} %get-tuple-element.95.refs_1_, f32[128,768]{1,0:T(8,128)S(1)} %collective-permute-done.19.got.refs_2_, f32[128,640]{1,0:T(8,128)S(1)} %collective-permute-done.20.refs_3_, ...), custom_call_target="tpu_custom_call" | custom-call | flops 5737807872 | bytes 1245184 | tf_op jit(solution)/shard_map/solve_leaf/pallas_call | solution.py:158
  102.5 0.7 maximum_bitcast_fusion
  (26 shorter events, 0.2 us)
Async XLA Ops:
  0.6 12.4 %copy-start.1 = (bf16[1536,512]{1,0:T(8,128)(2,1)S(1)}, bf16[1536,512]{1,0:T(8,128)(2,1)}, u32[]{:S(2)}) copy-start(bf16[1536,512]{1,0:T(8,128)(2,1)} %omega_ref.3) | copy-start | bytes 4718596
  0.6 12.4 %copy-start = (bf16[2048,1536]{1,0:T(8,128)(2,1)S(1)}, bf16[2048,1536]{1,0:T(8,128)(2,1)}, u32[]{:S(2)}) copy-start(bf16[2048,1536]{1,0:T(8,128)(2,1)} %a_ref.3) | copy-start | bytes 18874372
  6.8 10.1 %collective-permute-start.2 = (f32[64,2048]{1,0:T(8,128)}, f32[64,2048]{1,0:T(8,128)S(1)}, u32[]{:S(2)}, u32[]{:S(2)}) collective-permute-start(f32[64,2048]{1,0:T(8,128)} %get-tuple-element.61), channel_id=1, source_target_pairs={{0,1},{1,0},{2,3},{3,2},{16,19},{17,18},{18,17},{19,16},{4,5},{5,4... | collective-permute-start | bytes 1572872 | tf_op jit(solution)/shard_map/ppermute | solution.py:27
  10.1 9.5 %collective-permute-start.3 = (f32[64,2048]{1,0:T(8,128)}, f32[64,2048]{1,0:T(8,128)S(1)}, u32[]{:S(2)}, u32[]{:S(2)}) collective-permute-start(f32[64,2048]{1,0:T(8,128)} %get-tuple-element.63), channel_id=1, source_target_pairs={{0,4},{4,0},{8,12},{12,8},{16,28},{20,24},{24,20},{28,16},{1,5},{5... | collective-permute-start | bytes 1572872 | tf_op jit(solution)/shard_map/ppermute | solution.py:27
  12.8 9.7 %collective-permute-start = (f32[64,2048]{1,0:T(8,128)}, f32[64,2048]{1,0:T(8,128)S(1)}, u32[]{:S(2)}, u32[]{:S(2)}) collective-permute-start(f32[64,2048]{1,0:T(8,128)} %get-tuple-element.56), channel_id=1, source_target_pairs={{0,1},{1,0},{2,3},{3,2},{16,19},{17,18},{18,17},{19,16},{4,5},{5,4... | collective-permute-start | bytes 1572872 | tf_op jit(solution)/shard_map/ppermute | solution.py:27
  13.0 12.5 %collective-permute-start.1 = (f32[64,2048]{1,0:T(8,128)}, f32[64,2048]{1,0:T(8,128)S(1)}, u32[]{:S(2)}, u32[]{:S(2)}) collective-permute-start(f32[64,2048]{1,0:T(8,128)} %get-tuple-element.58), channel_id=1, source_target_pairs={{0,4},{4,0},{8,12},{12,8},{16,28},{20,24},{24,20},{28,16},{1,5},{5... | collective-permute-start | bytes 1572872 | tf_op jit(solution)/shard_map/ppermute | solution.py:27
  15.9 21.5 %copy-start.2 = (s32[3,8,1024]{2,1,0:T(8,128)S(1)}, s32[3,8,1024]{2,1,0:T(8,128)}, u32[]{:S(2)}) copy-start(s32[3,8,1024]{2,1,0:T(8,128)} %upper_ref.1) | copy-start | bytes 294916
  15.9 21.5 %copy-start.3 = (s32[1,2048]{1,0:T(1,128)S(1)}, s32[1,2048]{1,0:T(1,128)}, u32[]{:S(2)}) copy-start(s32[1,2048]{1,0:T(1,128)} %leaf_ref.1) | copy-start | bytes 24580
  15.9 21.5 %copy-start.4 = (s32[4,16]{1,0:T(4,128)S(1)}, s32[4,16]{1,0:T(4,128)}, u32[]{:S(2)}) copy-start(s32[4,16]{1,0:T(4,128)} %ranks_ref.1) | copy-start | bytes 772
  19.7 7.8 %collective-permute-start.6 = (f32[32,2048]{1,0:T(8,128)S(1)}, f32[32,2048]{1,0:T(8,128)S(1)}, u32[]{:S(2)}, u32[]{:S(2)}) collective-permute-start(f32[32,2048]{1,0:T(8,128)S(1)} %get-tuple-element.69), channel_id=1, source_target_pairs={{0,3},{1,2},{2,1},{3,0},{16,17},{17,16},{18,19},{19,18},{4,7},{5,6... | collective-permute-start | bytes 786440 | tf_op jit(solution)/shard_map/ppermute | solution.py:27
  19.8 7.7 %collective-permute-start.7 = (f32[32,2048]{1,0:T(8,128)S(1)}, f32[32,2048]{1,0:T(8,128)S(1)}, u32[]{:S(2)}, u32[]{:S(2)}) collective-permute-start(f32[32,2048]{1,0:T(8,128)S(1)} %get-tuple-element.71), channel_id=1, source_target_pairs={{0,12},{4,8},{8,4},{12,0},{16,20},{20,16},{24,28},{28,24},{1,13},{... | collective-permute-start | bytes 786440 | tf_op jit(solution)/shard_map/ppermute | solution.py:27
  20.2 11.6 %collective-permute-start.4 = (f32[32,2048]{1,0:T(8,128)S(1)}, f32[32,2048]{1,0:T(8,128)S(1)}, u32[]{:S(2)}, u32[]{:S(2)}) collective-permute-start(f32[32,2048]{1,0:T(8,128)S(1)} %get-tuple-element.64), channel_id=1, source_target_pairs={{0,3},{1,2},{2,1},{3,0},{16,17},{17,16},{18,19},{19,18},{4,7},{5,6... | collective-permute-start | bytes 786440 | tf_op jit(solution)/shard_map/ppermute | solution.py:27
  22.5 9.3 %collective-permute-start.5 = (f32[32,2048]{1,0:T(8,128)S(1)}, f32[32,2048]{1,0:T(8,128)S(1)}, u32[]{:S(2)}, u32[]{:S(2)}) collective-permute-start(f32[32,2048]{1,0:T(8,128)S(1)} %get-tuple-element.66), channel_id=1, source_target_pairs={{0,12},{4,8},{8,4},{12,0},{16,20},{20,16},{24,28},{28,24},{1,13},{... | collective-permute-start | bytes 786440 | tf_op jit(solution)/shard_map/ppermute | solution.py:27
  27.6 9.5 %collective-permute-start.8 = (f32[32,2048]{1,0:T(8,128)S(1)}, f32[32,2048]{1,0:T(8,128)S(1)}, u32[]{:S(2)}, u32[]{:S(2)}) collective-permute-start(f32[32,2048]{1,0:T(8,128)S(1)} %get-tuple-element.72), channel_id=1, source_target_pairs={{0,4},{4,0},{8,12},{12,8},{16,28},{20,24},{24,20},{28,16},{1,5},{5... | collective-permute-start | bytes 786440 | tf_op jit(solution)/shard_map/ppermute | solution.py:27
  30.1 7.0 %collective-permute-start.9 = (f32[32,2048]{1,0:T(8,128)S(1)}, f32[32,2048]{1,0:T(8,128)S(1)}, u32[]{:S(2)}, u32[]{:S(2)}) collective-permute-start(f32[32,2048]{1,0:T(8,128)S(1)} %get-tuple-element.74), channel_id=1, source_target_pairs={{0,1},{1,0},{2,3},{3,2},{16,19},{17,18},{18,17},{19,16},{4,5},{5,4... | collective-permute-start | bytes 786440 | tf_op jit(solution)/shard_map/ppermute | solution.py:27
  37.1 3.9 %collective-permute-start.10 = (f32[16,2048]{1,0:T(8,128)S(1)}, f32[16,2048]{1,0:T(8,128)S(1)}, u32[]{:S(2)}, u32[]{:S(2)}) collective-permute-start(f32[16,2048]{1,0:T(8,128)S(1)} %get-tuple-element.76), channel_id=1, source_target_pairs={{0,12},{4,8},{8,4},{12,0},{16,20},{20,16},{24,28},{28,24},{1,13},{... | collective-permute-start | bytes 393224 | tf_op jit(solution)/shard_map/ppermute | solution.py:27
  37.2 3.9 %collective-permute-start.11 = (f32[16,2048]{1,0:T(8,128)S(1)}, f32[16,2048]{1,0:T(8,128)S(1)}, u32[]{:S(2)}, u32[]{:S(2)}) collective-permute-start(f32[16,2048]{1,0:T(8,128)S(1)} %get-tuple-element.78), channel_id=1, source_target_pairs={{0,3},{1,2},{2,1},{3,0},{16,17},{17,16},{18,19},{19,18},{4,7},{5,6... | collective-permute-start | bytes 393224 | tf_op jit(solution)/shard_map/ppermute | solution.py:27
  41.6 5.0 %collective-permute-start.12 = (f32[32,512]{1,0:T(8,128)S(1)}, f32[32,512]{1,0:T(8,128)S(1)}, u32[]{:S(2)}, u32[]{:S(2)}) collective-permute-start(f32[32,512]{1,0:T(8,128)S(1)} %get-tuple-element.79.own.skeleton_ref), channel_id=1, source_target_pairs={{0,16},{16,0},{1,17},{17,1},{2,18},{18,2},{3,19},{19,3},{4,20},{20... | collective-permute-start | bytes 196616 | tf_op jit(solution)/shard_map/ppermute | solution.py:32
  47.1 3.9 %collective-permute-start.13 = (f32[32,512]{1,0:T(8,128)S(1)}, f32[32,512]{1,0:T(8,128)S(1)}, u32[]{:S(2)}, u32[]{:S(2)}) collective-permute-start(f32[32,512]{1,0:T(8,128)S(1)} %get-tuple-element.80.own.skeleton_1), channel_id=1, source_target_pairs={{0,32},{32,0},{64,96},{96,64},{128,160},{160,128},{192,224},{224,1... | collective-permute-start | bytes 196616 | tf_op jit(solution)/shard_map/ppermute | solution.py:32
  51.5 6.0 %collective-permute-start.15 = (f32[32,1536]{1,0:T(8,128)S(1)}, f32[32,1536]{1,0:T(8,128)S(1)}, u32[]{:S(2)}, u32[]{:S(2)}) collective-permute-start(f32[32,1536]{1,0:T(8,128)S(1)} %get-tuple-element.85.leaf), channel_id=1, source_target_pairs={{0,1},{1,0},{2,3},{3,2},{16,19},{17,18},{18,17},{19,16},{4,5},{5,4... | collective-permute-start | bytes 589832 | tf_op jit(solution)/shard_map/ppermute | solution.py:27
  54.4 0.7 collective-permute-start.14
  58.0 4.7 %collective-permute-start.17 = (f32[32,768]{1,0:T(8,128)S(1)}, f32[32,768]{1,0:T(8,128)S(1)}, u32[]{:S(2)}, u32[]{:S(2)}) collective-permute-start(f32[32,768]{1,0:T(8,128)S(1)} %get-tuple-element.91.own), channel_id=1, source_target_pairs={{0,4},{4,0},{8,12},{12,8},{16,28},{20,24},{24,20},{28,16},{1,5},{5... | collective-permute-start | bytes 294920 | tf_op jit(solution)/shard_map/ppermute | solution.py:27
  62.7 6.4 %collective-permute-start.18 = (f32[64,640]{1,0:T(8,128)S(1)}, f32[64,640]{1,0:T(8,128)S(1)}, u32[]{:S(2)}, u32[]{:S(2)}) collective-permute-start(f32[64,640]{1,0:T(8,128)S(1)} %get-tuple-element.93.own), channel_id=1, source_target_pairs={{0,1},{1,0},{2,3},{3,2},{16,19},{17,18},{18,17},{19,16},{4,5},{5,4... | collective-permute-start | bytes 491528 | tf_op jit(solution)/shard_map/ppermute | solution.py:27
  65.5 5.6 %collective-permute-start.16 = (f32[64,1024]{1,0:T(8,128)S(1)}, f32[64,1024]{1,0:T(8,128)S(1)}, u32[]{:S(2)}, u32[]{:S(2)}) collective-permute-start(f32[64,1024]{1,0:T(8,128)S(1)} %get-tuple-element.89.own), channel_id=1, source_target_pairs={{0,3},{1,2},{2,1},{3,0},{16,17},{17,16},{18,19},{19,18},{4,7},{5,6... | collective-permute-start | bytes 786440 | tf_op jit(solution)/shard_map/ppermute | solution.py:27
  69.1 6.3 %collective-permute-start.21 = (f32[128,640]{1,0:T(8,128)S(1)}, f32[128,640]{1,0:T(8,128)S(1)}, u32[]{:S(2)}, u32[]{:S(2)}) collective-permute-start(f32[128,640]{1,0:T(8,128)S(1)} %upper_3.1.refs_0_), channel_id=1, source_target_pairs={{0,3},{1,2},{2,1},{3,0},{16,17},{17,16},{18,19},{19,18},{4,7},{5,6... | collective-permute-start | bytes 983048 | tf_op jit(solution)/shard_map/ppermute | solution.py:27
  71.2 9.1 %collective-permute-start.19 = (f32[128,768]{1,0:T(8,128)S(1)}, f32[128,768]{1,0:T(8,128)S(1)}, u32[]{:S(2)}, u32[]{:S(2)}) collective-permute-start(f32[128,768]{1,0:T(8,128)S(1)} %get-tuple-element.95.refs_1_), channel_id=1, source_target_pairs={{0,4},{4,0},{8,12},{12,8},{16,28},{20,24},{24,20},{28,16},{1,5},{5... | collective-permute-start | bytes 1179656 | tf_op jit(solution)/shard_map/ppermute | solution.py:27
  72.5 8.2 %collective-permute-start.23 = (f32[128,640]{1,0:T(8,128)S(1)}, f32[128,640]{1,0:T(8,128)S(1)}, u32[]{:S(2)}, u32[]{:S(2)}) collective-permute-start(f32[128,640]{1,0:T(8,128)S(1)} %upper_3.1.refs_0_), channel_id=1, source_target_pairs={{0,12},{4,8},{8,4},{12,0},{16,20},{20,16},{24,28},{28,24},{1,13},{... | collective-permute-start | bytes 983048 | tf_op jit(solution)/shard_map/ppermute | solution.py:27
  75.4 11.0 %collective-permute-start.24 = (f32[128,640]{1,0:T(8,128)S(1)}, f32[128,640]{1,0:T(8,128)S(1)}, u32[]{:S(2)}, u32[]{:S(2)}) collective-permute-start(f32[128,640]{1,0:T(8,128)S(1)} %collective-permute-done.21.refs_0_.refs_1_), channel_id=1, source_target_pairs={{0,12},{4,8},{8,4},{12,0},{16,20},{20,16},{24,28},{28,24},{1,13},{... | collective-permute-start | bytes 983048 | tf_op jit(solution)/shard_map/ppermute | solution.py:27
  75.4 20.2 %collective-permute-start.20 = (f32[128,640]{1,0:T(8,128)S(1)}, f32[128,640]{1,0:T(8,128)S(1)}, u32[]{:S(2)}, u32[]{:S(2)}) collective-permute-start(f32[128,640]{1,0:T(8,128)S(1)} %get-tuple-element.96), channel_id=1, source_target_pairs={{0,12},{4,8},{8,4},{12,0},{16,20},{20,16},{24,28},{28,24},{1,13},{... | collective-permute-start | bytes 983048 | tf_op jit(solution)/shard_map/ppermute | solution.py:27
  80.3 15.3 %collective-permute-start.22 = (f32[128,640]{1,0:T(8,128)S(1)}, f32[128,640]{1,0:T(8,128)S(1)}, u32[]{:S(2)}, u32[]{:S(2)}) collective-permute-start(f32[128,640]{1,0:T(8,128)S(1)} %leaf_4.1), channel_id=1, source_target_pairs={{0,12},{4,8},{8,4},{12,0},{16,20},{20,16},{24,28},{28,24},{1,13},{... | collective-permute-start | bytes 983048 | tf_op jit(solution)/shard_map/ppermute | solution.py:27
  92.0 1.5 %collective-permute-start.25 = (f32[32,512]{1,0:T(8,128)S(1)}, f32[32,512]{1,0:T(8,128)S(1)}, u32[]{:S(2)}, u32[]{:S(2)}) collective-permute-start(f32[32,512]{1,0:T(8,128)S(1)} %get-tuple-element.98), channel_id=1, source_target_pairs={{0,16},{16,0},{1,17},{17,1},{2,18},{18,2},{3,19},{19,3},{4,20},{20... | collective-permute-start | bytes 196616 | tf_op jit(solution)/shard_map/ppermute | solution.py:32
  93.6 8.9 %collective-permute-start.26 = (f32[32,512]{1,0:T(8,128)S(1)}, f32[32,512]{1,0:T(8,128)S(1)}, u32[]{:S(2)}, u32[]{:S(2)}) collective-permute-start(f32[32,512]{1,0:T(8,128)S(1)} %get-tuple-element.103), channel_id=1, source_target_pairs={{0,32},{32,0},{64,96},{96,64},{128,160},{160,128},{192,224},{224,1... | collective-permute-start | bytes 196616 | tf_op jit(solution)/shard_map/ppermute | solution.py:32

commit v6 on v5

--- a/solution.py
+++ b/solution.py
@@ -33,7 +33,7 @@
 
 
 def ordered_kernel(omega_ref, a_ref, *refs, sent):
-    lhs_ref = refs[4]
+    outs, lhs_ref = refs[:-1], refs[-1]
 
     @pl.when(pl.program_id(0) == 0)
     def _():
@@ -62,14 +62,17 @@
     rows = lax.dot_general(
         lhs_ref[...], a_ref[...], (((1,), (1,)), ((), ())), preferred_element_type=F32
     )
-    for i in range(4):
-        refs[i][...] = rows[64 * i : 64 * i + 64]
+    low = 0
+    for out_ref in outs:
+        size = out_ref.shape[0]
+        out_ref[...] = rows[low : low + size]
+        low += size
 
 
 def ordered_samples(omega, a_matrix, sent):
+    sizes = (64, 32, 32) * 2 if sent else (64, 64) * 2
     depth = a_matrix.shape[1]
     block = 1024
-    out = jax.ShapeDtypeStruct((64, LEAF), F32)
     return pl.pallas_call(
         functools.partial(ordered_kernel, sent=sent),
         grid=(LEAF // block,),
@@ -77,9 +80,9 @@
             pl.BlockSpec((depth, S), lambda i: (0, 0)),
             pl.BlockSpec((block, depth), lambda i: (i, 0)),
         ],
-        out_specs=[pl.BlockSpec((64, block), lambda i: (0, i))] * 4,
+        out_specs=[pl.BlockSpec((size, block), lambda i: (0, i)) for size in sizes],
         scratch_shapes=[pltpu.VMEM((256, depth), BF16)],
-        out_shape=[out] * 4,
+        out_shape=[jax.ShapeDtypeStruct((size, LEAF), F32) for size in sizes],
         compiler_params=pltpu.CompilerParams(vmem_limit_bytes=(56 if sent else 16) * 2**20),
         cost_estimate=pl.CostEstimate(
             flops=2 * 256 * depth * (LEAF + S),
@@ -171,8 +174,9 @@
 def add_kernel(kept_a, got_a, kept_b, got_b, out_a, out_b, *, first):
     rows = out_a.shape[0]
     part = slice(first, first + rows)
-    out_a[...] = kept_a[part] + got_a[part]
-    out_b[...] = kept_b[part] + got_b[part]
+    got_part = part if got_a.shape[0] > rows else slice(0, rows)
+    out_a[...] = kept_a[part] + got_a[got_part]
+    out_b[...] = kept_b[part] + got_b[got_part]
 
 
 def added(kept, got, first, rows, name):
@@ -377,13 +381,14 @@
     z, core, y, x = (lax.axis_index(name) for name in ("z", "core", "y", "x"))
     leaf_order, leaf_rest, *orders = pivot_orders(ranks, leaf_pivots, upper_pivots)
 
-    near_a, both_a, near_b, both_b = ordered_samples(omega, a_matrix, True)
-    got_both = hop(both_a, "x", True), hop(both_b, "y", True)
+    near_a, low_a, high_a, near_b, low_b, high_b = ordered_samples(omega, a_matrix, True)
+    got_high = hop(high_a, "x", True), hop(high_b, "y", True)
+    got_low = hop(low_a, "x", True), hop(low_b, "y", True)
     got_near = hop(near_a, "x", True), hop(near_b, "y", True)
     own_a, far_a, own_b, far_b = ordered_samples(omega, a_matrix, False)
-    send = added((far_a, far_b), got_both, 32, 32, "add_sent")
+    send = added((far_a, far_b), got_high, 32, 32, "add_sent")
     got_ahead = hop(send[0], "x", False), hop(send[1], "y", False)
-    send = added((far_a, far_b), got_both, 0, 32, "add_sent")
+    send = added((far_a, far_b), got_low, 0, 32, "add_sent")
     got = hop(send[0], "x", False), hop(send[1], "y", False)
     send = added((own_a, own_b), got_near, 32, 32, "add_kept")
     kept = added((own_a, own_b), got_near, 0, 32, "add_kept")

time: 103 us -> 112 us (1.087)
  waiting for transfers between devices: 42.5 us -> 49.4 us
  starting transfers between devices: 33 us -> 34.8 us
    ppermute x22 -> x24, waiting for transfers between devices: 40.1 us -> 46.9 us  [hop(): return lax.ppermute(block, ('core', axis), route)]
    ppermute x4, starting transfers between devices: 8.58 us -> 13.7 us  [swapped(): return lax.ppermute(block, axis, [(i, i ^ mask) for i in range(count)])]
    ppermute x22 -> x24, starting transfers between devices: 23.8 us -> 20.5 us  [hop(): return lax.ppermute(block, ('core', axis), route)]
  transfers between devices with their start and end apart: 27 -> 29, of which waited for: 19 -> 16; matrix products, arithmetic and copies ran while one was open for 0% -> 0% of each run, Pallas kernels for 17% -> 16%
where the time goes in v6:
time: 112 us
  waiting for transfers between devices  49.4 us (44%)
  starting transfers between devices  34.8 us (31%)
  Pallas kernels  26 us (23%)
    ppermute x24, waiting for transfers between devices, hop(): return lax.ppermute(block, ('core', axis), route)  46.9 us
    ppermute x24, starting transfers between devices, hop(): return lax.ppermute(block, ('core', axis), route)  20.5 us
    ppermute x4, starting transfers between devices, swapped(): return lax.ppermute(block, axis, [(i, i ^ mask) for i in range(count)])  13.7 us
    pallas_call x2, Pallas kernels, solve(): pl.pallas_call(functools.partial(solve_kernel, packed=packed), out_shape=...  12.4 us
    pallas_call x2, Pallas kernels, ordered_samples(): pl.pallas_call(functools.partial(ordered_kernel, sent=sent), grid=(LEAF /...  8.93 us
    pallas_call x8, Pallas kernels, call(): pl.pallas_call(kernel, in_specs=[VMEM] * len(inputs) + [ANY] * len(after)...  2.95 us
    ppermute x4, waiting for transfers between devices, swapped(): return lax.ppermute(block, axis, [(i, i ^ mask) for i in range(count)])  2.43 us
  transfers between devices with their start and end apart: 29, of which 16 were waited for; matrix products, arithmetic and copies ran while one was open for 0% of the time, Pallas kernels for 16%

profile of v6, /device:TPU:1, one launch (start us, length us, event | category | flops | bytes accessed | tf_op | source)
XLA Modules:
  0.0 111.9 jit_solution(9719024878061035269)
XLA Ops:
  0.6 6.1 %sent_samples.1 = (f32[64,2048]{1,0:T(8,128)}, f32[32,2048]{1,0:T(8,128)}, f32[32,2048]{1,0:T(8,128)}, f32[64,2048]{1,0:T(8,128)}, f32[32,2048]{1,0:T(8,128)}, /*index=5*/f32[32,2048]{1,0:T(8,128)}) custom-call(bf16[1536,512]{1,0:T(8,128)(2,1)} %omega_ref.3, bf16[2048,1536]{1,0:T(8,128)(2,1)} %a_ref.3), custom_call_target="tpu_custom_call" | custom-call | flops 2013265920 | bytes 9961472 | tf_op jit(solution)/shard_map/sent_samples/pallas_call | solution.py:76
  6.8 3.3 %collective-permute-start.6 = (f32[32,2048]{1,0:T(8,128)}, f32[32,2048]{1,0:T(8,128)S(1)}, u32[]{:S(2)}, u32[]{:S(2)}) collective-permute-start(f32[32,2048]{1,0:T(8,128)} %get-tuple-element.71), channel_id=1, source_target_pairs={{0,1},{1,0},{2,3},{3,2},{16,19},{17,18},{18,17},{19,16},{4,5},{5,4... | collective-permute-start | bytes 786440 | tf_op jit(solution)/shard_map/ppermute | solution.py:27
  10.1 2.7 %collective-permute-start.7 = (f32[32,2048]{1,0:T(8,128)}, f32[32,2048]{1,0:T(8,128)S(1)}, u32[]{:S(2)}, u32[]{:S(2)}) collective-permute-start(f32[32,2048]{1,0:T(8,128)} %get-tuple-element.72), channel_id=1, source_target_pairs={{0,4},{4,0},{8,12},{12,8},{16,28},{20,24},{24,20},{28,16},{1,5},{5... | collective-permute-start | bytes 786440 | tf_op jit(solution)/shard_map/ppermute | solution.py:27
  12.8 0.2 collective-permute-start
  13.0 0.0 collective-permute-start.1
  13.0 2.5 %collective-permute-start.2 = (f32[32,2048]{1,0:T(8,128)}, f32[32,2048]{1,0:T(8,128)S(1)}, u32[]{:S(2)}, u32[]{:S(2)}) collective-permute-start(f32[32,2048]{1,0:T(8,128)} %get-tuple-element.63), channel_id=1, source_target_pairs={{0,1},{1,0},{2,3},{3,2},{16,19},{17,18},{18,17},{19,16},{4,5},{5,4... | collective-permute-start | bytes 786440 | tf_op jit(solution)/shard_map/ppermute | solution.py:27
  15.5 2.7 %collective-permute-start.3 = (f32[32,2048]{1,0:T(8,128)}, f32[32,2048]{1,0:T(8,128)S(1)}, u32[]{:S(2)}, u32[]{:S(2)}) collective-permute-start(f32[32,2048]{1,0:T(8,128)} %get-tuple-element.65), channel_id=1, source_target_pairs={{0,4},{4,0},{8,12},{12,8},{16,28},{20,24},{24,20},{28,16},{1,5},{5... | collective-permute-start | bytes 786440 | tf_op jit(solution)/shard_map/ppermute | solution.py:27
  18.2 2.8 %kept_samples.1 = (f32[64,2048]{1,0:T(8,128)S(1)}, f32[64,2048]{1,0:T(8,128)S(1)}, f32[64,2048]{1,0:T(8,128)S(1)}, f32[64,2048]{1,0:T(8,128)S(1)}) custom-call(bf16[1536,512]{1,0:T(8,128)(2,1)S(1)} %copy-done.1, bf16[2048,1536]{1,0:T(8,128)(2,1)S(1)} %copy-done), custom_call_target="tpu_custom_call" | custom-call | flops 2013265920 | bytes 9961472 | tf_op jit(solution)/shard_map/kept_samples/pallas_call | solution.py:76
  21.0 0.0 copy-start.2
  21.0 0.0 copy-start.3
  21.0 0.0 copy-start.4
  21.0 0.1 add_sent.5
  21.1 0.1 collective-permute-start.8
  21.2 5.5 %collective-permute-done.2.got_a = f32[32,2048]{1,0:T(8,128)S(1)} collective-permute-done((f32[32,2048]{1,0:T(8,128)}, f32[32,2048]{1,0:T(8,128)S(1)}, u32[]{:S(2)}, u32[]{:S(2)}) %collective-permute-start.2) | collective-permute-done | bytes 262176 | tf_op jit(solution)/shard_map/ppermute | solution.py:27
  26.7 0.1 add_sent.4
  26.8 0.1 collective-permute-start.4
  26.9 1.5 %collective-permute-start.5 = (f32[32,2048]{1,0:T(8,128)S(1)}, f32[32,2048]{1,0:T(8,128)S(1)}, u32[]{:S(2)}, u32[]{:S(2)}) collective-permute-start(f32[32,2048]{1,0:T(8,128)S(1)} %get-tuple-element.68), channel_id=1, source_target_pairs={{0,12},{4,8},{8,4},{12,0},{16,20},{20,16},{24,28},{28,24},{1,13},{... | collective-permute-start | bytes 786440 | tf_op jit(solution)/shard_map/ppermute | solution.py:27
  28.4 0.1 add_kept.6
  28.5 3.7 %collective-permute-done.9.got_b = f32[32,2048]{1,0:T(8,128)S(1)} collective-permute-done((f32[32,2048]{1,0:T(8,128)S(1)}, f32[32,2048]{1,0:T(8,128)S(1)}, u32[]{:S(2)}, u32[]{:S(2)}) %collective-permute-start.9) | collective-permute-done | bytes 262176 | tf_op jit(solution)/shard_map/ppermute | solution.py:27
  32.2 0.1 add_sent.6
  32.3 0.1 collective-permute-start.10
  32.4 0.9 collective-permute-start.11
  33.3 0.1 add_kept.4
  33.3 1.7 %collective-permute-done.5.got_b = f32[32,2048]{1,0:T(8,128)S(1)} collective-permute-done((f32[32,2048]{1,0:T(8,128)S(1)}, f32[32,2048]{1,0:T(8,128)S(1)}, u32[]{:S(2)}, u32[]{:S(2)}) %collective-permute-start.5) | collective-permute-done | bytes 262176 | tf_op jit(solution)/shard_map/ppermute | solution.py:27
  35.0 0.1 add_kept.5
  35.1 6.7 %collective-permute-done.10.got_a = f32[32,2048]{1,0:T(8,128)S(1)} collective-permute-done((f32[32,2048]{1,0:T(8,128)S(1)}, f32[32,2048]{1,0:T(8,128)S(1)}, u32[]{:S(2)}, u32[]{:S(2)}) %collective-permute-start.10) | collective-permute-done | bytes 262176 | tf_op jit(solution)/shard_map/ppermute | solution.py:27
  41.8 0.1 collective-permute-start.12
  41.9 0.1 collective-permute-start.13
  42.0 0.8 pivot_orders.1
  42.8 2.8 %collective-permute-done.12.refs_1_ = f32[16,2048]{1,0:T(8,128)S(1)} collective-permute-done((f32[16,2048]{1,0:T(8,128)S(1)}, f32[16,2048]{1,0:T(8,128)S(1)}, u32[]{:S(2)}, u32[]{:S(2)}) %collective-permute-start.12) | collective-permute-done | bytes 131104 | tf_op jit(solution)/shard_map/ppermute | solution.py:27
  45.7 0.1 collective-permute-done.13.refs_3_
  45.8 0.5 finish_samples.1
  46.3 6.6 %collective-permute-start.14 = (f32[32,512]{1,0:T(8,128)S(1)}, f32[32,512]{1,0:T(8,128)S(1)}, u32[]{:S(2)}, u32[]{:S(2)}) collective-permute-start(f32[32,512]{1,0:T(8,128)S(1)} %get-tuple-element.83.own.skeleton_ref), channel_id=1, source_target_pairs={{0,16},{16,0},{1,17},{17,1},{2,18},{18,2},{3,19},{19,3},{4,20},{20... | collective-permute-start | bytes 196616 | tf_op jit(solution)/shard_map/ppermute | solution.py:32
  52.8 0.9 collective-permute-done.14.sibling
  53.8 0.5 level_1.1
  54.2 1.8 %collective-permute-start.15 = (f32[32,512]{1,0:T(8,128)S(1)}, f32[32,512]{1,0:T(8,128)S(1)}, u32[]{:S(2)}, u32[]{:S(2)}) collective-permute-start(f32[32,512]{1,0:T(8,128)S(1)} %get-tuple-element.84.own.skeleton_1), channel_id=1, source_target_pairs={{0,32},{32,0},{64,96},{96,64},{128,160},{160,128},{192,224},{224,1... | collective-permute-start | bytes 196616 | tf_op jit(solution)/shard_map/ppermute | solution.py:32
  56.0 1.5 %leaf_redundant.1 = (f32[32,1536]{1,0:T(8,128)S(1)}, f32[32,1024]{1,0:T(8,128)S(1)}) custom-call(s32[1,2048]{1,0:T(1,128)S(1)} %get-tuple-element.85.order_ref, bf16[96,2048]{1,0:T(8,128)(2,1)S(1)} %get-tuple-element.86.parts_ref, f32[32,512]{1,0:T(8,128)S(1)} %get-tuple-element.83.own.skeleton_ref), custom_call_target="tpu_custom_call" | custom-call | flops 805306368 | bytes 1000000 | tf_op jit(solution)/shard_map/leaf_redundant/pallas_call | solution.py:245
  57.5 0.6 collective-permute-done.15.sibling
  58.1 0.5 level_2.1
  58.6 1.8 %collective-permute-start.17 = (f32[32,1536]{1,0:T(8,128)S(1)}, f32[32,1536]{1,0:T(8,128)S(1)}, u32[]{:S(2)}, u32[]{:S(2)}) collective-permute-start(f32[32,1536]{1,0:T(8,128)S(1)} %get-tuple-element.89.leaf), channel_id=1, source_target_pairs={{0,1},{1,0},{2,3},{3,2},{16,19},{17,18},{18,17},{19,16},{4,5},{5,4... | collective-permute-start | bytes 589832 | tf_op jit(solution)/shard_map/ppermute | solution.py:27
  60.4 0.7 collective-permute-start.16
  61.1 3.2 %collective-permute-done.17.got = f32[32,1536]{1,0:T(8,128)S(1)} collective-permute-done((f32[32,1536]{1,0:T(8,128)S(1)}, f32[32,1536]{1,0:T(8,128)S(1)}, u32[]{:S(2)}, u32[]{:S(2)}) %collective-permute-start.17) | collective-permute-done | bytes 196640 | tf_op jit(solution)/shard_map/ppermute | solution.py:27
  64.3 0.5 level_3.1
  64.8 0.1 collective-permute-start.19
  64.9 4.7 %collective-permute-done.19.got = f32[32,768]{1,0:T(8,128)S(1)} collective-permute-done((f32[32,768]{1,0:T(8,128)S(1)}, f32[32,768]{1,0:T(8,128)S(1)}, u32[]{:S(2)}, u32[]{:S(2)}) %collective-permute-start.19) | collective-permute-done | bytes 98336 | tf_op jit(solution)/shard_map/ppermute | solution.py:27
  69.6 1.9 %collective-permute-start.20 = (f32[64,640]{1,0:T(8,128)S(1)}, f32[64,640]{1,0:T(8,128)S(1)}, u32[]{:S(2)}, u32[]{:S(2)}) collective-permute-start(f32[64,640]{1,0:T(8,128)S(1)} %get-tuple-element.97.own), channel_id=1, source_target_pairs={{0,1},{1,0},{2,3},{3,2},{16,19},{17,18},{18,17},{19,16},{4,5},{5,4... | collective-permute-start | bytes 491528 | tf_op jit(solution)/shard_map/ppermute | solution.py:27
  71.5 3.6 %collective-permute-done.20.refs_0_.got = f32[64,640]{1,0:T(8,128)S(1)} collective-permute-done((f32[64,640]{1,0:T(8,128)S(1)}, f32[64,640]{1,0:T(8,128)S(1)}, u32[]{:S(2)}, u32[]{:S(2)}) %collective-permute-start.20) | collective-permute-done | bytes 163872 | tf_op jit(solution)/shard_map/ppermute | solution.py:27
  75.0 0.1 collective-permute-start.23
  75.1 3.1 %collective-permute-done.18.got = f32[64,1024]{1,0:T(8,128)S(1)} collective-permute-done((f32[64,1024]{1,0:T(8,128)S(1)}, f32[64,1024]{1,0:T(8,128)S(1)}, u32[]{:S(2)}, u32[]{:S(2)}) %collective-permute-start.18) | collective-permute-done | bytes 262176 | tf_op jit(solution)/shard_map/ppermute | solution.py:27
  78.2 0.1 leaf_3.1
  78.3 0.3 collective-permute-start.21
  78.6 0.2 collective-permute-start.25
  78.8 2.9 %collective-permute-done.23.refs_0_.refs_1_ = f32[128,640]{1,0:T(8,128)S(1)} collective-permute-done((f32[128,640]{1,0:T(8,128)S(1)}, f32[128,640]{1,0:T(8,128)S(1)}, u32[]{:S(2)}, u32[]{:S(2)}) %collective-permute-start.23) | collective-permute-done | bytes 327712 | tf_op jit(solution)/shard_map/ppermute | solution.py:27
  81.7 0.0 collective-permute-start.26
  81.8 1.4 %collective-permute-start.22 = (f32[128,640]{1,0:T(8,128)S(1)}, f32[128,640]{1,0:T(8,128)S(1)}, u32[]{:S(2)}, u32[]{:S(2)}) collective-permute-start(f32[128,640]{1,0:T(8,128)S(1)} %get-tuple-element.100), channel_id=1, source_target_pairs={{0,12},{4,8},{8,4},{12,0},{16,20},{20,16},{24,28},{28,24},{1,13},{... | collective-permute-start | bytes 983048 | tf_op jit(solution)/shard_map/ppermute | solution.py:27
  83.2 4.5 %collective-permute-done.21.got.refs_2_ = f32[128,768]{1,0:T(8,128)S(1)} collective-permute-done((f32[128,768]{1,0:T(8,128)S(1)}, f32[128,768]{1,0:T(8,128)S(1)}, u32[]{:S(2)}, u32[]{:S(2)}) %collective-permute-start.21) | collective-permute-done | bytes 393248 | tf_op jit(solution)/shard_map/ppermute | solution.py:27
  87.8 0.3 collective-permute-start.24
  88.1 4.4 %collective-permute-done.26.refs_3_ = f32[128,640]{1,0:T(8,128)S(1)} collective-permute-done((f32[128,640]{1,0:T(8,128)S(1)}, f32[128,640]{1,0:T(8,128)S(1)}, u32[]{:S(2)}, u32[]{:S(2)}) %collective-permute-start.26) | collective-permute-done | bytes 327712 | tf_op jit(solution)/shard_map/ppermute | solution.py:27
  92.5 5.6 %solve_upper.1 = (f32[32,512]{1,0:T(8,128)S(1)}, f32[8,128]{1,0:T(8,128)}) custom-call(f32[128,640]{1,0:T(8,128)S(1)} %upper_3.1.refs_0_, f32[128,640]{1,0:T(8,128)S(1)} %collective-permute-done.23.refs_0_.refs_1_, f32[128,640]{1,0:T(8,128)S(1)} %collective-permute-done.25.refs_2_, f32[128,640]{1,0:T(8,128)S(1)} %collective-permute-done.26.refs_3_), custom_call_target="tpu_custom_call" | custom-call | flops 5133828096 | bytes 1114112 | tf_op jit(solution)/shard_map/solve_upper/pallas_call | solution.py:161
  98.1 1.5 %collective-permute-start.27 = (f32[32,512]{1,0:T(8,128)S(1)}, f32[32,512]{1,0:T(8,128)S(1)}, u32[]{:S(2)}, u32[]{:S(2)}) collective-permute-start(f32[32,512]{1,0:T(8,128)S(1)} %get-tuple-element.102), channel_id=1, source_target_pairs={{0,16},{16,0},{1,17},{17,1},{2,18},{18,2},{3,19},{19,3},{4,20},{20... | collective-permute-start | bytes 196616 | tf_op jit(solution)/shard_map/ppermute | solution.py:32
  99.6 0.9 collective-permute-done.27.refs_5_
  100.5 3.8 %collective-permute-start.28 = (f32[32,512]{1,0:T(8,128)S(1)}, f32[32,512]{1,0:T(8,128)S(1)}, u32[]{:S(2)}, u32[]{:S(2)}) collective-permute-start(f32[32,512]{1,0:T(8,128)S(1)} %get-tuple-element.107), channel_id=1, source_target_pairs={{0,32},{32,0},{64,96},{96,64},{128,160},{160,128},{192,224},{224,1... | collective-permute-start | bytes 196616 | tf_op jit(solution)/shard_map/ppermute | solution.py:32
  104.3 6.8 %solve_leaf.1 = (f32[96,512]{1,0:T(8,128)}, f32[8,128]{1,0:T(8,128)}) custom-call(f32[128,128]{1,0:T(8,128)S(1)} %get-tuple-element.98.refs_0_, f32[128,768]{1,0:T(8,128)S(1)} %get-tuple-element.99.refs_1_, f32[128,768]{1,0:T(8,128)S(1)} %collective-permute-done.21.got.refs_2_, f32[128,640]{1,0:T(8,128)S(1)} %collective-permute-done.22.refs_3_, ...), custom_call_target="tpu_custom_call" | custom-call | flops 5737807872 | bytes 1245184 | tf_op jit(solution)/shard_map/solve_leaf/pallas_call | solution.py:161
  111.2 0.7 maximum_bitcast_fusion
  (30 shorter events, 0.2 us)
Async XLA Ops:
  0.6 17.6 %copy-start.1 = (bf16[1536,512]{1,0:T(8,128)(2,1)S(1)}, bf16[1536,512]{1,0:T(8,128)(2,1)}, u32[]{:S(2)}) copy-start(bf16[1536,512]{1,0:T(8,128)(2,1)} %omega_ref.3) | copy-start | bytes 4718596
  0.6 17.6 %copy-start = (bf16[2048,1536]{1,0:T(8,128)(2,1)S(1)}, bf16[2048,1536]{1,0:T(8,128)(2,1)}, u32[]{:S(2)}) copy-start(bf16[2048,1536]{1,0:T(8,128)(2,1)} %a_ref.3) | copy-start | bytes 18874372
  6.8 8.7 %collective-permute-start.6 = (f32[32,2048]{1,0:T(8,128)}, f32[32,2048]{1,0:T(8,128)S(1)}, u32[]{:S(2)}, u32[]{:S(2)}) collective-permute-start(f32[32,2048]{1,0:T(8,128)} %get-tuple-element.71), channel_id=1, source_target_pairs={{0,1},{1,0},{2,3},{3,2},{16,19},{17,18},{18,17},{19,16},{4,5},{5,4... | collective-permute-start | bytes 786440 | tf_op jit(solution)/shard_map/ppermute | solution.py:27
  10.1 10.9 %collective-permute-start.7 = (f32[32,2048]{1,0:T(8,128)}, f32[32,2048]{1,0:T(8,128)S(1)}, u32[]{:S(2)}, u32[]{:S(2)}) collective-permute-start(f32[32,2048]{1,0:T(8,128)} %get-tuple-element.72), channel_id=1, source_target_pairs={{0,4},{4,0},{8,12},{12,8},{16,28},{20,24},{24,20},{28,16},{1,5},{5... | collective-permute-start | bytes 786440 | tf_op jit(solution)/shard_map/ppermute | solution.py:27
  12.8 14.0 %collective-permute-start = (f32[64,2048]{1,0:T(8,128)}, f32[64,2048]{1,0:T(8,128)S(1)}, u32[]{:S(2)}, u32[]{:S(2)}) collective-permute-start(f32[64,2048]{1,0:T(8,128)} %get-tuple-element.58), channel_id=1, source_target_pairs={{0,1},{1,0},{2,3},{3,2},{16,19},{17,18},{18,17},{19,16},{4,5},{5,4... | collective-permute-start | bytes 1572872 | tf_op jit(solution)/shard_map/ppermute | solution.py:27
  13.0 15.4 %collective-permute-start.1 = (f32[64,2048]{1,0:T(8,128)}, f32[64,2048]{1,0:T(8,128)S(1)}, u32[]{:S(2)}, u32[]{:S(2)}) collective-permute-start(f32[64,2048]{1,0:T(8,128)} %get-tuple-element.60), channel_id=1, source_target_pairs={{0,4},{4,0},{8,12},{12,8},{16,28},{20,24},{24,20},{28,16},{1,5},{5... | collective-permute-start | bytes 1572872 | tf_op jit(solution)/shard_map/ppermute | solution.py:27
  13.0 13.6 %collective-permute-start.2 = (f32[32,2048]{1,0:T(8,128)}, f32[32,2048]{1,0:T(8,128)S(1)}, u32[]{:S(2)}, u32[]{:S(2)}) collective-permute-start(f32[32,2048]{1,0:T(8,128)} %get-tuple-element.63), channel_id=1, source_target_pairs={{0,1},{1,0},{2,3},{3,2},{16,19},{17,18},{18,17},{19,16},{4,5},{5,4... | collective-permute-start | bytes 786440 | tf_op jit(solution)/shard_map/ppermute | solution.py:27
  15.5 11.2 %collective-permute-start.3 = (f32[32,2048]{1,0:T(8,128)}, f32[32,2048]{1,0:T(8,128)S(1)}, u32[]{:S(2)}, u32[]{:S(2)}) collective-permute-start(f32[32,2048]{1,0:T(8,128)} %get-tuple-element.65), channel_id=1, source_target_pairs={{0,4},{4,0},{8,12},{12,8},{16,28},{20,24},{24,20},{28,16},{1,5},{5... | collective-permute-start | bytes 786440 | tf_op jit(solution)/shard_map/ppermute | solution.py:27
  21.0 21.0 %copy-start.2 = (s32[3,8,1024]{2,1,0:T(8,128)S(1)}, s32[3,8,1024]{2,1,0:T(8,128)}, u32[]{:S(2)}) copy-start(s32[3,8,1024]{2,1,0:T(8,128)} %upper_ref.1) | copy-start | bytes 294916
  21.0 21.0 %copy-start.3 = (s32[1,2048]{1,0:T(1,128)S(1)}, s32[1,2048]{1,0:T(1,128)}, u32[]{:S(2)}) copy-start(s32[1,2048]{1,0:T(1,128)} %leaf_ref.1) | copy-start | bytes 24580
  21.0 21.0 %copy-start.4 = (s32[4,16]{1,0:T(4,128)S(1)}, s32[4,16]{1,0:T(4,128)}, u32[]{:S(2)}) copy-start(s32[4,16]{1,0:T(4,128)} %ranks_ref.1) | copy-start | bytes 772
  21.1 7.4 %collective-permute-start.8 = (f32[32,2048]{1,0:T(8,128)S(1)}, f32[32,2048]{1,0:T(8,128)S(1)}, u32[]{:S(2)}, u32[]{:S(2)}) collective-permute-start(f32[32,2048]{1,0:T(8,128)S(1)} %get-tuple-element.73), channel_id=1, source_target_pairs={{0,3},{1,2},{2,1},{3,0},{16,17},{17,16},{18,19},{19,18},{4,7},{5,6... | collective-permute-start | bytes 786440 | tf_op jit(solution)/shard_map/ppermute | solution.py:27
  26.7 5.5 %collective-permute-start.9 = (f32[32,2048]{1,0:T(8,128)S(1)}, f32[32,2048]{1,0:T(8,128)S(1)}, u32[]{:S(2)}, u32[]{:S(2)}) collective-permute-start(f32[32,2048]{1,0:T(8,128)S(1)} %get-tuple-element.75), channel_id=1, source_target_pairs={{0,12},{4,8},{8,4},{12,0},{16,20},{20,16},{24,28},{28,24},{1,13},{... | collective-permute-start | bytes 786440 | tf_op jit(solution)/shard_map/ppermute | solution.py:27
  26.8 6.6 %collective-permute-start.4 = (f32[32,2048]{1,0:T(8,128)S(1)}, f32[32,2048]{1,0:T(8,128)S(1)}, u32[]{:S(2)}, u32[]{:S(2)}) collective-permute-start(f32[32,2048]{1,0:T(8,128)S(1)} %get-tuple-element.66), channel_id=1, source_target_pairs={{0,3},{1,2},{2,1},{3,0},{16,17},{17,16},{18,19},{19,18},{4,7},{5,6... | collective-permute-start | bytes 786440 | tf_op jit(solution)/shard_map/ppermute | solution.py:27
  26.9 8.1 %collective-permute-start.5 = (f32[32,2048]{1,0:T(8,128)S(1)}, f32[32,2048]{1,0:T(8,128)S(1)}, u32[]{:S(2)}, u32[]{:S(2)}) collective-permute-start(f32[32,2048]{1,0:T(8,128)S(1)} %get-tuple-element.68), channel_id=1, source_target_pairs={{0,12},{4,8},{8,4},{12,0},{16,20},{20,16},{24,28},{28,24},{1,13},{... | collective-permute-start | bytes 786440 | tf_op jit(solution)/shard_map/ppermute | solution.py:27
  32.3 9.5 %collective-permute-start.10 = (f32[32,2048]{1,0:T(8,128)S(1)}, f32[32,2048]{1,0:T(8,128)S(1)}, u32[]{:S(2)}, u32[]{:S(2)}) collective-permute-start(f32[32,2048]{1,0:T(8,128)S(1)} %get-tuple-element.76), channel_id=1, source_target_pairs={{0,4},{4,0},{8,12},{12,8},{16,28},{20,24},{24,20},{28,16},{1,5},{5... | collective-permute-start | bytes 786440 | tf_op jit(solution)/shard_map/ppermute | solution.py:27
  32.4 9.4 %collective-permute-start.11 = (f32[32,2048]{1,0:T(8,128)S(1)}, f32[32,2048]{1,0:T(8,128)S(1)}, u32[]{:S(2)}, u32[]{:S(2)}) collective-permute-start(f32[32,2048]{1,0:T(8,128)S(1)} %get-tuple-element.78), channel_id=1, source_target_pairs={{0,1},{1,0},{2,3},{3,2},{16,19},{17,18},{18,17},{19,16},{4,5},{5,4... | collective-permute-start | bytes 786440 | tf_op jit(solution)/shard_map/ppermute | solution.py:27
  41.8 3.9 %collective-permute-start.12 = (f32[16,2048]{1,0:T(8,128)S(1)}, f32[16,2048]{1,0:T(8,128)S(1)}, u32[]{:S(2)}, u32[]{:S(2)}) collective-permute-start(f32[16,2048]{1,0:T(8,128)S(1)} %get-tuple-element.80), channel_id=1, source_target_pairs={{0,12},{4,8},{8,4},{12,0},{16,20},{20,16},{24,28},{28,24},{1,13},{... | collective-permute-start | bytes 393224 | tf_op jit(solution)/shard_map/ppermute | solution.py:27
  41.9 3.9 %collective-permute-start.13 = (f32[16,2048]{1,0:T(8,128)S(1)}, f32[16,2048]{1,0:T(8,128)S(1)}, u32[]{:S(2)}, u32[]{:S(2)}) collective-permute-start(f32[16,2048]{1,0:T(8,128)S(1)} %get-tuple-element.82), channel_id=1, source_target_pairs={{0,3},{1,2},{2,1},{3,0},{16,17},{17,16},{18,19},{19,18},{4,7},{5,6... | collective-permute-start | bytes 393224 | tf_op jit(solution)/shard_map/ppermute | solution.py:27
  46.3 7.5 %collective-permute-start.14 = (f32[32,512]{1,0:T(8,128)S(1)}, f32[32,512]{1,0:T(8,128)S(1)}, u32[]{:S(2)}, u32[]{:S(2)}) collective-permute-start(f32[32,512]{1,0:T(8,128)S(1)} %get-tuple-element.83.own.skeleton_ref), channel_id=1, source_target_pairs={{0,16},{16,0},{1,17},{17,1},{2,18},{18,2},{3,19},{19,3},{4,20},{20... | collective-permute-start | bytes 196616 | tf_op jit(solution)/shard_map/ppermute | solution.py:32
  54.2 3.9 %collective-permute-start.15 = (f32[32,512]{1,0:T(8,128)S(1)}, f32[32,512]{1,0:T(8,128)S(1)}, u32[]{:S(2)}, u32[]{:S(2)}) collective-permute-start(f32[32,512]{1,0:T(8,128)S(1)} %get-tuple-element.84.own.skeleton_1), channel_id=1, source_target_pairs={{0,32},{32,0},{64,96},{96,64},{128,160},{160,128},{192,224},{224,1... | collective-permute-start | bytes 196616 | tf_op jit(solution)/shard_map/ppermute | solution.py:32
  58.6 5.8 %collective-permute-start.17 = (f32[32,1536]{1,0:T(8,128)S(1)}, f32[32,1536]{1,0:T(8,128)S(1)}, u32[]{:S(2)}, u32[]{:S(2)}) collective-permute-start(f32[32,1536]{1,0:T(8,128)S(1)} %get-tuple-element.89.leaf), channel_id=1, source_target_pairs={{0,1},{1,0},{2,3},{3,2},{16,19},{17,18},{18,17},{19,16},{4,5},{5,4... | collective-permute-start | bytes 589832 | tf_op jit(solution)/shard_map/ppermute | solution.py:27
  60.4 0.7 collective-permute-start.16
  64.8 4.7 %collective-permute-start.19 = (f32[32,768]{1,0:T(8,128)S(1)}, f32[32,768]{1,0:T(8,128)S(1)}, u32[]{:S(2)}, u32[]{:S(2)}) collective-permute-start(f32[32,768]{1,0:T(8,128)S(1)} %get-tuple-element.95.own), channel_id=1, source_target_pairs={{0,4},{4,0},{8,12},{12,8},{16,28},{20,24},{24,20},{28,16},{1,5},{5... | collective-permute-start | bytes 294920 | tf_op jit(solution)/shard_map/ppermute | solution.py:27
  69.6 5.5 %collective-permute-start.20 = (f32[64,640]{1,0:T(8,128)S(1)}, f32[64,640]{1,0:T(8,128)S(1)}, u32[]{:S(2)}, u32[]{:S(2)}) collective-permute-start(f32[64,640]{1,0:T(8,128)S(1)} %get-tuple-element.97.own), channel_id=1, source_target_pairs={{0,1},{1,0},{2,3},{3,2},{16,19},{17,18},{18,17},{19,16},{4,5},{5,4... | collective-permute-start | bytes 491528 | tf_op jit(solution)/shard_map/ppermute | solution.py:27
  71.4 6.8 %collective-permute-start.18 = (f32[64,1024]{1,0:T(8,128)S(1)}, f32[64,1024]{1,0:T(8,128)S(1)}, u32[]{:S(2)}, u32[]{:S(2)}) collective-permute-start(f32[64,1024]{1,0:T(8,128)S(1)} %get-tuple-element.93.own), channel_id=1, source_target_pairs={{0,3},{1,2},{2,1},{3,0},{16,17},{17,16},{18,19},{19,18},{4,7},{5,6... | collective-permute-start | bytes 786440 | tf_op jit(solution)/shard_map/ppermute | solution.py:27
  75.0 6.7 %collective-permute-start.23 = (f32[128,640]{1,0:T(8,128)S(1)}, f32[128,640]{1,0:T(8,128)S(1)}, u32[]{:S(2)}, u32[]{:S(2)}) collective-permute-start(f32[128,640]{1,0:T(8,128)S(1)} %upper_3.1.refs_0_), channel_id=1, source_target_pairs={{0,3},{1,2},{2,1},{3,0},{16,17},{17,16},{18,19},{19,18},{4,7},{5,6... | collective-permute-start | bytes 983048 | tf_op jit(solution)/shard_map/ppermute | solution.py:27
  78.3 9.5 %collective-permute-start.21 = (f32[128,768]{1,0:T(8,128)S(1)}, f32[128,768]{1,0:T(8,128)S(1)}, u32[]{:S(2)}, u32[]{:S(2)}) collective-permute-start(f32[128,768]{1,0:T(8,128)S(1)} %get-tuple-element.99.refs_1_), channel_id=1, source_target_pairs={{0,4},{4,0},{8,12},{12,8},{16,28},{20,24},{24,20},{28,16},{1,5},{5... | collective-permute-start | bytes 1179656 | tf_op jit(solution)/shard_map/ppermute | solution.py:27
  78.6 9.5 %collective-permute-start.25 = (f32[128,640]{1,0:T(8,128)S(1)}, f32[128,640]{1,0:T(8,128)S(1)}, u32[]{:S(2)}, u32[]{:S(2)}) collective-permute-start(f32[128,640]{1,0:T(8,128)S(1)} %upper_3.1.refs_0_), channel_id=1, source_target_pairs={{0,12},{4,8},{8,4},{12,0},{16,20},{20,16},{24,28},{28,24},{1,13},{... | collective-permute-start | bytes 983048 | tf_op jit(solution)/shard_map/ppermute | solution.py:27
  81.7 10.8 %collective-permute-start.26 = (f32[128,640]{1,0:T(8,128)S(1)}, f32[128,640]{1,0:T(8,128)S(1)}, u32[]{:S(2)}, u32[]{:S(2)}) collective-permute-start(f32[128,640]{1,0:T(8,128)S(1)} %collective-permute-done.23.refs_0_.refs_1_), channel_id=1, source_target_pairs={{0,12},{4,8},{8,4},{12,0},{16,20},{20,16},{24,28},{28,24},{1,13},{... | collective-permute-start | bytes 983048 | tf_op jit(solution)/shard_map/ppermute | solution.py:27
  81.8 22.5 %collective-permute-start.22 = (f32[128,640]{1,0:T(8,128)S(1)}, f32[128,640]{1,0:T(8,128)S(1)}, u32[]{:S(2)}, u32[]{:S(2)}) collective-permute-start(f32[128,640]{1,0:T(8,128)S(1)} %get-tuple-element.100), channel_id=1, source_target_pairs={{0,12},{4,8},{8,4},{12,0},{16,20},{20,16},{24,28},{28,24},{1,13},{... | collective-permute-start | bytes 983048 | tf_op jit(solution)/shard_map/ppermute | solution.py:27
  87.8 16.5 %collective-permute-start.24 = (f32[128,640]{1,0:T(8,128)S(1)}, f32[128,640]{1,0:T(8,128)S(1)}, u32[]{:S(2)}, u32[]{:S(2)}) collective-permute-start(f32[128,640]{1,0:T(8,128)S(1)} %leaf_4.1), channel_id=1, source_target_pairs={{0,12},{4,8},{8,4},{12,0},{16,20},{20,16},{24,28},{28,24},{1,13},{... | collective-permute-start | bytes 983048 | tf_op jit(solution)/shard_map/ppermute | solution.py:27
  98.1 2.4 %collective-permute-start.27 = (f32[32,512]{1,0:T(8,128)S(1)}, f32[32,512]{1,0:T(8,128)S(1)}, u32[]{:S(2)}, u32[]{:S(2)}) collective-permute-start(f32[32,512]{1,0:T(8,128)S(1)} %get-tuple-element.102), channel_id=1, source_target_pairs={{0,16},{16,0},{1,17},{17,1},{2,18},{18,2},{3,19},{19,3},{4,20},{20... | collective-permute-start | bytes 196616 | tf_op jit(solution)/shard_map/ppermute | solution.py:32
  100.5 10.6 %collective-permute-start.28 = (f32[32,512]{1,0:T(8,128)S(1)}, f32[32,512]{1,0:T(8,128)S(1)}, u32[]{:S(2)}, u32[]{:S(2)}) collective-permute-start(f32[32,512]{1,0:T(8,128)S(1)} %get-tuple-element.107), channel_id=1, source_target_pairs={{0,32},{32,0},{64,96},{96,64},{128,160},{160,128},{192,224},{224,1... | collective-permute-start | bytes 196616 | tf_op jit(solution)/shard_map/ppermute | solution.py:32
